TPU v7x, 32 devices: a whole 2x2x4 slice. The times are simulated.
32 devices in a mesh: leaf: 16 (over z, y, x), group: 2 (over core).
Axes of the slice: x: 2, y: 2, z: 4, core: 2. Of those that a mesh axis runs over, the one named last changes fastest.
Arguments:
- low_solved: float32 [16384, 256], P(('group', 'leaf')), may hold values from -4 to 4, as said below
- low_basis: float32 [16384, 256], P(('group', 'leaf')), may hold values from -0.002734375 to 0.002734375, as said below
- upper_solved: float32 [16384, 512], P(('group', 'leaf')), may hold values from -4 to 4, as said below
- upper_basis: float32 [16384, 256], P(('group', 'leaf')), may hold values from -0.0016572815 to 0.0016572815, as said below
Outputs:
- pair_solved: float32 [16384, 256], P(('group', 'leaf'))
- next_solved: float32 [16384, 256], P(('group', 'leaf'))
Inputs may be any that keep to these rules, and one draw needn't show every extreme that they name: `low_solved`: independent entries of mean zero. `low_basis`: independent entries of mean zero. `upper_solved`: independent entries of mean zero. `upper_basis`: independent entries of mean zero.
All inputs are finite; a program needn't handle non-finite values.
Results may differ from a plain program's by a relative error of at most 0.0003.
Values sent between devices are 32-bit elements; how exact they have to be, the bound alone decides.
No kernel may reach another device: no remote copies, remote signals or barrier semaphores. Data moves between devices by JAX's collectives and lax.ppermute only.
A program may use at most 64 MiB of HBM per device.

v0:
```python
import jax
import jax.numpy as jnp
from jax import lax
from jax.sharding import PartitionSpec as P

ITERS = 4


def partner(x, axis, stride):
    return lax.ppermute(x, axis, [(i, i ^ 1 << stride) for i in range(lax.axis_size(axis))])


def product(left, right):
    return jnp.dot(left, right, precision=lax.Precision.HIGHEST, preferred_element_type=jnp.float32)


def transposed_product(left, right):
    return lax.dot_general(
        left,
        right,
        (((0,), (0,)), ((), ())),
        precision=lax.Precision.HIGHEST,
        preferred_element_type=jnp.float32,
    )


def jacobi(couple_first, rhs_first, couple_second, rhs_second):
    update_first = jnp.zeros(rhs_second.shape, jnp.float32)
    update_second = jnp.zeros(rhs_first.shape, jnp.float32)
    for sweep_index in range(ITERS):
        update_first, update_second = (
            rhs_second - product(couple_second, update_second),
            rhs_first - product(couple_first, update_first),
        )
    return (update_first, update_second)


def body(low_solved, low_basis, upper_solved, upper_basis):
    rank_width = low_solved.shape[1]
    leaves = lax.axis_size("leaf")
    half_index = lax.axis_index("leaf") // (leaves // 2)
    slot_mask = (jnp.arange(2) == half_index).astype(jnp.float32)
    joined = jnp.concatenate([low_solved, upper_solved], axis=1)
    both_basis = jnp.concatenate([low_basis, upper_basis], axis=1)
    local_terms = transposed_product(both_basis, joined)
    totals = lax.psum(slot_mask[:, None, None] * local_terms[None], "leaf")
    first_half = totals[0]
    second_half = totals[1]
    update_first, update_second = jacobi(
        first_half[:rank_width, :rank_width],
        first_half[:rank_width, rank_width:],
        second_half[:rank_width, :rank_width],
        second_half[:rank_width, rank_width:],
    )
    own_update = jnp.where(half_index == 0, update_first, update_second)
    middle = upper_solved - product(low_solved, own_update)
    group_total = first_half[rank_width:, rank_width:] - product(
        first_half[rank_width:, :rank_width], update_first
    )
    group_total = (
        group_total
        + second_half[rank_width:, rank_width:]
        - product(second_half[rank_width:, :rank_width], update_second)
    )
    pair_solved = middle[:, :rank_width]
    sibling = partner(group_total, "group", 0)
    parity = lax.axis_index("group") % 2
    first_group = jnp.where(parity == 0, group_total, sibling)
    second_group = jnp.where(parity == 0, sibling, group_total)
    pair_first, pair_second = jacobi(
        first_group[:, :rank_width],
        first_group[:, rank_width:],
        second_group[:, :rank_width],
        second_group[:, rank_width:],
    )
    pair_update = jnp.where(parity == 0, pair_first, pair_second)
    next_solved = middle[:, rank_width:] - product(pair_solved, pair_update)
    return (pair_solved, next_solved)


def solution(mesh):
    return jax.shard_map(
        body,
        mesh=mesh,
        in_specs=(
            P(("group", "leaf"), None),
            P(("group", "leaf"), None),
            P(("group", "leaf"), None),
            P(("group", "leaf"), None),
        ),
        out_specs=(P(("group", "leaf"), None), P(("group", "leaf"), None)),
        check_vma=False,
    )
```

profile of v0, /device:TPU:0, one launch (start us, length us, event | category | flops | bytes accessed | tf_op | source)
XLA Modules:
  0.0 189.9 jit_solution(17188581265749702999)
XLA Ops:
  7.2 0.0 all-reduce.2.cloned.1.call-start
  7.2 4.5 %fusion = f32[512,768]{1,0:T(8,128)S(1)} fusion(f32[512,512]{1,0:T(8,128)} %param.6, f32[512,256]{1,0:T(8,128)} %param.4, f32[512,256]{1,0:T(8,128)} %param.7, f32[512,256]{1,0:T(8,128)} %param.5), kind=kOutput, calls=%fused_computation.2 | convolution fusion | flops 2416574464 | bytes 4194304 | tf_op jit(solution)/shard_map/dot_general | solution.py:18
  11.8 2.0 %broadcast_multiply_fusion = f32[2,512,768]{2,1,0:T(8,128)} fusion(f32[512,768]{1,0:T(8,128)S(1)} %fusion, f32[2]{0:T(128)S(1)} %compare_convert_fusion), kind=kLoop, calls=%fused_computation.6 | loop fusion | flops 786432 | bytes 4718600 | tf_op jit(solution)/shard_map/mul | solution.py:46
  13.7 0.0 all-reduce.2.cloned.1.call-update
  13.7 149.8 %all-reduce.2.cloned.1.call-done = f32[2,512,768]{2,1,0:T(8,128)} async-done(((f32[2,512,768]{2,1,0:T(8,128)}), f32[2,512,768]{2,1,0:T(8,128)}) %all-reduce.2.cloned.1.call-update) | async-done | bytes 3145744 | tf_op jit(solution)/shard_map/psum | solution.py:46
  163.5 2.1 %slice_bitcast_fusion.1 = (f32[512,768]{1,0:T(8,128)S(1)}, f32[512,768]{1,0:T(8,128)S(1)}) fusion(f32[2,512,768]{2,1,0:T(8,128)} %all-reduce.2.cloned.1.call-done), kind=kLoop, calls=%fused_computation.1 | loop fusion | bytes 6291456 | tf_op jit(solution)/shard_map/squeeze | solution.py:48
  165.6 0.6 convolution_subtract_fusion.10
  166.2 0.6 convolution_subtract_fusion.6
  166.7 0.6 convolution_subtract_fusion.9
  167.3 0.6 convolution_subtract_fusion.8
  168.0 0.6 convolution_subtract_fusion.7
  168.6 0.6 fusion.5
  169.2 0.6 convolution_subtract_fusion.5
  169.9 0.6 convolution_subtract_fusion.4
  170.5 0.0 copy-start
  170.5 0.6 convolution_subtract_fusion.3
  171.2 1.4 convolution_subtract_fusion.1
  172.6 0.0 collective-permute-start
  172.6 0.0 copy-done
  172.6 0.3 copy.6
  172.9 2.9 %fusion.4 = f32[512,512]{0,1:T(8,128)S(1)} fusion(f32[512,512]{0,1:T(8,128)S(1)} %copy.6, f32[512,256]{1,0:T(8,128)} %param.4, f32[256,512]{1,0:T(8,128)S(1)} %convolution_subtract_fusion.7, f32[256,512]{1,0:T(8,128)S(1)} %convolution_subtract_fusion.3, pred[]{:T(512)S(6)} %eq.20), kind=kOutput, calls=%fused_computation.8 | convolution fusion | flops 805699584 | bytes 3670017 | tf_op jit(solution)/shard_map/dot_general | solution.py:14
  175.9 1.0 copy.8
  176.9 0.0 collective-permute-done
  176.9 1.3 broadcast_select_fusion
  178.2 0.3 convolution_subtract_fusion.18
  178.6 0.3 convolution_subtract_fusion.14
  178.9 0.4 convolution_subtract_fusion.17
  179.3 0.6 convolution_subtract_fusion.16
  179.9 0.4 convolution_subtract_fusion.13
  180.3 0.4 convolution_subtract_fusion.12
  180.7 0.4 convolution_subtract_fusion.11
  181.0 0.4 fusion.6
  181.4 0.7 convolution_subtract_fusion
  182.1 1.0 copy.9
  (2 shorter events, 0.0 us)
Async XLA Ops:
  7.2 156.3 %all-reduce.2.cloned.1.call-start = ((), (), s32[]{:S(2)}) async-start(), calls=%async_computation | async-start | bytes 6291456 | tf_op jit(solution)/shard_map/psum | solution.py:46
  170.5 2.1 %copy-start = (f32[512,512]{1,0:T(8,128)S(1)}, f32[512,512]{1,0:T(8,128)}, u32[]{:S(2)}) copy-start(f32[512,512]{1,0:T(8,128)} %param.6) | copy-start | bytes 3145732
  172.6 4.3 %collective-permute-start = (f32[256,512]{1,0:T(8,128)}, f32[256,512]{1,0:T(8,128)}, u32[]{:S(2)}, u32[]{:S(2)}) collective-permute-start(f32[256,512]{1,0:T(8,128)} %convolution_subtract_fusion.1), channel_id=1, source_target_pairs={{0,1},{1,0},{2,3},{3,2},{4,5},{5,4},{6,7},{7,6},{8,9},{9,8},{10,11... | collective-permute-start | bytes 1572872 | tf_op jit(solution)/shard_map/ppermute | solution.py:10
Sparse Core Ops, SparseCore 0:
  13.9 149.5 all-reduce.1
where the time goes:
time: 190 us
  waiting for transfers between devices  150 us (79%)
  matrix products  18.2 us (10%)
  between operations  14.3 us (8%)
  local copies, waits for them, and re-layouts  4.45 us (2%)
  other arithmetic  3.26 us (2%)
    psum x1, waiting for transfers between devices, body(): totals = lax.psum(slot_mask[:, None, None] * local_terms[None], 'leaf')  150 us
    dot_general x20, matrix products, product(): jnp.dot(left, right, precision=lax.Precision.HIGHEST, preferred_element_t...  13.6 us
    dot_general x1, matrix products, transposed_product(): lax.dot_general(left, right, (((0,), (0,)), ((), ())), precision=lax.Prec...  4.53 us
  transfers between devices with their start and end apart: 2, of which 1 were waited for; matrix products, arithmetic and copies ran while one was open for 2% of the time, Pallas kernels for 0%

commit v1 on v0

v1 whole, which is shorter than its diff:
```python
import jax
import jax.numpy as jnp
from jax import lax
from jax.sharding import PartitionSpec as P

ITERS = 4


def flip(x, axis, bit):
    return lax.ppermute(x, axis, [(i, i ^ (1 << bit)) for i in range(lax.axis_size(axis))])


def product(left, right):
    return jnp.dot(left, right, precision=lax.Precision.HIGHEST, preferred_element_type=jnp.float32)


def transposed_product(left, right):
    return lax.dot_general(
        left,
        right,
        (((0,), (0,)), ((), ())),
        precision=lax.Precision.HIGHEST,
        preferred_element_type=jnp.float32,
    )


def jacobi(couple_first, rhs_first, couple_second, rhs_second):
    update_first = rhs_second
    update_second = rhs_first
    for sweep_index in range(ITERS - 1):
        update_first, update_second = (
            rhs_second - product(couple_second, update_second),
            rhs_first - product(couple_first, update_first),
        )
    return (update_first, update_second)


def scatter_sums(pieces, bits, own):
    order = [[(p + t) % bits for t in range(bits)] for p in range(len(pieces))]
    left = [list(reversed(range(bits))) for _ in pieces]
    for t in range(bits):
        sends, keeps = [], []
        for p, piece in enumerate(pieces):
            bit = order[p][t]
            dim = 1 + left[p].index(bit)
            left[p].remove(bit)
            sends.append(lax.dynamic_index_in_dim(piece, 1 - own[bit], dim, keepdims=False))
            keeps.append(lax.dynamic_index_in_dim(piece, own[bit], dim, keepdims=False))
        got = [flip(s, "leaf", order[p][t]) for p, s in enumerate(sends)]
        pieces = [k + g for k, g in zip(keeps, got)]
    return pieces


def gather_blocks(pieces, bits, own):
    have = [[] for _ in pieces]
    for t in range(bits):
        got = [flip(s, "leaf", (p + t) % bits) for p, s in enumerate(pieces)]
        grown = []
        for p in range(len(pieces)):
            bit = (p + t) % bits
            low = jnp.where(own[bit] == 0, pieces[p], got[p])
            high = jnp.where(own[bit] == 0, got[p], pieces[p])
            place = sum(1 for b in have[p] if b > bit)
            have[p].insert(place, bit)
            grown.append(jnp.stack([low, high], axis=1 + place))
        pieces = grown
    return [p.reshape(p.shape[0], -1, p.shape[-1]) for p in pieces]


def body(low_solved, low_basis, upper_solved, upper_basis):
    rank = low_solved.shape[1]
    leaves = lax.axis_size("leaf")
    bits = leaves.bit_length() - 2
    blocks = 1 << bits
    index = lax.axis_index("leaf")
    half = index // blocks
    own = [(index >> b) & 1 for b in range(bits)]
    basis = jnp.concatenate([low_basis, upper_basis], axis=1)
    panels = [low_solved, upper_solved[:, :rank], upper_solved[:, rank:]]
    local = [transposed_product(basis, panel) for panel in panels]
    local = [x.reshape([2] + [2] * bits + [rank // blocks, rank]) for x in local]
    sums = scatter_sums(local, bits, own)
    mine = [x[0] for x in sums]
    theirs = [flip(x, "leaf", bits) for x in mine]
    both = [
        jnp.stack([jnp.where(half == 0, m, t), jnp.where(half == 0, t, m)])
        for m, t in zip(mine, theirs)
    ]
    couple, rhs_low, rhs_high = gather_blocks(both, bits, own)
    rhs = jnp.concatenate([rhs_low, rhs_high], axis=2)
    update_first, update_second = jacobi(couple[0], rhs[0], couple[1], rhs[1])
    own_update = jnp.where(half == 0, update_first, update_second)
    rows = [
        sums[1 + i][1] - product(sums[0][1], own_update[:, i * rank : (i + 1) * rank])
        for i in range(2)
    ]
    rows = [x + flip(x, "leaf", bits) for x in rows]
    group_total = gather_blocks([x[None] for x in rows], bits, own)
    group_total = jnp.concatenate([x[0] for x in group_total], axis=1)
    sibling = flip(group_total, "group", 0)
    middle = upper_solved - product(low_solved, own_update)
    pair_solved = middle[:, :rank]
    parity = lax.axis_index("group") % 2
    first_group = jnp.where(parity == 0, group_total, sibling)
    second_group = jnp.where(parity == 0, sibling, group_total)
    pair_first, pair_second = jacobi(
        first_group[:, :rank],
        first_group[:, rank:],
        second_group[:, :rank],
        second_group[:, rank:],
    )
    pair_update = jnp.where(parity == 0, pair_first, pair_second)
    next_solved = middle[:, rank:] - product(pair_solved, pair_update)
    return (pair_solved, next_solved)


def solution(mesh):
    spec = P(("group", "leaf"), None)
    return jax.shard_map(
        body,
        mesh=mesh,
        in_specs=(spec, spec, spec, spec),
        out_specs=(spec, spec),
        check_vma=False,
    )
```

time: 190 us -> 90.4 us (0.48)
  waiting for transfers between devices: 150 us -> 24.7 us
  starting transfers between devices: 0.04 us -> 38.4 us
  between operations: 14.3 us -> 1.4 us
  matrix products: 18.2 us -> 14.4 us
    psum x1 -> x0, waiting for transfers between devices: 150 us -> none  [body(): totals = lax.psum(slot_mask[:, None, None] * local_terms[None], 'leaf')]
    ppermute x1 -> x30, starting transfers between devices: 0.01 us -> 38.4 us  [flip(): lax.ppermute(x, axis, [(i, i ^ 1 << bit) for i in range(lax.axis_size(axi...]
    ppermute x1 -> x30, waiting for transfers between devices: 0.01 us -> 24.7 us  [flip(): lax.ppermute(x, axis, [(i, i ^ 1 << bit) for i in range(lax.axis_size(axi...]
    dot_general x20 -> x16, matrix products: 13.6 us -> 9.01 us  [product(): jnp.dot(left, right, precision=lax.Precision.HIGHEST, preferred_element_t...]
    unnamed x5 -> x24, local copies, waits for them, and re-layouts: 2.33 us -> 5.18 us
    add x0 -> x9, other arithmetic: none -> 2.1 us  [scatter_sums(): pieces = [k + g for k, g in zip(keeps, got)]]
    mul x1 -> x0, other arithmetic: 1.95 us -> none  [body(): totals = lax.psum(slot_mask[:, None, None] * local_terms[None], 'leaf')]
    dot_general x1 -> x3, matrix products: 4.53 us -> 5.43 us  [transposed_product(): lax.dot_general(left, right, (((0,), (0,)), ((), ())), precision=lax.Prec...]
  transfers between devices with their start and end apart: 2 -> 30, of which waited for: 1 -> 19; matrix products, arithmetic and copies ran while one was open for 2% -> 11% of each run, Pallas kernels for 0% -> 0%
where the time goes in v1:
time: 90.4 us; the launch traced here: 90.1 us
  starting transfers between devices  38.4 us (42%)
  waiting for transfers between devices  24.7 us (27%)
  matrix products  14.4 us (16%)
  local copies, waits for them, and re-layouts  6.31 us (7%)
  other arithmetic  4.91 us (5%)
  between operations  1.4 us (2%)
    ppermute x30, starting transfers between devices, flip(): lax.ppermute(x, axis, [(i, i ^ 1 << bit) for i in range(lax.axis_size(axi...  38.4 us
    ppermute x30, waiting for transfers between devices, flip(): lax.ppermute(x, axis, [(i, i ^ 1 << bit) for i in range(lax.axis_size(axi...  24.7 us
    dot_general x16, matrix products, product(): jnp.dot(left, right, precision=lax.Precision.HIGHEST, preferred_element_t...  9.01 us
    dot_general x3, matrix products, transposed_product(): lax.dot_general(left, right, (((0,), (0,)), ((), ())), precision=lax.Prec...  5.43 us
    unnamed x24, local copies, waits for them, and re-layouts  5.18 us
    add x9, other arithmetic, scatter_sums(): pieces = [k + g for k, g in zip(keeps, got)]  2.1 us
  transfers between devices with their start and end apart: 30, of which 19 were waited for; matrix products, arithmetic and copies ran while one was open for 11% of the time, Pallas kernels for 0%

profile of v1, /device:TPU:0, one launch (start us, length us, event | category | flops | bytes accessed | tf_op | source)
XLA Modules:
  0.0 90.1 jit_solution(11249705652727901347)
XLA Ops:
  0.7 1.2 %constant_dynamic-update-slice_fusion.1 = f32[512,512]{1,0:T(8,128)S(1)} fusion(f32[512,256]{1,0:T(8,128)} %param.5), kind=kLoop, calls=%fused_computation.128 | loop fusion | bytes 1048576
  2.0 1.8 %fusion.30 = f32[512,256]{1,0:T(8,128)S(1)} fusion(f32[512,512]{1,0:T(8,128)S(1)} %constant_dynamic-update-slice_fusion, f32[512,256]{1,0:T(8,128)S(1)} %copy-done), kind=kOutput, calls=%fused_computation.136 | convolution fusion | flops 805306368 | bytes 2097152 | tf_op jit(solution)/shard_map/dot_general | solution.py:18
  3.8 0.8 copy-done.7
  4.6 0.7 dynamic-slice_bitcast_fusion
  5.3 2.9 %collective-permute-start.14 = (f32[2,2,2,32,256]{4,3,2,1,0:T(8,128)}, f32[2,2,2,32,256]{4,3,2,1,0:T(8,128)}, u32[]{:S(2)}, u32[]{:S(2)}) collective-permute-start(f32[2,2,2,32,256]{4,3,2,1,0:T(8,128)} %dynamic-slice_bitcast_fusion), channel_id=1, source_target_pairs={{0,2},{2,0},{4,6},{6,4},{8,10},{10,8},{12,14},{14,12},{16,18},{18,... | collective-permute-start | bytes 786440 | tf_op jit(solution)/shard_map/ppermute | solution.py:10
  8.3 1.8 %fusion.8 = f32[512,256]{1,0:T(8,128)S(1)} fusion(f32[512,512]{1,0:T(8,128)S(1)} %constant_dynamic-update-slice_fusion, f32[512,512]{1,0:T(8,128)S(1)} %copy-done.1), kind=kOutput, calls=%fused_computation.30 | convolution fusion | flops 805306368 | bytes 2097152 | tf_op jit(solution)/shard_map/dot_general | solution.py:18
  10.1 1.6 %collective-permute-start = (f32[2,2,2,32,256]{4,3,2,1,0:T(8,128)S(1)}, f32[2,2,2,32,256]{4,3,2,1,0:T(8,128)}, u32[]{:S(2)}, u32[]{:S(2)}) collective-permute-start(f32[2,2,2,32,256]{4,3,2,1,0:T(8,128)S(1)} %dynamic-slice_bitcast_fusion.2), channel_id=1, source_target_pairs={{0,4},{2,6},{4,0},{6,2},{8,12},{10,14},{12,8},{14,10},{16,20},{18,... | collective-permute-start | bytes 786440 | tf_op jit(solution)/shard_map/ppermute | solution.py:10
  11.7 1.8 %fusion.6 = f32[512,256]{1,0:T(8,128)S(1)} fusion(f32[512,512]{1,0:T(8,128)S(1)} %constant_dynamic-update-slice_fusion, f32[512,512]{1,0:T(8,128)S(1)} %copy-done.1), kind=kOutput, calls=%fused_computation.28 | convolution fusion | flops 805306368 | bytes 2097152 | tf_op jit(solution)/shard_map/dot_general | solution.py:18
  13.6 0.8 copy-done.5
  14.4 1.6 %collective-permute-start.7 = (f32[2,2,2,32,256]{4,3,2,1,0:T(8,128)S(1)}, f32[2,2,2,32,256]{4,3,2,1,0:T(8,128)S(1)}, u32[]{:S(2)}, u32[]{:S(2)}) collective-permute-start(f32[2,2,2,32,256]{4,3,2,1,0:T(8,128)S(1)} %dynamic-slice_bitcast_fusion.1), channel_id=1, source_target_pairs={{0,8},{2,10},{4,12},{6,14},{8,0},{10,2},{12,4},{14,6},{16,24},{18,... | collective-permute-start | bytes 786440 | tf_op jit(solution)/shard_map/ppermute | solution.py:10
  16.0 1.0 %bitcast_add_fusion = f32[2,2,2,32,256]{4,3,2,1,0:T(8,128)S(1)} fusion(f32[2,2,2,32,256]{4,3,2,1,0:T(8,128)} %collective-permute-done.14, f32[2,2,2,2,32,256]{5,4,3,2,1,0:T(8,128)S(1)} %bitcast.204, s32[]{:T(128)S(6)} %select_n.273), kind=kLoop, calls=%fused_computation.43 | loop fusion | flops 65536 | bytes 786436 | tf_op jit(solution)/shard_map/add | solution.py:50
  17.1 0.7 collective-permute-start.15
  18.1 1.0 %bitcast_add_fusion.2 = f32[2,2,2,32,256]{4,3,2,1,0:T(8,128)S(1)} fusion(f32[2,2,2,32,256]{4,3,2,1,0:T(8,128)} %collective-permute-done, f32[2,2,2,2,32,256]{5,4,3,2,1,0:T(8,128)S(1)} %bitcast.200, s32[]{:T(128)S(6)} %select_n.269), kind=kLoop, calls=%fused_computation.45 | loop fusion | flops 65536 | bytes 786436 | tf_op jit(solution)/shard_map/add | solution.py:50
  19.1 1.7 %collective-permute-start.1 = (f32[2,2,32,256]{3,2,0,1:T(8,128)S(1)}, f32[2,2,32,256]{3,2,0,1:T(8,128)S(1)}, u32[]{:S(2)}, u32[]{:S(2)}) collective-permute-start(f32[2,2,32,256]{3,2,0,1:T(8,128)S(1)} %bitcast.208), channel_id=1, source_target_pairs={{0,8},{2,10},{4,12},{6,14},{8,0},{10,2},{12,4},{14,6},{16,24},{18,... | collective-permute-start | bytes 393224 | tf_op jit(solution)/shard_map/ppermute | solution.py:10
  20.9 2.5 %collective-permute-done.7 = f32[2,2,2,32,256]{4,3,2,1,0:T(8,128)S(1)} collective-permute-done((f32[2,2,2,32,256]{4,3,2,1,0:T(8,128)S(1)}, f32[2,2,2,32,256]{4,3,2,1,0:T(8,128)S(1)}, u32[]{:S(2)}, u32[]{:S(2)}) %collective-permute-start.7) | collective-permute-done | bytes 262176 | tf_op jit(solution)/shard_map/ppermute | solution.py:10
  23.6 1.6 %collective-permute-start.16 = (f32[2,32,256]{2,1,0:T(8,128)S(1)}, f32[2,32,256]{2,1,0:T(8,128)S(1)}, u32[]{:S(2)}, u32[]{:S(2)}) collective-permute-start(f32[2,32,256]{2,1,0:T(8,128)S(1)} %dynamic-slice_bitcast_fusion.3), channel_id=1, source_target_pairs={{0,8},{2,10},{4,12},{6,14},{8,0},{10,2},{12,4},{14,6},{16,24},{18,... | collective-permute-start | bytes 196616 | tf_op jit(solution)/shard_map/ppermute | solution.py:10
  25.5 1.8 %collective-permute-start.2 = (f32[2,32,256]{2,1,0:T(8,128)S(1)}, f32[2,32,256]{2,1,0:T(8,128)S(1)}, u32[]{:S(2)}, u32[]{:S(2)}) collective-permute-start(f32[2,32,256]{2,1,0:T(8,128)S(1)} %dynamic-slice_bitcast_fusion.5), channel_id=1, source_target_pairs={{0,2},{2,0},{4,6},{6,4},{8,10},{10,8},{12,14},{14,12},{16,18},{18,... | collective-permute-start | bytes 196616 | tf_op jit(solution)/shard_map/ppermute | solution.py:10
  27.3 1.1 %collective-permute-done.8 = f32[2,2,32,256]{3,2,0,1:T(8,128)S(1)} collective-permute-done((f32[2,2,32,256]{3,2,0,1:T(8,128)S(1)}, f32[2,2,32,256]{3,2,0,1:T(8,128)S(1)}, u32[]{:S(2)}, u32[]{:S(2)}) %collective-permute-start.8) | collective-permute-done | bytes 131104 | tf_op jit(solution)/shard_map/ppermute | solution.py:10
  28.6 2.7 %collective-permute-start.17 = (f32[32,256]{1,0:T(8,128)S(1)}, f32[32,256]{1,0:T(8,128)S(1)}, u32[]{:S(2)}, u32[]{:S(2)}) collective-permute-start(f32[32,256]{1,0:T(8,128)S(1)} %slice_bitcast_fusion.3), channel_id=1, source_target_pairs={{0,16},{2,18},{4,20},{6,22},{8,24},{10,26},{12,28},{14,30},{16,0},... | collective-permute-start | bytes 98312 | tf_op jit(solution)/shard_map/ppermute | solution.py:10
  31.3 1.2 %collective-permute-start.3 = (f32[32,256]{1,0:T(8,128)S(1)}, f32[32,256]{1,0:T(8,128)S(1)}, u32[]{:S(2)}, u32[]{:S(2)}) collective-permute-start(f32[32,256]{1,0:T(8,128)S(1)} %slice_bitcast_fusion.5), channel_id=1, source_target_pairs={{0,16},{2,18},{4,20},{6,22},{8,24},{10,26},{12,28},{14,30},{16,0},... | collective-permute-start | bytes 98312 | tf_op jit(solution)/shard_map/ppermute | solution.py:10
  32.9 2.7 %collective-permute-start.10 = (f32[32,256]{1,0:T(8,128)S(1)}, f32[32,256]{1,0:T(8,128)S(1)}, u32[]{:S(2)}, u32[]{:S(2)}) collective-permute-start(f32[32,256]{1,0:T(8,128)S(1)} %slice_bitcast_fusion.4), channel_id=1, source_target_pairs={{0,16},{2,18},{4,20},{6,22},{8,24},{10,26},{12,28},{14,30},{16,0},... | collective-permute-start | bytes 98312 | tf_op jit(solution)/shard_map/ppermute | solution.py:10
  36.3 2.0 %collective-permute-start.4 = (f32[2,32,256]{2,1,0:T(8,128)S(1)}, f32[2,32,256]{2,1,0:T(8,128)S(1)}, u32[]{:S(2)}, u32[]{:S(2)}) collective-permute-start(f32[2,32,256]{2,1,0:T(8,128)S(1)} %pad_maximum_fusion.15), channel_id=1, source_target_pairs={{0,4},{2,6},{4,0},{6,2},{8,12},{10,14},{12,8},{14,10},{16,20},{18,... | collective-permute-start | bytes 196616 | tf_op jit(solution)/shard_map/ppermute | solution.py:10
  38.3 1.6 %collective-permute-start.11 = (f32[2,32,256]{2,1,0:T(8,128)S(1)}, f32[2,32,256]{2,1,0:T(8,128)S(1)}, u32[]{:S(2)}, u32[]{:S(2)}) collective-permute-start(f32[2,32,256]{2,1,0:T(8,128)S(1)} %pad_maximum_fusion.16), channel_id=1, source_target_pairs={{0,8},{2,10},{4,12},{6,14},{8,0},{10,2},{12,4},{14,6},{16,24},{18,... | collective-permute-start | bytes 196616 | tf_op jit(solution)/shard_map/ppermute | solution.py:10
  40.6 0.9 %collective-permute-start.19 = (f32[2,2,32,256]{3,2,0,1:T(8,128)S(1)}, f32[2,2,32,256]{3,2,0,1:T(8,128)S(1)}, u32[]{:S(2)}, u32[]{:S(2)}) collective-permute-start(f32[2,2,32,256]{3,2,0,1:T(8,128)S(1)} %pad_maximum_fusion.12), channel_id=1, source_target_pairs={{0,4},{2,6},{4,0},{6,2},{8,12},{10,14},{12,8},{14,10},{16,20},{18,... | collective-permute-start | bytes 393224 | tf_op jit(solution)/shard_map/ppermute | solution.py:10
  41.6 1.6 %collective-permute-start.5 = (f32[2,2,32,256]{3,2,0,1:T(8,128)S(1)}, f32[2,2,32,256]{3,2,0,1:T(8,128)S(1)}, u32[]{:S(2)}, u32[]{:S(2)}) collective-permute-start(f32[2,2,32,256]{3,2,0,1:T(8,128)S(1)} %pad_maximum_fusion.10), channel_id=1, source_target_pairs={{0,8},{2,10},{4,12},{6,14},{8,0},{10,2},{12,4},{14,6},{16,24},{18,... | collective-permute-start | bytes 393224 | tf_op jit(solution)/shard_map/ppermute | solution.py:10
  43.4 1.4 %collective-permute-start.12 = (f32[2,2,32,256]{3,2,0,1:T(8,128)S(1)}, f32[2,2,32,256]{3,2,0,1:T(8,128)S(1)}, u32[]{:S(2)}, u32[]{:S(2)}) collective-permute-start(f32[2,2,32,256]{3,2,0,1:T(8,128)S(1)} %pad_maximum_fusion.11), channel_id=1, source_target_pairs={{0,2},{2,0},{4,6},{6,4},{8,10},{10,8},{12,14},{14,12},{16,18},{18,... | collective-permute-start | bytes 393224 | tf_op jit(solution)/shard_map/ppermute | solution.py:10
  44.8 2.2 %collective-permute-done.19 = f32[2,2,32,256]{3,2,0,1:T(8,128)S(1)} collective-permute-done((f32[2,2,32,256]{3,2,0,1:T(8,128)S(1)}, f32[2,2,32,256]{3,2,0,1:T(8,128)S(1)}, u32[]{:S(2)}, u32[]{:S(2)}) %collective-permute-start.19) | collective-permute-done | bytes 131104 | tf_op jit(solution)/shard_map/ppermute | solution.py:10
  47.0 1.6 %collective-permute-start.20 = (f32[2,2,2,32,256]{4,3,0,2,1:T(8,128)S(1)}, f32[2,2,2,32,256]{4,3,0,2,1:T(8,128)S(1)}, u32[]{:S(2)}, u32[]{:S(2)}) collective-permute-start(f32[2,2,2,32,256]{4,3,0,2,1:T(8,128)S(1)} %pad_maximum_fusion.7), channel_id=1, source_target_pairs={{0,8},{2,10},{4,12},{6,14},{8,0},{10,2},{12,4},{14,6},{16,24},{18,... | collective-permute-start | bytes 786440 | tf_op jit(solution)/shard_map/ppermute | solution.py:10
  49.8 5.3 %collective-permute-done.6 = f32[2,2,2,32,256]{4,3,0,2,1:T(8,128)S(1)} collective-permute-done((f32[2,2,2,32,256]{4,3,0,2,1:T(8,128)S(1)}, f32[2,2,2,32,256]{4,3,0,2,1:T(8,128)S(1)}, u32[]{:S(2)}, u32[]{:S(2)}) %collective-permute-start.6) | collective-permute-done | bytes 262176 | tf_op jit(solution)/shard_map/ppermute | solution.py:10
  60.2 1.7 %collective-permute-start.25 = (f32[32,256]{1,0:T(8,128)S(1)}, f32[32,256]{1,0:T(8,128)S(1)}, u32[]{:S(2)}, u32[]{:S(2)}) collective-permute-start(f32[32,256]{1,0:T(8,128)S(1)} %fusion.23), channel_id=1, source_target_pairs={{0,16},{2,18},{4,20},{6,22},{8,24},{10,26},{12,28},{14,30},{16,0},... | collective-permute-start | bytes 98312 | tf_op jit(solution)/shard_map/ppermute | solution.py:10
  62.2 1.5 %collective-permute-start.21 = (f32[32,256]{1,0:T(8,128)S(1)}, f32[32,256]{1,0:T(8,128)S(1)}, u32[]{:S(2)}, u32[]{:S(2)}) collective-permute-start(f32[32,256]{1,0:T(8,128)S(1)} %fusion.24), channel_id=1, source_target_pairs={{0,16},{2,18},{4,20},{6,22},{8,24},{10,26},{12,28},{14,30},{16,0},... | collective-permute-start | bytes 98312 | tf_op jit(solution)/shard_map/ppermute | solution.py:10
  63.7 1.8 %collective-permute-done.25 = f32[32,256]{1,0:T(8,128)S(1)} collective-permute-done((f32[32,256]{1,0:T(8,128)S(1)}, f32[32,256]{1,0:T(8,128)S(1)}, u32[]{:S(2)}, u32[]{:S(2)}) %collective-permute-start.25) | collective-permute-done | bytes 32800 | tf_op jit(solution)/shard_map/ppermute | solution.py:10
  65.9 1.5 %collective-permute-done.21 = f32[32,256]{1,0:T(8,128)S(1)} collective-permute-done((f32[32,256]{1,0:T(8,128)S(1)}, f32[32,256]{1,0:T(8,128)S(1)}, u32[]{:S(2)}, u32[]{:S(2)}) %collective-permute-start.21) | collective-permute-done | bytes 32800 | tf_op jit(solution)/shard_map/ppermute | solution.py:10
  67.4 1.0 %collective-permute-start.22 = (f32[1,32,256]{2,1,0:T(8,128)S(1)}, f32[1,32,256]{2,1,0:T(8,128)S(1)}, u32[]{:S(2)}, u32[]{:S(2)}) collective-permute-start(f32[1,32,256]{2,1,0:T(8,128)S(1)} %add_bitcast_fusion.1), channel_id=1, source_target_pairs={{0,2},{2,0},{4,6},{6,4},{8,10},{10,8},{12,14},{14,12},{16,18},{18,... | collective-permute-start | bytes 98312 | tf_op jit(solution)/shard_map/ppermute | solution.py:10
  68.4 1.0 %collective-permute-done.26 = f32[1,32,256]{2,1,0:T(8,128)S(1)} collective-permute-done((f32[1,32,256]{2,1,0:T(8,128)S(1)}, f32[1,32,256]{2,1,0:T(8,128)S(1)}, u32[]{:S(2)}, u32[]{:S(2)}) %collective-permute-start.26) | collective-permute-done | bytes 32800 | tf_op jit(solution)/shard_map/ppermute | solution.py:10
  69.9 1.4 %collective-permute-done.22 = f32[1,32,256]{2,1,0:T(8,128)S(1)} collective-permute-done((f32[1,32,256]{2,1,0:T(8,128)S(1)}, f32[1,32,256]{2,1,0:T(8,128)S(1)}, u32[]{:S(2)}, u32[]{:S(2)}) %collective-permute-start.22) | collective-permute-done | bytes 32800 | tf_op jit(solution)/shard_map/ppermute | solution.py:10
  71.3 1.1 %collective-permute-start.23 = (f32[1,2,32,256]{3,2,1,0:T(8,128)S(1)}, f32[1,2,32,256]{3,2,1,0:T(8,128)S(1)}, u32[]{:S(2)}, u32[]{:S(2)}) collective-permute-start(f32[1,2,32,256]{3,2,1,0:T(8,128)S(1)} %pad_maximum_fusion.18), channel_id=1, source_target_pairs={{0,4},{2,6},{4,0},{6,2},{8,12},{10,14},{12,8},{14,10},{16,20},{18,... | collective-permute-start | bytes 196616 | tf_op jit(solution)/shard_map/ppermute | solution.py:10
  72.4 1.3 %collective-permute-done.27 = f32[1,2,32,256]{3,2,1,0:T(8,128)S(1)} collective-permute-done((f32[1,2,32,256]{3,2,1,0:T(8,128)S(1)}, f32[1,2,32,256]{3,2,1,0:T(8,128)S(1)}, u32[]{:S(2)}, u32[]{:S(2)}) %collective-permute-start.27) | collective-permute-done | bytes 65568 | tf_op jit(solution)/shard_map/ppermute | solution.py:10
  73.8 1.5 %collective-permute-start.28 = (f32[1,2,2,32,256]{4,3,2,1,0:T(8,128)S(1)}, f32[1,2,2,32,256]{4,3,2,1,0:T(8,128)S(1)}, u32[]{:S(2)}, u32[]{:S(2)}) collective-permute-start(f32[1,2,2,32,256]{4,3,2,1,0:T(8,128)S(1)} %pad_maximum_fusion.14), channel_id=1, source_target_pairs={{0,2},{2,0},{4,6},{6,4},{8,10},{10,8},{12,14},{14,12},{16,18},{18,... | collective-permute-start | bytes 393224 | tf_op jit(solution)/shard_map/ppermute | solution.py:10
  75.7 1.3 %collective-permute-start.24 = (f32[1,2,2,32,256]{4,3,2,1,0:T(8,128)S(1)}, f32[1,2,2,32,256]{4,3,2,1,0:T(8,128)S(1)}, u32[]{:S(2)}, u32[]{:S(2)}) collective-permute-start(f32[1,2,2,32,256]{4,3,2,1,0:T(8,128)S(1)} %pad_maximum_fusion.13), channel_id=1, source_target_pairs={{0,8},{2,10},{4,12},{6,14},{8,0},{10,2},{12,4},{14,6},{16,24},{18,... | collective-permute-start | bytes 393224 | tf_op jit(solution)/shard_map/ppermute | solution.py:10
  77.0 1.8 %collective-permute-done.28 = f32[1,2,2,32,256]{4,3,2,1,0:T(8,128)S(1)} collective-permute-done((f32[1,2,2,32,256]{4,3,2,1,0:T(8,128)S(1)}, f32[1,2,2,32,256]{4,3,2,1,0:T(8,128)S(1)}, u32[]{:S(2)}, u32[]{:S(2)}) %collective-permute-start.28) | collective-permute-done | bytes 131104 | tf_op jit(solution)/shard_map/ppermute | solution.py:10
  78.9 1.8 %collective-permute-done.24 = f32[1,2,2,32,256]{4,3,2,1,0:T(8,128)S(1)} collective-permute-done((f32[1,2,2,32,256]{4,3,2,1,0:T(8,128)S(1)}, f32[1,2,2,32,256]{4,3,2,1,0:T(8,128)S(1)}, u32[]{:S(2)}, u32[]{:S(2)}) %collective-permute-start.24) | collective-permute-done | bytes 131104 | tf_op jit(solution)/shard_map/ppermute | solution.py:10
  80.8 0.9 pad_maximum_fusion.3
  82.0 1.9 %fusion = f32[512,512]{0,1:T(8,128)S(1)} fusion(f32[512,512]{0,1:T(8,128)S(1)} %copy.26, f32[256,512]{1,0:T(8,128)S(1)} %fusion.1, f32[512,256]{1,0:T(8,128)S(1)} %copy-done), kind=kOutput, calls=%fused_computation.1 | convolution fusion | flops 805568512 | bytes 3145728 | tf_op jit(solution)/shard_map/dot_general | solution.py:14
  83.9 1.0 %copy.29 = f32[512,256]{1,0:T(8,128)} copy(f32[512,256]{0,1:T(8,128)S(1)} %slice.90) | data formatting | bytes 1048576
  84.9 1.2 %broadcast_select_fusion.1 = (f32[256,512]{1,0:T(8,128)S(1)}, f32[256,512]{1,0:T(8,128)S(1)}) fusion(f32[256,512]{1,0:T(8,128)} %collective-permute-done.29, pred[]{:T(512)S(6)} %eq.15, f32[256,256]{1,0:T(8,128)S(1)} %bitcast.196, f32[256,256]{1,0:T(8,128)S(1)} %bitcast.198), kind=kLoop, calls=%fused_computation.56 | loop fusion | flops 393216 | bytes 2097153 | tf_op jit(solution)/shard_map/jit(_where)/select_n | solution.py:105
  88.4 0.7 convolution_subtract_fusion
  89.1 1.0 %copy.30 = f32[512,256]{1,0:T(8,128)} copy(f32[512,256]{0,1:T(8,128)S(1)} %convolution_subtract_fusion) | data formatting | bytes 1048576
  (125 shorter events, 13.7 us)
Async XLA Ops:
  0.6 1.4 %copy-start = (f32[512,256]{1,0:T(8,128)S(1)}, f32[512,256]{1,0:T(8,128)}, u32[]{:S(2)}) copy-start(f32[512,256]{1,0:T(8,128)} %param.4) | copy-start | bytes 1572868
  0.7 1.3 %copy-start.9 = (f32[512,256]{1,0:T(8,128)S(1)}, f32[512,256]{1,0:T(8,128)}, u32[]{:S(2)}) copy-start(f32[512,256]{1,0:T(8,128)} %param.7) | copy-start | bytes 1572868
  2.0 6.3 %copy-start.1 = (f32[512,512]{1,0:T(8,128)S(1)}, f32[512,512]{1,0:T(8,128)}, u32[]{:S(2)}) copy-start(f32[512,512]{1,0:T(8,128)} %param.6) | copy-start | bytes 3145732
  3.8 0.8 copy-start.7
  5.3 10.7 %collective-permute-start.14 = (f32[2,2,2,32,256]{4,3,2,1,0:T(8,128)}, f32[2,2,2,32,256]{4,3,2,1,0:T(8,128)}, u32[]{:S(2)}, u32[]{:S(2)}) collective-permute-start(f32[2,2,2,32,256]{4,3,2,1,0:T(8,128)} %dynamic-slice_bitcast_fusion), channel_id=1, source_target_pairs={{0,2},{2,0},{4,6},{6,4},{8,10},{10,8},{12,14},{14,12},{16,18},{18,... | collective-permute-start | bytes 786440 | tf_op jit(solution)/shard_map/ppermute | solution.py:10
  10.1 7.9 %collective-permute-start = (f32[2,2,2,32,256]{4,3,2,1,0:T(8,128)S(1)}, f32[2,2,2,32,256]{4,3,2,1,0:T(8,128)}, u32[]{:S(2)}, u32[]{:S(2)}) collective-permute-start(f32[2,2,2,32,256]{4,3,2,1,0:T(8,128)S(1)} %dynamic-slice_bitcast_fusion.2), channel_id=1, source_target_pairs={{0,4},{2,6},{4,0},{6,2},{8,12},{10,14},{12,8},{14,10},{16,20},{18,... | collective-permute-start | bytes 786440 | tf_op jit(solution)/shard_map/ppermute | solution.py:10
  13.5 0.8 copy-start.5
  13.6 2.5 %copy-start.8 = (f32[512,256]{1,0:T(8,128)S(1)}, f32[512,256]{1,0:T(8,128)}, u32[]{:S(2)}) copy-start(f32[512,256]{1,0:T(8,128)} %copy-done.7) | copy-start | bytes 1572868
  14.4 9.0 %collective-permute-start.7 = (f32[2,2,2,32,256]{4,3,2,1,0:T(8,128)S(1)}, f32[2,2,2,32,256]{4,3,2,1,0:T(8,128)S(1)}, u32[]{:S(2)}, u32[]{:S(2)}) collective-permute-start(f32[2,2,2,32,256]{4,3,2,1,0:T(8,128)S(1)} %dynamic-slice_bitcast_fusion.1), channel_id=1, source_target_pairs={{0,8},{2,10},{4,12},{6,14},{8,0},{10,2},{12,4},{14,6},{16,24},{18,... | collective-permute-start | bytes 786440 | tf_op jit(solution)/shard_map/ppermute | solution.py:10
  17.1 6.4 %collective-permute-start.15 = (f32[2,2,32,256]{3,2,0,1:T(8,128)S(1)}, f32[2,2,32,256]{3,2,0,1:T(8,128)S(1)}, u32[]{:S(2)}, u32[]{:S(2)}) collective-permute-start(f32[2,2,32,256]{3,2,0,1:T(8,128)S(1)} %bitcast.207), channel_id=1, source_target_pairs={{0,4},{2,6},{4,0},{6,2},{8,12},{10,14},{12,8},{14,10},{16,20},{18,... | collective-permute-start | bytes 393224 | tf_op jit(solution)/shard_map/ppermute | solution.py:10
  19.1 4.3 %copy-start.6 = (f32[512,256]{1,0:T(8,128)S(1)}, f32[512,256]{1,0:T(8,128)}, u32[]{:S(2)}) copy-start(f32[512,256]{1,0:T(8,128)} %copy-done.5) | copy-start | bytes 1572868
  19.1 6.3 %collective-permute-start.1 = (f32[2,2,32,256]{3,2,0,1:T(8,128)S(1)}, f32[2,2,32,256]{3,2,0,1:T(8,128)S(1)}, u32[]{:S(2)}, u32[]{:S(2)}) collective-permute-start(f32[2,2,32,256]{3,2,0,1:T(8,128)S(1)} %bitcast.208), channel_id=1, source_target_pairs={{0,8},{2,10},{4,12},{6,14},{8,0},{10,2},{12,4},{14,6},{16,24},{18,... | collective-permute-start | bytes 393224 | tf_op jit(solution)/shard_map/ppermute | solution.py:10
  23.4 5.0 %collective-permute-start.8 = (f32[2,2,32,256]{3,2,0,1:T(8,128)S(1)}, f32[2,2,32,256]{3,2,0,1:T(8,128)S(1)}, u32[]{:S(2)}, u32[]{:S(2)}) collective-permute-start(f32[2,2,32,256]{3,2,0,1:T(8,128)S(1)} %bitcast.209), channel_id=1, source_target_pairs={{0,2},{2,0},{4,6},{6,4},{8,10},{10,8},{12,14},{14,12},{16,18},{18,... | collective-permute-start | bytes 393224 | tf_op jit(solution)/shard_map/ppermute | solution.py:10
  23.6 5.0 %collective-permute-start.16 = (f32[2,32,256]{2,1,0:T(8,128)S(1)}, f32[2,32,256]{2,1,0:T(8,128)S(1)}, u32[]{:S(2)}, u32[]{:S(2)}) collective-permute-start(f32[2,32,256]{2,1,0:T(8,128)S(1)} %dynamic-slice_bitcast_fusion.3), channel_id=1, source_target_pairs={{0,8},{2,10},{4,12},{6,14},{8,0},{10,2},{12,4},{14,6},{16,24},{18,... | collective-permute-start | bytes 196616 | tf_op jit(solution)/shard_map/ppermute | solution.py:10
  25.5 5.8 %collective-permute-start.2 = (f32[2,32,256]{2,1,0:T(8,128)S(1)}, f32[2,32,256]{2,1,0:T(8,128)S(1)}, u32[]{:S(2)}, u32[]{:S(2)}) collective-permute-start(f32[2,32,256]{2,1,0:T(8,128)S(1)} %dynamic-slice_bitcast_fusion.5), channel_id=1, source_target_pairs={{0,2},{2,0},{4,6},{6,4},{8,10},{10,8},{12,14},{14,12},{16,18},{18,... | collective-permute-start | bytes 196616 | tf_op jit(solution)/shard_map/ppermute | solution.py:10
  28.5 4.3 %collective-permute-start.9 = (f32[2,32,256]{2,1,0:T(8,128)S(1)}, f32[2,32,256]{2,1,0:T(8,128)S(1)}, u32[]{:S(2)}, u32[]{:S(2)}) collective-permute-start(f32[2,32,256]{2,1,0:T(8,128)S(1)} %dynamic-slice_bitcast_fusion.4), channel_id=1, source_target_pairs={{0,4},{2,6},{4,0},{6,2},{8,12},{10,14},{12,8},{14,10},{16,20},{18,... | collective-permute-start | bytes 196616 | tf_op jit(solution)/shard_map/ppermute | solution.py:10
  28.6 6.9 %collective-permute-start.17 = (f32[32,256]{1,0:T(8,128)S(1)}, f32[32,256]{1,0:T(8,128)S(1)}, u32[]{:S(2)}, u32[]{:S(2)}) collective-permute-start(f32[32,256]{1,0:T(8,128)S(1)} %slice_bitcast_fusion.3), channel_id=1, source_target_pairs={{0,16},{2,18},{4,20},{6,22},{8,24},{10,26},{12,28},{14,30},{16,0},... | collective-permute-start | bytes 98312 | tf_op jit(solution)/shard_map/ppermute | solution.py:10
  31.3 5.0 %collective-permute-start.3 = (f32[32,256]{1,0:T(8,128)S(1)}, f32[32,256]{1,0:T(8,128)S(1)}, u32[]{:S(2)}, u32[]{:S(2)}) collective-permute-start(f32[32,256]{1,0:T(8,128)S(1)} %slice_bitcast_fusion.5), channel_id=1, source_target_pairs={{0,16},{2,18},{4,20},{6,22},{8,24},{10,26},{12,28},{14,30},{16,0},... | collective-permute-start | bytes 98312 | tf_op jit(solution)/shard_map/ppermute | solution.py:10
  32.9 5.4 %collective-permute-start.10 = (f32[32,256]{1,0:T(8,128)S(1)}, f32[32,256]{1,0:T(8,128)S(1)}, u32[]{:S(2)}, u32[]{:S(2)}) collective-permute-start(f32[32,256]{1,0:T(8,128)S(1)} %slice_bitcast_fusion.4), channel_id=1, source_target_pairs={{0,16},{2,18},{4,20},{6,22},{8,24},{10,26},{12,28},{14,30},{16,0},... | collective-permute-start | bytes 98312 | tf_op jit(solution)/shard_map/ppermute | solution.py:10
  35.5 5.0 %collective-permute-start.18 = (f32[2,32,256]{2,1,0:T(8,128)S(1)}, f32[2,32,256]{2,1,0:T(8,128)S(1)}, u32[]{:S(2)}, u32[]{:S(2)}) collective-permute-start(f32[2,32,256]{2,1,0:T(8,128)S(1)} %pad_maximum_fusion.17), channel_id=1, source_target_pairs={{0,2},{2,0},{4,6},{6,4},{8,10},{10,8},{12,14},{14,12},{16,18},{18,... | collective-permute-start | bytes 196616 | tf_op jit(solution)/shard_map/ppermute | solution.py:10
  36.3 5.2 %collective-permute-start.4 = (f32[2,32,256]{2,1,0:T(8,128)S(1)}, f32[2,32,256]{2,1,0:T(8,128)S(1)}, u32[]{:S(2)}, u32[]{:S(2)}) collective-permute-start(f32[2,32,256]{2,1,0:T(8,128)S(1)} %pad_maximum_fusion.15), channel_id=1, source_target_pairs={{0,4},{2,6},{4,0},{6,2},{8,12},{10,14},{12,8},{14,10},{16,20},{18,... | collective-permute-start | bytes 196616 | tf_op jit(solution)/shard_map/ppermute | solution.py:10
  38.3 5.0 %collective-permute-start.11 = (f32[2,32,256]{2,1,0:T(8,128)S(1)}, f32[2,32,256]{2,1,0:T(8,128)S(1)}, u32[]{:S(2)}, u32[]{:S(2)}) collective-permute-start(f32[2,32,256]{2,1,0:T(8,128)S(1)} %pad_maximum_fusion.16), channel_id=1, source_target_pairs={{0,8},{2,10},{4,12},{6,14},{8,0},{10,2},{12,4},{14,6},{16,24},{18,... | collective-permute-start | bytes 196616 | tf_op jit(solution)/shard_map/ppermute | solution.py:10
  40.6 6.4 %collective-permute-start.19 = (f32[2,2,32,256]{3,2,0,1:T(8,128)S(1)}, f32[2,2,32,256]{3,2,0,1:T(8,128)S(1)}, u32[]{:S(2)}, u32[]{:S(2)}) collective-permute-start(f32[2,2,32,256]{3,2,0,1:T(8,128)S(1)} %pad_maximum_fusion.12), channel_id=1, source_target_pairs={{0,4},{2,6},{4,0},{6,2},{8,12},{10,14},{12,8},{14,10},{16,20},{18,... | collective-permute-start | bytes 393224 | tf_op jit(solution)/shard_map/ppermute | solution.py:10
  41.6 7.1 %collective-permute-start.5 = (f32[2,2,32,256]{3,2,0,1:T(8,128)S(1)}, f32[2,2,32,256]{3,2,0,1:T(8,128)S(1)}, u32[]{:S(2)}, u32[]{:S(2)}) collective-permute-start(f32[2,2,32,256]{3,2,0,1:T(8,128)S(1)} %pad_maximum_fusion.10), channel_id=1, source_target_pairs={{0,8},{2,10},{4,12},{6,14},{8,0},{10,2},{12,4},{14,6},{16,24},{18,... | collective-permute-start | bytes 393224 | tf_op jit(solution)/shard_map/ppermute | solution.py:10
  43.4 5.9 %collective-permute-start.12 = (f32[2,2,32,256]{3,2,0,1:T(8,128)S(1)}, f32[2,2,32,256]{3,2,0,1:T(8,128)S(1)}, u32[]{:S(2)}, u32[]{:S(2)}) collective-permute-start(f32[2,2,32,256]{3,2,0,1:T(8,128)S(1)} %pad_maximum_fusion.11), channel_id=1, source_target_pairs={{0,2},{2,0},{4,6},{6,4},{8,10},{10,8},{12,14},{14,12},{16,18},{18,... | collective-permute-start | bytes 393224 | tf_op jit(solution)/shard_map/ppermute | solution.py:10
  47.0 8.9 %collective-permute-start.20 = (f32[2,2,2,32,256]{4,3,0,2,1:T(8,128)S(1)}, f32[2,2,2,32,256]{4,3,0,2,1:T(8,128)S(1)}, u32[]{:S(2)}, u32[]{:S(2)}) collective-permute-start(f32[2,2,2,32,256]{4,3,0,2,1:T(8,128)S(1)} %pad_maximum_fusion.7), channel_id=1, source_target_pairs={{0,8},{2,10},{4,12},{6,14},{8,0},{10,2},{12,4},{14,6},{16,24},{18,... | collective-permute-start | bytes 786440 | tf_op jit(solution)/shard_map/ppermute | solution.py:10
  48.7 6.4 %collective-permute-start.6 = (f32[2,2,2,32,256]{4,3,0,2,1:T(8,128)S(1)}, f32[2,2,2,32,256]{4,3,0,2,1:T(8,128)S(1)}, u32[]{:S(2)}, u32[]{:S(2)}) collective-permute-start(f32[2,2,2,32,256]{4,3,0,2,1:T(8,128)S(1)} %pad_maximum_fusion.5), channel_id=1, source_target_pairs={{0,2},{2,0},{4,6},{6,4},{8,10},{10,8},{12,14},{14,12},{16,18},{18,... | collective-permute-start | bytes 786440 | tf_op jit(solution)/shard_map/ppermute | solution.py:10
  49.4 6.4 %collective-permute-start.13 = (f32[2,2,2,32,256]{4,3,0,1,2:T(8,128)S(1)}, f32[2,2,2,32,256]{4,3,0,1,2:T(8,128)S(1)}, u32[]{:S(2)}, u32[]{:S(2)}) collective-permute-start(f32[2,2,2,32,256]{4,3,0,1,2:T(8,128)S(1)} %pad_maximum_fusion.6), channel_id=1, source_target_pairs={{0,4},{2,6},{4,0},{6,2},{8,12},{10,14},{12,8},{14,10},{16,20},{18,... | collective-permute-start | bytes 786440 | tf_op jit(solution)/shard_map/ppermute | solution.py:10
  60.2 5.2 %collective-permute-start.25 = (f32[32,256]{1,0:T(8,128)S(1)}, f32[32,256]{1,0:T(8,128)S(1)}, u32[]{:S(2)}, u32[]{:S(2)}) collective-permute-start(f32[32,256]{1,0:T(8,128)S(1)} %fusion.23), channel_id=1, source_target_pairs={{0,16},{2,18},{4,20},{6,22},{8,24},{10,26},{12,28},{14,30},{16,0},... | collective-permute-start | bytes 98312 | tf_op jit(solution)/shard_map/ppermute | solution.py:10
  62.2 5.2 %collective-permute-start.21 = (f32[32,256]{1,0:T(8,128)S(1)}, f32[32,256]{1,0:T(8,128)S(1)}, u32[]{:S(2)}, u32[]{:S(2)}) collective-permute-start(f32[32,256]{1,0:T(8,128)S(1)} %fusion.24), channel_id=1, source_target_pairs={{0,16},{2,18},{4,20},{6,22},{8,24},{10,26},{12,28},{14,30},{16,0},... | collective-permute-start | bytes 98312 | tf_op jit(solution)/shard_map/ppermute | solution.py:10
  65.4 3.9 %collective-permute-start.26 = (f32[1,32,256]{2,1,0:T(8,128)S(1)}, f32[1,32,256]{2,1,0:T(8,128)S(1)}, u32[]{:S(2)}, u32[]{:S(2)}) collective-permute-start(f32[1,32,256]{2,1,0:T(8,128)S(1)} %add_bitcast_fusion), channel_id=1, source_target_pairs={{0,4},{2,6},{4,0},{6,2},{8,12},{10,14},{12,8},{14,10},{16,20},{18,... | collective-permute-start | bytes 98312 | tf_op jit(solution)/shard_map/ppermute | solution.py:10
  67.4 3.9 %collective-permute-start.22 = (f32[1,32,256]{2,1,0:T(8,128)S(1)}, f32[1,32,256]{2,1,0:T(8,128)S(1)}, u32[]{:S(2)}, u32[]{:S(2)}) collective-permute-start(f32[1,32,256]{2,1,0:T(8,128)S(1)} %add_bitcast_fusion.1), channel_id=1, source_target_pairs={{0,2},{2,0},{4,6},{6,4},{8,10},{10,8},{12,14},{14,12},{16,18},{18,... | collective-permute-start | bytes 98312 | tf_op jit(solution)/shard_map/ppermute | solution.py:10
  69.4 4.3 %collective-permute-start.27 = (f32[1,2,32,256]{3,2,1,0:T(8,128)S(1)}, f32[1,2,32,256]{3,2,1,0:T(8,128)S(1)}, u32[]{:S(2)}, u32[]{:S(2)}) collective-permute-start(f32[1,2,32,256]{3,2,1,0:T(8,128)S(1)} %pad_maximum_fusion.19), channel_id=1, source_target_pairs={{0,8},{2,10},{4,12},{6,14},{8,0},{10,2},{12,4},{14,6},{16,24},{18,... | collective-permute-start | bytes 196616 | tf_op jit(solution)/shard_map/ppermute | solution.py:10
  71.3 4.3 %collective-permute-start.23 = (f32[1,2,32,256]{3,2,1,0:T(8,128)S(1)}, f32[1,2,32,256]{3,2,1,0:T(8,128)S(1)}, u32[]{:S(2)}, u32[]{:S(2)}) collective-permute-start(f32[1,2,32,256]{3,2,1,0:T(8,128)S(1)} %pad_maximum_fusion.18), channel_id=1, source_target_pairs={{0,4},{2,6},{4,0},{6,2},{8,12},{10,14},{12,8},{14,10},{16,20},{18,... | collective-permute-start | bytes 196616 | tf_op jit(solution)/shard_map/ppermute | solution.py:10
  73.8 5.0 %collective-permute-start.28 = (f32[1,2,2,32,256]{4,3,2,1,0:T(8,128)S(1)}, f32[1,2,2,32,256]{4,3,2,1,0:T(8,128)S(1)}, u32[]{:S(2)}, u32[]{:S(2)}) collective-permute-start(f32[1,2,2,32,256]{4,3,2,1,0:T(8,128)S(1)} %pad_maximum_fusion.14), channel_id=1, source_target_pairs={{0,2},{2,0},{4,6},{6,4},{8,10},{10,8},{12,14},{14,12},{16,18},{18,... | collective-permute-start | bytes 393224 | tf_op jit(solution)/shard_map/ppermute | solution.py:10
  75.7 5.0 %collective-permute-start.24 = (f32[1,2,2,32,256]{4,3,2,1,0:T(8,128)S(1)}, f32[1,2,2,32,256]{4,3,2,1,0:T(8,128)S(1)}, u32[]{:S(2)}, u32[]{:S(2)}) collective-permute-start(f32[1,2,2,32,256]{4,3,2,1,0:T(8,128)S(1)} %pad_maximum_fusion.13), channel_id=1, source_target_pairs={{0,8},{2,10},{4,12},{6,14},{8,0},{10,2},{12,4},{14,6},{16,24},{18,... | collective-permute-start | bytes 393224 | tf_op jit(solution)/shard_map/ppermute | solution.py:10
  78.9 2.8 %copy-start.2 = (f32[512,512]{1,0:T(8,128)S(1)}, f32[512,512]{1,0:T(8,128)}, u32[]{:S(2)}) copy-start(f32[512,512]{1,0:T(8,128)} %param.6) | copy-start | bytes 3145732
  80.8 0.9 copy-start.3
  81.6 3.3 %collective-permute-start.29 = (f32[256,512]{1,0:T(8,128)}, f32[256,512]{1,0:T(8,128)}, u32[]{:S(2)}, u32[]{:S(2)}) collective-permute-start(f32[256,512]{1,0:T(8,128)} %pad_maximum_fusion.3), channel_id=1, source_target_pairs={{0,1},{1,0},{2,3},{3,2},{4,5},{5,4},{6,7},{7,6},{8,9},{9,8},{10,11... | collective-permute-start | bytes 1572872 | tf_op jit(solution)/shard_map/ppermute | solution.py:10
  83.9 1.0 %copy-start.4 = (f32[1,2,2,2,32,256]{5,4,3,2,1,0:T(8,128)S(1)}, f32[1,2,2,2,32,256]{5,4,3,2,1,0:T(8,128)}, u32[]{:S(2)}) copy-start(f32[1,2,2,2,32,256]{5,4,3,2,1,0:T(8,128)} %copy-done.3) | copy-start | bytes 786436

commit v2 on v1

v2 whole, which is shorter than its diff:
```python
import jax
import jax.numpy as jnp
from jax import lax
from jax.sharding import PartitionSpec as P

ITERS = 4


def flip(x, axis, bit):
    return lax.ppermute(x, axis, [(i, i ^ (1 << bit)) for i in range(lax.axis_size(axis))])


def product(left, right):
    return jnp.dot(left, right, precision=lax.Precision.HIGHEST, preferred_element_type=jnp.float32)


def transposed_product(left, right):
    return lax.dot_general(
        left,
        right,
        (((0,), (0,)), ((), ())),
        precision=lax.Precision.HIGHEST,
        preferred_element_type=jnp.float32,
    )


def jacobi(couple_first, rhs_first, couple_second, rhs_second):
    update_first = rhs_second
    update_second = rhs_first
    for sweep_index in range(ITERS - 1):
        update_first, update_second = (
            rhs_second - product(couple_second, update_second),
            rhs_first - product(couple_first, update_first),
        )
    return (update_first, update_second)


def swap_blocks(x, blocks):
    groups = [list(range(blocks)), list(range(blocks, 2 * blocks))]
    return lax.all_to_all(x, "leaf", 0, 0, axis_index_groups=groups)


def body(low_solved, low_basis, upper_solved, upper_basis):
    rank = low_solved.shape[1]
    leaves = lax.axis_size("leaf")
    bits = leaves.bit_length() - 2
    blocks = 1 << bits
    index = lax.axis_index("leaf")
    half = index // blocks
    joined = jnp.concatenate([low_solved, upper_solved], axis=1)
    low_terms = transposed_product(low_basis, joined).reshape(blocks, rank // blocks, 3 * rank)
    low_parts = swap_blocks(low_terms, blocks)
    upper_terms = transposed_product(upper_basis, joined).reshape(blocks, rank // blocks, 3 * rank)
    upper_parts = swap_blocks(upper_terms, blocks)
    mine = jnp.sum(low_parts, axis=0)
    theirs = flip(mine, "leaf", bits)
    both = jnp.stack([jnp.where(half == 0, mine, theirs), jnp.where(half == 0, theirs, mine)])
    low = swap_blocks(jnp.broadcast_to(both, (blocks,) + both.shape), blocks)
    low = low.transpose(1, 0, 2, 3).reshape(2, rank, 3 * rank)
    update_first, update_second = jacobi(
        low[0, :, :rank], low[0, :, rank:], low[1, :, :rank], low[1, :, rank:]
    )
    own_update = jnp.where(half == 0, update_first, update_second)
    upper = jnp.sum(upper_parts, axis=0)
    rows = upper[:, rank:] - product(upper[:, :rank], own_update)
    rows = rows + flip(rows, "leaf", bits)
    group_total = swap_blocks(jnp.broadcast_to(rows, (blocks,) + rows.shape), blocks)
    group_total = group_total.reshape(rank, 2 * rank)
    sibling = flip(group_total, "group", 0)
    middle = upper_solved - product(low_solved, own_update)
    pair_solved = middle[:, :rank]
    parity = lax.axis_index("group") % 2
    first_group = jnp.where(parity == 0, group_total, sibling)
    second_group = jnp.where(parity == 0, sibling, group_total)
    pair_first, pair_second = jacobi(
        first_group[:, :rank],
        first_group[:, rank:],
        second_group[:, :rank],
        second_group[:, rank:],
    )
    pair_update = jnp.where(parity == 0, pair_first, pair_second)
    next_solved = middle[:, rank:] - product(pair_solved, pair_update)
    return (pair_solved, next_solved)


def solution(mesh):
    spec = P(("group", "leaf"), None)
    return jax.shard_map(
        body,
        mesh=mesh,
        in_specs=(spec, spec, spec, spec),
        out_specs=(spec, spec),
        check_vma=False,
    )
```

time: 90.4 us -> 95.8 us (1.060)
  starting transfers between devices: 38.4 us -> 18.2 us
  waiting for transfers between devices: 24.7 us -> 43.4 us
  blocking collectives: 0 us -> 11.1 us
  other arithmetic: 4.91 us -> 1.43 us
    ppermute x30 -> x3, starting transfers between devices: 38.4 us -> 3.45 us  [flip(): lax.ppermute(x, axis, [(i, i ^ 1 << bit) for i in range(lax.axis_size(axi...]
    all_to_all x0 -> x3, waiting for transfers between devices: none -> 30.8 us  [swap_blocks(): return lax.all_to_all(x, 'leaf', 0, 0, axis_index_groups=groups)]
    all_to_all x0 -> x3, starting transfers between devices: none -> 14.7 us  [swap_blocks(): return lax.all_to_all(x, 'leaf', 0, 0, axis_index_groups=groups)]
    ppermute x30 -> x3, waiting for transfers between devices: 24.7 us -> 12.6 us  [flip(): lax.ppermute(x, axis, [(i, i ^ 1 << bit) for i in range(lax.axis_size(axi...]
    all_to_all x0 -> x1, blocking collectives: none -> 11.1 us  [swap_blocks(): return lax.all_to_all(x, 'leaf', 0, 0, axis_index_groups=groups)]
    add x9 -> x1, other arithmetic: 2.1 us -> 0.01 us  [body(): rows = rows + flip(rows, 'leaf', bits)]
    unnamed x24 -> x12, local copies, waits for them, and re-layouts: 5.18 us -> 3.78 us
    broadcast_in_dim x0 -> x2, local copies, waits for them, and re-layouts: none -> 1.35 us  [the longest x1 1.3 us: body(): low = swap_blocks(jnp.broadcast_to(both, (blocks,) + both.shape), blocks)]
  transfers between devices with their start and end apart: 30 -> 6, of which waited for: 19 -> 5; matrix products, arithmetic and copies ran while one was open for 11% -> 7% of each run, Pallas kernels for 0% -> 0%
where the time goes in v2:
time: 95.8 us; the launch traced here: 95.3 us
  waiting for transfers between devices  43.4 us (45%)
  starting transfers between devices  18.2 us (19%)
  matrix products  15 us (16%)
  blocking collectives  11.1 us (12%)
  local copies, waits for them, and re-layouts  5.37 us (6%)
  other arithmetic  1.43 us (1%)
    all_to_all x3, waiting for transfers between devices, swap_blocks(): return lax.all_to_all(x, 'leaf', 0, 0, axis_index_groups=groups)  30.8 us
    all_to_all x3, starting transfers between devices, swap_blocks(): return lax.all_to_all(x, 'leaf', 0, 0, axis_index_groups=groups)  14.7 us
    ppermute x3, waiting for transfers between devices, flip(): lax.ppermute(x, axis, [(i, i ^ 1 << bit) for i in range(lax.axis_size(axi...  12.6 us
    all_to_all x1, blocking collectives, swap_blocks(): return lax.all_to_all(x, 'leaf', 0, 0, axis_index_groups=groups)  11.1 us
    dot_general x15, matrix products, product(): jnp.dot(left, right, precision=lax.Precision.HIGHEST, preferred_element_t...  10 us
    dot_general x2, matrix products, transposed_product(): lax.dot_general(left, right, (((0,), (0,)), ((), ())), precision=lax.Prec...  4.94 us
    unnamed x12, local copies, waits for them, and re-layouts  3.78 us
    ppermute x3, starting transfers between devices, flip(): lax.ppermute(x, axis, [(i, i ^ 1 << bit) for i in range(lax.axis_size(axi...  3.45 us
  transfers between devices with their start and end apart: 6, of which 5 were waited for; matrix products, arithmetic and copies ran while one was open for 7% of the time, Pallas kernels for 0%

profile of v2, /device:TPU:0, one launch (start us, length us, event | category | flops | bytes accessed | tf_op | source)
XLA Modules:
  0.0 95.3 jit_solution(622401895018957308)
XLA Ops:
  0.6 0.0 copy-start
  0.6 0.0 copy-start.1
  0.7 1.2 %constant_dynamic-update-slice_fusion.1 = f32[512,768]{1,0:T(8,128)S(1)} fusion(f32[512,256]{1,0:T(8,128)} %param.4), kind=kLoop, calls=%fused_computation.37 | loop fusion | bytes 1048576
  1.9 0.2 copy-done.1
  2.1 0.1 constant_dynamic-update-slice_fusion
  2.2 0.0 copy-done
  2.2 0.0 copy-start.3
  2.2 2.5 %fusion.13 = f32[768,256]{0,1:T(8,128)} fusion(f32[512,768]{1,0:T(8,128)S(1)} %constant_dynamic-update-slice_fusion, f32[512,256]{1,0:T(8,128)S(1)} %copy-done), kind=kOutput, calls=%fused_computation.39 | convolution fusion | flops 1207959552 | bytes 2883584 | tf_op jit(solution)/shard_map/dot_general | solution.py:18
  4.6 6.2 %all-to-all-start = ((f32[8,32,768]{2,1,0:T(8,128)}), f32[8,32,768]{2,1,0:T(8,128)S(1)}, u32[]{:S(2)}, u32[]{:S(2)}) async-start(f32[8,32,768]{2,1,0:T(8,128)} %bitcast.71), calls=%async_computation | async-start | bytes 1572864 | tf_op jit(solution)/shard_map/all_to_all | solution.py:40
  10.8 0.0 copy-done.3
  10.8 2.5 %fusion.14 = f32[768,256]{0,1:T(8,128)} fusion(f32[512,768]{1,0:T(8,128)S(1)} %constant_dynamic-update-slice_fusion, f32[512,256]{1,0:T(8,128)S(1)} %copy-done.3), kind=kOutput, calls=%fused_computation.40 | convolution fusion | flops 1207959552 | bytes 2883584 | tf_op jit(solution)/shard_map/dot_general | solution.py:18
  13.3 9.2 %all-to-all-done = f32[8,32,768]{2,1,0:T(8,128)S(1)} async-done(((f32[8,32,768]{2,1,0:T(8,128)}), f32[8,32,768]{2,1,0:T(8,128)S(1)}, u32[]{:S(2)}, u32[]{:S(2)}) %all-to-all-start) | async-done | bytes 786464 | tf_op jit(solution)/shard_map/all_to_all | solution.py:40
  22.5 3.5 %all-to-all-start.2 = ((f32[8,32,768]{2,1,0:T(8,128)}), f32[8,32,768]{2,1,0:T(8,128)S(1)}, u32[]{:S(2)}, u32[]{:S(2)}) async-start(f32[8,32,768]{2,1,0:T(8,128)} %bitcast.70), calls=%async_computation.2 | async-start | bytes 1572864 | tf_op jit(solution)/shard_map/all_to_all | solution.py:40
  26.1 2.7 %collective-permute-start = (f32[32,768]{1,0:T(8,128)S(1)}, f32[32,768]{1,0:T(8,128)S(1)}, u32[]{:S(2)}, u32[]{:S(2)}) collective-permute-start(f32[32,768]{1,0:T(8,128)S(1)} %reduce_sum.18), channel_id=1, source_target_pairs={{0,16},{2,18},{4,20},{6,22},{8,24},{10,26},{12,28},{14,30},{16,0},... | collective-permute-start | bytes 294920 | tf_op jit(solution)/shard_map/ppermute | solution.py:10
  28.8 7.4 %collective-permute-done = f32[32,768]{1,0:T(8,128)S(1)} collective-permute-done((f32[32,768]{1,0:T(8,128)S(1)}, f32[32,768]{1,0:T(8,128)S(1)}, u32[]{:S(2)}, u32[]{:S(2)}) %collective-permute-start) | collective-permute-done | bytes 98336 | tf_op jit(solution)/shard_map/ppermute | solution.py:10
  36.2 2.9 %all-to-all-done.2 = f32[8,32,768]{2,1,0:T(8,128)S(1)} async-done(((f32[8,32,768]{2,1,0:T(8,128)}), f32[8,32,768]{2,1,0:T(8,128)S(1)}, u32[]{:S(2)}, u32[]{:S(2)}) %all-to-all-start.2) | async-done | bytes 786464 | tf_op jit(solution)/shard_map/all_to_all | solution.py:40
  39.2 1.3 %broadcast_in_dim.6 = f32[8,2,32,768]{3,2,1,0:T(8,128)} broadcast(f32[2,32,768]{2,1,0:T(8,128)S(1)} %pad_maximum_fusion), dimensions={1,2,3} | broadcast | bytes 1769472 | tf_op jit(solution)/shard_map/broadcast_in_dim | solution.py:58
  40.5 5.0 %all-to-all-start.1 = ((f32[8,2,32,768]{3,2,1,0:T(8,128)}), f32[8,2,32,768]{3,2,1,0:T(8,128)S(1)}, u32[]{:S(2)}, u32[]{:S(2)}) async-start(f32[8,2,32,768]{3,2,1,0:T(8,128)} %broadcast_in_dim.6), calls=%async_computation.1 | async-start | bytes 3145728 | tf_op jit(solution)/shard_map/all_to_all | solution.py:40
  45.6 18.7 %all-to-all-done.1 = f32[8,2,32,768]{3,2,1,0:T(8,128)S(1)} async-done(((f32[8,2,32,768]{3,2,1,0:T(8,128)}), f32[8,2,32,768]{3,2,1,0:T(8,128)S(1)}, u32[]{:S(2)}, u32[]{:S(2)}) %all-to-all-start.1) | async-done | bytes 1572896 | tf_op jit(solution)/shard_map/all_to_all | solution.py:40
  64.2 0.1 copy.10
  64.4 0.6 convolution_subtract_fusion.3
  65.0 0.6 convolution_subtract_fusion.6
  65.6 0.6 convolution_subtract_fusion.2
  66.3 0.6 convolution_subtract_fusion.5
  66.9 0.6 convolution_subtract_fusion.4
  67.5 0.6 fusion.1
  68.2 0.0 copy-start.2
  68.2 0.4 convolution_subtract_fusion.13
  68.6 0.8 collective-permute-start.1
  69.4 5.1 %collective-permute-done.1 = f32[32,512]{1,0:T(8,128)S(1)} collective-permute-done((f32[32,512]{1,0:T(8,128)S(1)}, f32[32,512]{1,0:T(8,128)S(1)}, u32[]{:S(2)}, u32[]{:S(2)}) %collective-permute-start.1) | collective-permute-done | bytes 65568 | tf_op jit(solution)/shard_map/ppermute | solution.py:10
  74.5 0.1 broadcast_in_dim.7
  74.6 11.1 %all_to_all.20 = f32[8,32,512]{2,1,0:T(8,128)} all-to-all(f32[8,32,512]{2,1,0:T(8,128)S(1)} %broadcast_in_dim.7), channel_id=1, replica_groups={{0,2,4,6,8,10,12,14},{16,18,20,22,24,26,28,30},{1,3,5,7,9,11,13,15},{17..., dimensions={0} | all-to-all | bytes 1048576 | tf_op jit(solution)/shard_map/all_to_all | solution.py:40
  85.7 0.0 collective-permute-start.2
  85.7 0.0 copy-done.2
  85.7 0.3 copy.11
  86.1 2.9 %fusion = f32[512,512]{0,1:T(8,128)S(1)} fusion(f32[512,512]{0,1:T(8,128)S(1)} %copy.11, f32[256,512]{1,0:T(8,128)S(1)} %fusion.1, f32[512,256]{1,0:T(8,128)} %param.4), kind=kOutput, calls=%fused_computation.1 | convolution fusion | flops 805568512 | bytes 3145728 | tf_op jit(solution)/shard_map/dot_general | solution.py:14
  89.0 1.0 %copy.13 = f32[512,256]{1,0:T(8,128)} copy(f32[512,256]{0,1:T(8,128)S(1)} %slice.52) | data formatting | bytes 1048576
  90.0 0.0 collective-permute-done.2
  90.0 1.3 %broadcast_select_fusion.1 = (f32[256,512]{1,0:T(8,128)S(1)}, f32[256,512]{1,0:T(8,128)S(1)}) fusion(f32[256,512]{1,0:T(8,128)} %collective-permute-done.2, pred[]{:T(512)S(6)} %eq.7, f32[8,32,512]{2,1,0:T(8,128)} %all_to_all.20), kind=kLoop, calls=%fused_computation.23 | loop fusion | flops 262144 | bytes 2097153 | tf_op jit(solution)/shard_map/jit(_where)/select_n | solution.py:74
  91.3 0.4 convolution_subtract_fusion.12
  91.7 0.4 convolution_subtract_fusion.9
  92.1 0.4 convolution_subtract_fusion.11
  92.5 0.4 convolution_subtract_fusion.8
  92.9 0.4 convolution_subtract_fusion.7
  93.3 0.4 fusion.2
  93.7 0.7 convolution_subtract_fusion
  94.3 1.0 %copy.14 = f32[512,256]{1,0:T(8,128)} copy(f32[512,256]{0,1:T(8,128)S(1)} %convolution_subtract_fusion) | data formatting | bytes 1048576
  (6 shorter events, 0.2 us)
Async XLA Ops:
  0.6 1.5 %copy-start = (f32[512,256]{1,0:T(8,128)S(1)}, f32[512,256]{1,0:T(8,128)}, u32[]{:S(2)}) copy-start(f32[512,256]{1,0:T(8,128)} %param.5) | copy-start | bytes 1572868
  0.6 1.4 %copy-start.1 = (f32[512,512]{1,0:T(8,128)S(1)}, f32[512,512]{1,0:T(8,128)}, u32[]{:S(2)}) copy-start(f32[512,512]{1,0:T(8,128)} %param.6) | copy-start | bytes 3145732
  2.2 8.7 %copy-start.3 = (f32[512,256]{1,0:T(8,128)S(1)}, f32[512,256]{1,0:T(8,128)}, u32[]{:S(2)}) copy-start(f32[512,256]{1,0:T(8,128)} %param.7) | copy-start | bytes 1572868
  4.6 17.9 %all-to-all-start = ((f32[8,32,768]{2,1,0:T(8,128)}), f32[8,32,768]{2,1,0:T(8,128)S(1)}, u32[]{:S(2)}, u32[]{:S(2)}) async-start(f32[8,32,768]{2,1,0:T(8,128)} %bitcast.71), calls=%async_computation | async-start | bytes 1572864 | tf_op jit(solution)/shard_map/all_to_all | solution.py:40
  22.5 16.7 %all-to-all-start.2 = ((f32[8,32,768]{2,1,0:T(8,128)}), f32[8,32,768]{2,1,0:T(8,128)S(1)}, u32[]{:S(2)}, u32[]{:S(2)}) async-start(f32[8,32,768]{2,1,0:T(8,128)} %bitcast.70), calls=%async_computation.2 | async-start | bytes 1572864 | tf_op jit(solution)/shard_map/all_to_all | solution.py:40
  26.1 10.1 %collective-permute-start = (f32[32,768]{1,0:T(8,128)S(1)}, f32[32,768]{1,0:T(8,128)S(1)}, u32[]{:S(2)}, u32[]{:S(2)}) collective-permute-start(f32[32,768]{1,0:T(8,128)S(1)} %reduce_sum.18), channel_id=1, source_target_pairs={{0,16},{2,18},{4,20},{6,22},{8,24},{10,26},{12,28},{14,30},{16,0},... | collective-permute-start | bytes 294920 | tf_op jit(solution)/shard_map/ppermute | solution.py:10
  40.5 23.7 %all-to-all-start.1 = ((f32[8,2,32,768]{3,2,1,0:T(8,128)}), f32[8,2,32,768]{3,2,1,0:T(8,128)S(1)}, u32[]{:S(2)}, u32[]{:S(2)}) async-start(f32[8,2,32,768]{3,2,1,0:T(8,128)} %broadcast_in_dim.6), calls=%async_computation.1 | async-start | bytes 3145728 | tf_op jit(solution)/shard_map/all_to_all | solution.py:40
  68.2 17.5 %copy-start.2 = (f32[512,512]{1,0:T(8,128)S(1)}, f32[512,512]{1,0:T(8,128)}, u32[]{:S(2)}) copy-start(f32[512,512]{1,0:T(8,128)} %param.6) | copy-start | bytes 3145732
  68.6 5.9 %collective-permute-start.1 = (f32[32,512]{1,0:T(8,128)S(1)}, f32[32,512]{1,0:T(8,128)S(1)}, u32[]{:S(2)}, u32[]{:S(2)}) collective-permute-start(f32[32,512]{1,0:T(8,128)S(1)} %convolution_subtract_fusion.13), channel_id=1, source_target_pairs={{0,16},{2,18},{4,20},{6,22},{8,24},{10,26},{12,28},{14,30},{16,0},... | collective-permute-start | bytes 196616 | tf_op jit(solution)/shard_map/ppermute | solution.py:10
  85.7 4.3 %collective-permute-start.2 = (f32[256,512]{1,0:T(8,128)}, f32[256,512]{1,0:T(8,128)}, u32[]{:S(2)}, u32[]{:S(2)}) collective-permute-start(f32[256,512]{1,0:T(8,128)} %bitcast.13), channel_id=1, source_target_pairs={{0,1},{1,0},{2,3},{3,2},{4,5},{5,4},{6,7},{7,6},{8,9},{9,8},{10,11... | collective-permute-start | bytes 1572872 | tf_op jit(solution)/shard_map/ppermute | solution.py:10

commit v3 on v2

v3 whole, which is shorter than its diff:
```python
import functools

import jax
import jax.numpy as jnp
from jax import lax
from jax.experimental import pallas as pl
from jax.experimental.pallas import tpu as pltpu
from jax.sharding import PartitionSpec as P

AXES = ("leaf", "group")


def axis_order(chain, core, bits, stage):
    if chain == "low":
        first = core
    else:
        first = 2
    order = [(first + t) % bits for t in range(bits)]
    return order if stage == "scatter" else order[::-1]


def relative_bits(order, r, first_is_high):
    bits = len(order)
    out = 0
    for t in range(bits):
        place = bits - 1 - t if first_is_high else t
        if (r >> place) & 1:
            out |= 1 << order[t]
    return out


def step(x, chain, t, bits, stage):
    leaves, groups = lax.axis_size("leaf"), lax.axis_size("group")
    pairs = []
    for leaf in range(leaves):
        for group in range(groups):
            bit = axis_order(chain, group % 2, bits, stage)[t]
            pairs.append((leaf * groups + group, (leaf ^ (1 << bit)) * groups + group))
    return lax.ppermute(x, AXES, pairs)


def flip(x, axis, bit):
    return lax.ppermute(x, axis, [(i, i ^ (1 << bit)) for i in range(lax.axis_size(axis))])


def split(x):
    high = x.astype(jnp.bfloat16)
    low = (x - high.astype(jnp.float32)).astype(jnp.bfloat16)
    return high, low


def dot3(left, right, dims=(((1,), (0,)), ((), ()))):
    dot = functools.partial(
        lax.dot_general, dimension_numbers=dims, preferred_element_type=jnp.float32
    )
    return dot(left[0], right[0]) + (dot(left[0], right[1]) + dot(left[1], right[0]))


def block_of(r, chain, bits, stage):
    orders = [axis_order(chain, core, bits, stage) for core in range(2)]
    moves = [relative_bits(order, r, stage == "scatter") for order in orders]
    own = lax.rem(lax.axis_index("leaf"), 1 << bits)
    core = lax.rem(lax.axis_index("group"), 2)
    return lax.bitwise_xor(own, jnp.where(core == 0, moves[0], moves[1]))


def local_kernel(chain, bits, basis_ref, y_ref, z_ref, send_ref, keep_ref, sums):
    rank = y_ref.shape[1]
    blocks = 1 << bits
    rows = rank // blocks
    dims = (((0,), (0,)), ((), ()))
    basis = split(basis_ref[...])
    sums[:, :rank] = dot3(basis, split(y_ref[...]), dims)
    sums[:, rank:] = dot3(basis, split(z_ref[...]), dims)
    for r in range(blocks):
        start = pl.multiple_of(block_of(r, chain, bits, "scatter") * rows, rows)
        target = send_ref if r >= blocks // 2 else keep_ref
        target[r % (blocks // 2)] = sums[pl.ds(start, rows), :]


def place(parts, chain, bits, target):
    blocks = 1 << bits
    rows = target.shape[-2] // blocks
    for r in range(blocks):
        start = pl.multiple_of(block_of(r, chain, bits, "gather") * rows, rows)
        piece = parts[r // (blocks // 2)][r % (blocks // 2)]
        if len(target.shape) == 3:
            target[:, pl.ds(start, rows), :] = piece
        else:
            target[pl.ds(start, rows), :] = piece


def solve_kernel(bits, first_ref, second_ref, update_ref, terms):
    rank = update_ref.shape[1]
    place((first_ref, second_ref), "low", bits, terms)
    couples = [split(terms[i, :, :rank]) for i in range(2)]
    for i in range(2):
        mine, other = couples[i], couples[1 - i]
        start = terms[1 - i, :, rank:] - dot3(other, split(terms[i, :, rank:]))
        update_ref[i] = start + dot3(other, split(dot3(mine, split(start))))


def total_kernel(bits, first_ref, second_ref, update_ref, total_ref, terms):
    rank = total_ref.shape[0]
    place((first_ref, second_ref), "high", bits, terms)
    total = terms[:, 2 * rank :]
    for i in range(2):
        total = total - dot3(split(terms[:, i * rank : (i + 1) * rank]), split(update_ref[i]))
    total_ref[...] = total


def middle_kernel(y_ref, z_ref, update_ref, pair_ref, next_ref):
    rank = y_ref.shape[1]
    middle = z_ref[...] - dot3(split(y_ref[...]), split(update_ref[0]))
    pair_ref[...] = middle[:, :rank]
    next_ref[...] = middle[:, rank:]


def final_kernel(mine_ref, other_ref, pair_ref, next_ref, out_ref):
    rank = mine_ref.shape[0]
    mine = split(mine_ref[:, :rank])
    other = split(other_ref[:, :rank])
    start = other_ref[:, rank:] - dot3(other, split(mine_ref[:, rank:]))
    update = start + dot3(other, split(dot3(mine, split(start))))
    out_ref[...] = next_ref[...] - dot3(split(pair_ref[...]), split(update))


def run(kernel, shapes, args, scratch=(), flops=0):
    bytes_moved = sum(a.size * 4 for a in args) + sum(4 * s.size for s in shapes)
    return pl.pallas_call(
        kernel,
        out_shape=shapes,
        in_specs=[pl.BlockSpec(memory_space=pltpu.VMEM)] * len(args),
        out_specs=[pl.BlockSpec(memory_space=pltpu.VMEM)] * len(shapes),
        scratch_shapes=list(scratch),
        compiler_params=pltpu.CompilerParams(vmem_limit_bytes=24 * 1024 * 1024),
        cost_estimate=pl.CostEstimate(flops=flops, bytes_accessed=bytes_moved, transcendentals=0),
    )(*args)


def array(*shape):
    return jax.ShapeDtypeStruct(shape, jnp.float32)


def body(low_solved, low_basis, upper_solved, upper_basis):
    depth, rank = low_solved.shape
    leaves = lax.axis_size("leaf")
    bits = leaves.bit_length() - 2
    blocks = 1 << bits
    rows = rank // blocks
    unit = 6 * rank * rank

    def scatter_terms(chain, basis):
        half = array(blocks // 2, rows, 3 * rank)
        return run(
            functools.partial(local_kernel, chain, bits),
            [half, half],
            [basis, low_solved, upper_solved],
            [pltpu.VMEM((rank, 3 * rank), jnp.float32)],
            flops=3 * unit * depth,
        )

    def scatter(chain, send, keep):
        for t in range(bits):
            got = step(send, chain, t, bits, "scatter")
            if t == bits - 1:
                return keep[0] + got[0]
            half = keep.shape[0] // 2
            send = keep[half:] + got[half:]
            keep = keep[:half] + got[:half]

    def gather(chain, x):
        for t in range(bits):
            got = step(x, chain, t, bits, "gather")
            if t == bits - 1:
                return x, got
            x = jnp.concatenate([x, got], axis=0)

    low_mine = scatter("low", *scatter_terms("low", low_basis))
    low_other = flip(low_mine, "leaf", bits)
    low_parts = gather("low", jnp.stack([low_mine, low_other])[None])

    high_mine = scatter("high", *scatter_terms("high", upper_basis))
    high_other = flip(high_mine, "leaf", bits)
    joined = jnp.concatenate(
        [high_mine[:, :rank], high_other[:, :rank], high_mine[:, rank:] + high_other[:, rank:]],
        axis=1,
    )
    high_parts = gather("high", joined[None])

    (update,) = run(
        functools.partial(solve_kernel, bits),
        [array(2, rank, 2 * rank)],
        low_parts,
        [pltpu.VMEM((2, rank, 3 * rank), jnp.float32)],
        flops=12 * unit * rank,
    )
    (total,) = run(
        functools.partial(total_kernel, bits),
        [array(rank, 2 * rank)],
        [*high_parts, update],
        [pltpu.VMEM((rank, 4 * rank), jnp.float32)],
        flops=4 * unit * rank,
    )
    sibling = flip(total, "group", 0)
    pair_solved, next_terms = run(
        middle_kernel,
        [array(depth, rank), array(depth, rank)],
        [low_solved, upper_solved, update],
        flops=2 * unit * depth,
    )
    (next_solved,) = run(
        final_kernel,
        [array(depth, rank)],
        [total, sibling, pair_solved, next_terms],
        flops=3 * unit * rank + unit * depth,
    )
    return pair_solved, next_solved


def solution(mesh):
    spec = P(("group", "leaf"), None)
    return jax.shard_map(
        body,
        mesh=mesh,
        in_specs=(spec, spec, spec, spec),
        out_specs=(spec, spec),
        check_vma=False,
    )
```

time: 95.8 us -> 80.4 us (0.84)
  matrix products: 15 us -> 0 us
  blocking collectives: 11.1 us -> 0 us
  Pallas kernels: 0 us -> 8.09 us
  starting transfers between devices: 18.2 us -> 23 us
  other arithmetic: 1.43 us -> 0.32 us
    ppermute x0 -> x12, waiting for transfers between devices: none -> 42.6 us  [step(): return lax.ppermute(x, AXES, pairs)]
    all_to_all x3 -> x0, waiting for transfers between devices: 30.8 us -> none  [swap_blocks(): return lax.all_to_all(x, 'leaf', 0, 0, axis_index_groups=groups)]
    ppermute x0 -> x12, starting transfers between devices: none -> 17.6 us  [step(): return lax.ppermute(x, AXES, pairs)]
    dot_general x17 -> x0, matrix products: 15 us -> none  [the longest x15 10 us: product(): jnp.dot(left, right, precision=lax.Precision.HIGHEST, preferred_element_t...]
    all_to_all x3 -> x0, starting transfers between devices: 14.7 us -> none  [swap_blocks(): return lax.all_to_all(x, 'leaf', 0, 0, axis_index_groups=groups)]
    ppermute x3, waiting for transfers between devices: 12.6 us -> 0.58 us  [flip(): lax.ppermute(x, axis, [(i, i ^ 1 << bit) for i in range(lax.axis_size(axi...]
    all_to_all x1 -> x0, blocking collectives: 11.1 us -> none  [swap_blocks(): return lax.all_to_all(x, 'leaf', 0, 0, axis_index_groups=groups)]
    pallas_call x0 -> x6, Pallas kernels: none -> 8.09 us  [run(): pl.pallas_call(kernel, out_shape=shapes, in_specs=[pl.BlockSpec(memory_sp...]
  transfers between devices with their start and end apart: 6 -> 15, of which waited for: 5 -> 11; matrix products, arithmetic and copies ran while one was open for 7% -> 0% of each run, Pallas kernels for 0% -> 5%
where the time goes in v3:
time: 80.4 us; the launch traced here: 80 us
  waiting for transfers between devices  43.2 us (54%)
  starting transfers between devices  23 us (29%)
  Pallas kernels  8.09 us (10%)
  local copies, waits for them, and re-layouts  4.64 us (6%)
  between operations  0.82 us (1%)
    ppermute x12, waiting for transfers between devices, step(): return lax.ppermute(x, AXES, pairs)  42.6 us
    ppermute x12, starting transfers between devices, step(): return lax.ppermute(x, AXES, pairs)  17.6 us
    pallas_call x6, Pallas kernels, run(): pl.pallas_call(kernel, out_shape=shapes, in_specs=[pl.BlockSpec(memory_sp...  8.09 us
    ppermute x3, starting transfers between devices, flip(): lax.ppermute(x, axis, [(i, i ^ 1 << bit) for i in range(lax.axis_size(axi...  5.33 us
    unnamed x14, local copies, waits for them, and re-layouts  4.63 us
  transfers between devices with their start and end apart: 15, of which 11 were waited for; matrix products, arithmetic and copies ran while one was open for 0% of the time, Pallas kernels for 5%

profile of v3, /device:TPU:0, one launch (start us, length us, event | category | flops | bytes accessed | tf_op | source)
XLA Modules:
  0.0 80.0 jit_solution(15351201867842806351)
XLA Ops:
  0.6 0.0 copy-start
  0.6 1.2 %copy-done = f32[512,512]{1,0:T(8,128)S(1)} copy-done((f32[512,512]{1,0:T(8,128)S(1)}, f32[512,512]{1,0:T(8,128)}, u32[]{:S(2)}) %copy-start) | copy-done | bytes 1048600
  1.9 0.0 copy-start.2
  1.9 1.0 %copy-done.2 = f32[512,256]{1,0:T(8,128)S(1)} copy-done((f32[512,256]{1,0:T(8,128)S(1)}, f32[512,256]{1,0:T(8,128)}, u32[]{:S(2)}) %copy-start.2) | copy-done | bytes 524312
  2.9 1.0 %copy-done.5 = f32[512,256]{1,0:T(8,128)S(1)} copy-done((f32[512,256]{1,0:T(8,128)S(1)}, f32[512,256]{1,0:T(8,128)}, u32[]{:S(2)}) %copy-start.5) | copy-done | bytes 524312
  3.9 0.9 %shard_map.59 = (f32[4,32,768]{2,1,0:T(8,128)S(1)}, f32[4,32,768]{2,1,0:T(8,128)S(1)}) custom-call(f32[512,256]{1,0:T(8,128)S(1)} %copy-done.5, f32[512,256]{1,0:T(8,128)S(1)} %copy-done.2, f32[512,512]{1,0:T(8,128)S(1)} %copy-done), custom_call_target="tpu_custom_call" | custom-call | flops 603979776 | bytes 2883584 | tf_op jit(solution)/shard_map/pallas_call | solution.py:130
  4.8 0.0 copy-start.1
  4.9 3.0 %collective-permute-start = (f32[4,32,768]{2,1,0:T(8,128)S(1)}, f32[4,32,768]{2,1,0:T(8,128)S(1)}, u32[]{:S(2)}, u32[]{:S(2)}) collective-permute-start(f32[4,32,768]{2,1,0:T(8,128)S(1)} %get-tuple-element.9), channel_id=1, source_target_pairs={{0,2},{1,5},{2,0},{3,7},{4,6},{5,1},{6,4},{7,3},{8,10},{9,13},{10,... | collective-permute-start | bytes 1179656 | tf_op jit(solution)/shard_map/ppermute | solution.py:39
  7.9 5.8 %collective-permute-done = f32[4,32,768]{2,1,0:T(8,128)S(1)} collective-permute-done((f32[4,32,768]{2,1,0:T(8,128)S(1)}, f32[4,32,768]{2,1,0:T(8,128)S(1)}, u32[]{:S(2)}, u32[]{:S(2)}) %collective-permute-start) | collective-permute-done | bytes 393248 | tf_op jit(solution)/shard_map/ppermute | solution.py:39
  13.7 2.1 %collective-permute-start.1 = (f32[2,32,768]{2,1,0:T(8,128)S(1)}, f32[2,32,768]{2,1,0:T(8,128)S(1)}, u32[]{:S(2)}, u32[]{:S(2)}) collective-permute-start(f32[2,32,768]{2,1,0:T(8,128)S(1)} %get-tuple-element.17), channel_id=1, source_target_pairs={{0,4},{1,9},{2,6},{3,11},{4,0},{5,13},{6,2},{7,15},{8,12},{9,1},{1... | collective-permute-start | bytes 589832 | tf_op jit(solution)/shard_map/ppermute | solution.py:39
  15.8 0.0 copy-done.6
  15.8 0.0 copy-done.1
  15.8 0.9 %shard_map.62 = (f32[4,32,768]{2,1,0:T(8,128)S(1)}, f32[4,32,768]{2,1,0:T(8,128)S(1)}) custom-call(f32[512,256]{1,0:T(8,128)S(1)} %copy-done.6, f32[512,256]{1,0:T(8,128)S(1)} %copy-done.2, f32[512,512]{1,0:T(8,128)S(1)} %copy-done.1), custom_call_target="tpu_custom_call" | custom-call | flops 603979776 | bytes 2883584 | tf_op jit(solution)/shard_map/pallas_call | solution.py:130
  16.7 1.6 %collective-permute-start.7 = (f32[4,32,768]{2,1,0:T(8,128)S(1)}, f32[4,32,768]{2,1,0:T(8,128)S(1)}, u32[]{:S(2)}, u32[]{:S(2)}) collective-permute-start(f32[4,32,768]{2,1,0:T(8,128)S(1)} %get-tuple-element.12), channel_id=1, source_target_pairs={{0,8},{1,9},{2,10},{3,11},{4,12},{5,13},{6,14},{7,15},{8,0},{9,1},... | collective-permute-start | bytes 1179656 | tf_op jit(solution)/shard_map/ppermute | solution.py:39
  18.3 1.1 %collective-permute-done.1 = f32[2,32,768]{2,1,0:T(8,128)S(1)} collective-permute-done((f32[2,32,768]{2,1,0:T(8,128)S(1)}, f32[2,32,768]{2,1,0:T(8,128)S(1)}, u32[]{:S(2)}, u32[]{:S(2)}) %collective-permute-start.1) | collective-permute-done | bytes 196640 | tf_op jit(solution)/shard_map/ppermute | solution.py:39
  19.4 2.1 %collective-permute-start.2 = (f32[1,32,768]{2,1,0:T(8,128)S(1)}, f32[1,32,768]{2,1,0:T(8,128)S(1)}, u32[]{:S(2)}, u32[]{:S(2)}) collective-permute-start(f32[1,32,768]{2,1,0:T(8,128)S(1)} %slice_add_fusion.6), channel_id=1, source_target_pairs={{0,8},{1,3},{2,10},{3,1},{4,12},{5,7},{6,14},{7,5},{8,0},{9,11},{1... | collective-permute-start | bytes 294920 | tf_op jit(solution)/shard_map/ppermute | solution.py:39
  21.6 4.9 %collective-permute-done.7 = f32[4,32,768]{2,1,0:T(8,128)S(1)} collective-permute-done((f32[4,32,768]{2,1,0:T(8,128)S(1)}, f32[4,32,768]{2,1,0:T(8,128)S(1)}, u32[]{:S(2)}, u32[]{:S(2)}) %collective-permute-start.7) | collective-permute-done | bytes 393248 | tf_op jit(solution)/shard_map/ppermute | solution.py:39
  26.6 1.6 %collective-permute-start.8 = (f32[2,32,768]{2,1,0:T(8,128)S(1)}, f32[2,32,768]{2,1,0:T(8,128)S(1)}, u32[]{:S(2)}, u32[]{:S(2)}) collective-permute-start(f32[2,32,768]{2,1,0:T(8,128)S(1)} %get-tuple-element.15), channel_id=1, source_target_pairs={{0,2},{1,3},{2,0},{3,1},{4,6},{5,7},{6,4},{7,5},{8,10},{9,11},{10,... | collective-permute-start | bytes 589832 | tf_op jit(solution)/shard_map/ppermute | solution.py:39
  28.1 0.0 collective-permute-done.2
  28.1 2.7 %collective-permute-start.3 = (f32[32,768]{1,0:T(8,128)S(1)}, f32[32,768]{1,0:T(8,128)S(1)}, u32[]{:S(2)}, u32[]{:S(2)}) collective-permute-start(f32[32,768]{1,0:T(8,128)S(1)} %bitcast.8), channel_id=1, source_target_pairs={{0,16},{2,18},{4,20},{6,22},{8,24},{10,26},{12,28},{14,30},{16,0},... | collective-permute-start | bytes 294920 | tf_op jit(solution)/shard_map/ppermute | solution.py:43
  30.8 1.5 %collective-permute-done.8 = f32[2,32,768]{2,1,0:T(8,128)S(1)} collective-permute-done((f32[2,32,768]{2,1,0:T(8,128)S(1)}, f32[2,32,768]{2,1,0:T(8,128)S(1)}, u32[]{:S(2)}, u32[]{:S(2)}) %collective-permute-start.8) | collective-permute-done | bytes 196640 | tf_op jit(solution)/shard_map/ppermute | solution.py:39
  32.3 2.1 %collective-permute-start.9 = (f32[1,32,768]{2,1,0:T(8,128)S(1)}, f32[1,32,768]{2,1,0:T(8,128)S(1)}, u32[]{:S(2)}, u32[]{:S(2)}) collective-permute-start(f32[1,32,768]{2,1,0:T(8,128)S(1)} %slice_add_fusion.4), channel_id=1, source_target_pairs={{0,4},{1,5},{2,6},{3,7},{4,0},{5,1},{6,2},{7,3},{8,12},{9,13},{10,... | collective-permute-start | bytes 294920 | tf_op jit(solution)/shard_map/ppermute | solution.py:39
  34.4 0.3 collective-permute-done.3
  34.8 0.7 collective-permute-start.4
  35.5 1.6 %collective-permute-done.9 = f32[1,32,768]{2,1,0:T(8,128)S(1)} collective-permute-done((f32[1,32,768]{2,1,0:T(8,128)S(1)}, f32[1,32,768]{2,1,0:T(8,128)S(1)}, u32[]{:S(2)}, u32[]{:S(2)}) %collective-permute-start.9) | collective-permute-done | bytes 98336 | tf_op jit(solution)/shard_map/ppermute | solution.py:39
  37.1 2.6 %collective-permute-start.10 = (f32[32,768]{1,0:T(8,128)S(1)}, f32[32,768]{1,0:T(8,128)S(1)}, u32[]{:S(2)}, u32[]{:S(2)}) collective-permute-start(f32[32,768]{1,0:T(8,128)S(1)} %fusion.1), channel_id=1, source_target_pairs={{0,16},{2,18},{4,20},{6,22},{8,24},{10,26},{12,28},{14,30},{16,0},... | collective-permute-start | bytes 294920 | tf_op jit(solution)/shard_map/ppermute | solution.py:43
  39.7 4.4 %collective-permute-done.4 = f32[1,2,32,768]{3,2,1,0:T(8,128)S(1)} collective-permute-done((f32[1,2,32,768]{3,2,1,0:T(8,128)S(1)}, f32[1,2,32,768]{3,2,1,0:T(8,128)S(1)}, u32[]{:S(2)}, u32[]{:S(2)}) %collective-permute-start.4) | collective-permute-done | bytes 196640 | tf_op jit(solution)/shard_map/ppermute | solution.py:39
  44.1 1.4 %collective-permute-start.5 = (f32[2,2,32,768]{3,2,1,0:T(8,128)S(1)}, f32[2,2,32,768]{3,2,1,0:T(8,128)S(1)}, u32[]{:S(2)}, u32[]{:S(2)}) collective-permute-start(f32[2,2,32,768]{3,2,1,0:T(8,128)S(1)} %pad_maximum_fusion.2), channel_id=1, source_target_pairs={{0,4},{1,9},{2,6},{3,11},{4,0},{5,13},{6,2},{7,15},{8,12},{9,1},{1... | collective-permute-start | bytes 1179656 | tf_op jit(solution)/shard_map/ppermute | solution.py:39
  45.4 0.0 collective-permute-done.10
  45.5 0.8 collective-permute-start.11
  46.3 10.9 %collective-permute-done.11 = f32[1,32,1024]{2,1,0:T(8,128)S(1)} collective-permute-done((f32[1,32,1024]{2,1,0:T(8,128)S(1)}, f32[1,32,1024]{2,1,0:T(8,128)S(1)}, u32[]{:S(2)}, u32[]{:S(2)}) %collective-permute-start.11) | collective-permute-done | bytes 131104 | tf_op jit(solution)/shard_map/ppermute | solution.py:39
  57.2 0.1 collective-permute-start.12
  57.3 0.0 collective-permute-done.5
  57.3 0.1 pad_maximum_fusion.first_ref
  57.3 2.1 %collective-permute-start.6 = (f32[4,2,32,768]{3,2,1,0:T(8,128)S(1)}, f32[4,2,32,768]{3,2,1,0:T(8,128)S(1)}, u32[]{:S(2)}, u32[]{:S(2)}) collective-permute-start(f32[4,2,32,768]{3,2,1,0:T(8,128)S(1)} %pad_maximum_fusion.first_ref), channel_id=1, source_target_pairs={{0,2},{1,5},{2,0},{3,7},{4,6},{5,1},{6,4},{7,3},{8,10},{9,13},{10,... | collective-permute-start | bytes 2359304 | tf_op jit(solution)/shard_map/ppermute | solution.py:39
  59.4 4.2 %collective-permute-done.12 = f32[2,32,1024]{2,1,0:T(8,128)S(1)} collective-permute-done((f32[2,32,1024]{2,1,0:T(8,128)S(1)}, f32[2,32,1024]{2,1,0:T(8,128)S(1)}, u32[]{:S(2)}, u32[]{:S(2)}) %collective-permute-start.12) | collective-permute-done | bytes 262176 | tf_op jit(solution)/shard_map/ppermute | solution.py:39
  63.7 0.1 collective-permute-start.13
  63.7 8.3 %collective-permute-done.6.second_ref = f32[4,2,32,768]{3,2,1,0:T(8,128)S(1)} collective-permute-done((f32[4,2,32,768]{3,2,1,0:T(8,128)S(1)}, f32[4,2,32,768]{3,2,1,0:T(8,128)S(1)}, u32[]{:S(2)}, u32[]{:S(2)}) %collective-permute-start.6) | collective-permute-done | bytes 786464 | tf_op jit(solution)/shard_map/ppermute | solution.py:39
  72.0 2.1 %shard_map.60.update_ref = f32[2,256,512]{2,1,0:T(8,128)S(1)} custom-call(f32[4,2,32,768]{3,2,1,0:T(8,128)S(1)} %pad_maximum_fusion.first_ref, f32[4,2,32,768]{3,2,1,0:T(8,128)S(1)} %collective-permute-done.6.second_ref), custom_call_target="tpu_custom_call" | custom-call | flops 1207959552 | bytes 2621440 | tf_op jit(solution)/shard_map/pallas_call | solution.py:130
  74.1 0.0 copy-start.3
  74.1 0.0 collective-permute-done.13.second_ref
  74.1 0.7 shard_map.63.mine_ref
  74.8 0.1 collective-permute-start.14
  74.9 0.3 copy-done.3
  75.2 1.4 %shard_map.61 = (f32[512,256]{1,0:T(8,128)}, f32[512,256]{1,0:T(8,128)S(1)}) custom-call(f32[512,256]{1,0:T(8,128)S(1)} %copy-done.3, f32[512,512]{1,0:T(8,128)S(1)} %copy-done.1, f32[2,256,512]{2,1,0:T(8,128)S(1)} %shard_map.60.update_ref), custom_call_target="tpu_custom_call" | custom-call | flops 402653184 | bytes 3670016 | tf_op jit(solution)/shard_map/pallas_call | solution.py:130
  76.5 0.2 collective-permute-done.14.other_ref
  76.8 1.0 %copy-done.4 = f32[512,256]{1,0:T(8,128)S(1)} copy-done((f32[512,256]{1,0:T(8,128)S(1)}, f32[512,256]{1,0:T(8,128)}, u32[]{:S(2)}) %copy-start.4) | copy-done | bytes 524312
  77.8 2.2 %shard_map.64 = f32[512,256]{1,0:T(8,128)} custom-call(f32[256,512]{1,0:T(8,128)S(1)} %shard_map.63.mine_ref, f32[256,512]{1,0:T(8,128)S(1)} %collective-permute-done.14.other_ref, f32[512,256]{1,0:T(8,128)S(1)} %copy-done.4, f32[512,256]{1,0:T(8,128)S(1)} %get-tuple-element.13.next_ref), custom_call_target="tpu_custom_call" | custom-call | flops 503316480 | bytes 2621440 | tf_op jit(solution)/shard_map/pallas_call | solution.py:130
  (17 shorter events, 0.3 us)
Async XLA Ops:
  0.6 1.2 %copy-start = (f32[512,512]{1,0:T(8,128)S(1)}, f32[512,512]{1,0:T(8,128)}, u32[]{:S(2)}) copy-start(f32[512,512]{1,0:T(8,128)} %z_ref.5) | copy-start | bytes 3145732
  1.9 1.0 %copy-start.2 = (f32[512,256]{1,0:T(8,128)S(1)}, f32[512,256]{1,0:T(8,128)}, u32[]{:S(2)}) copy-start(f32[512,256]{1,0:T(8,128)} %y_ref.5) | copy-start | bytes 1572868
  2.9 1.0 %copy-start.5 = (f32[512,256]{1,0:T(8,128)S(1)}, f32[512,256]{1,0:T(8,128)}, u32[]{:S(2)}) copy-start(f32[512,256]{1,0:T(8,128)} %basis_ref.2) | copy-start | bytes 1572868
  3.9 11.8 %copy-start.6 = (f32[512,256]{1,0:T(8,128)S(1)}, f32[512,256]{1,0:T(8,128)}, u32[]{:S(2)}) copy-start(f32[512,256]{1,0:T(8,128)} %basis_ref.3) | copy-start | bytes 1572868
  4.8 10.9 %copy-start.1 = (f32[512,512]{1,0:T(8,128)S(1)}, f32[512,512]{1,0:T(8,128)}, u32[]{:S(2)}) copy-start(f32[512,512]{1,0:T(8,128)} %z_ref.5) | copy-start | bytes 3145732
  4.9 8.8 %collective-permute-start = (f32[4,32,768]{2,1,0:T(8,128)S(1)}, f32[4,32,768]{2,1,0:T(8,128)S(1)}, u32[]{:S(2)}, u32[]{:S(2)}) collective-permute-start(f32[4,32,768]{2,1,0:T(8,128)S(1)} %get-tuple-element.9), channel_id=1, source_target_pairs={{0,2},{1,5},{2,0},{3,7},{4,6},{5,1},{6,4},{7,3},{8,10},{9,13},{10,... | collective-permute-start | bytes 1179656 | tf_op jit(solution)/shard_map/ppermute | solution.py:39
  13.7 5.8 %collective-permute-start.1 = (f32[2,32,768]{2,1,0:T(8,128)S(1)}, f32[2,32,768]{2,1,0:T(8,128)S(1)}, u32[]{:S(2)}, u32[]{:S(2)}) collective-permute-start(f32[2,32,768]{2,1,0:T(8,128)S(1)} %get-tuple-element.17), channel_id=1, source_target_pairs={{0,4},{1,9},{2,6},{3,11},{4,0},{5,13},{6,2},{7,15},{8,12},{9,1},{1... | collective-permute-start | bytes 589832 | tf_op jit(solution)/shard_map/ppermute | solution.py:39
  16.7 9.8 %collective-permute-start.7 = (f32[4,32,768]{2,1,0:T(8,128)S(1)}, f32[4,32,768]{2,1,0:T(8,128)S(1)}, u32[]{:S(2)}, u32[]{:S(2)}) collective-permute-start(f32[4,32,768]{2,1,0:T(8,128)S(1)} %get-tuple-element.12), channel_id=1, source_target_pairs={{0,8},{1,9},{2,10},{3,11},{4,12},{5,13},{6,14},{7,15},{8,0},{9,1},... | collective-permute-start | bytes 1179656 | tf_op jit(solution)/shard_map/ppermute | solution.py:39
  19.4 8.7 %collective-permute-start.2 = (f32[1,32,768]{2,1,0:T(8,128)S(1)}, f32[1,32,768]{2,1,0:T(8,128)S(1)}, u32[]{:S(2)}, u32[]{:S(2)}) collective-permute-start(f32[1,32,768]{2,1,0:T(8,128)S(1)} %slice_add_fusion.6), channel_id=1, source_target_pairs={{0,8},{1,3},{2,10},{3,1},{4,12},{5,7},{6,14},{7,5},{8,0},{9,11},{1... | collective-permute-start | bytes 294920 | tf_op jit(solution)/shard_map/ppermute | solution.py:39
  26.6 5.7 %collective-permute-start.8 = (f32[2,32,768]{2,1,0:T(8,128)S(1)}, f32[2,32,768]{2,1,0:T(8,128)S(1)}, u32[]{:S(2)}, u32[]{:S(2)}) collective-permute-start(f32[2,32,768]{2,1,0:T(8,128)S(1)} %get-tuple-element.15), channel_id=1, source_target_pairs={{0,2},{1,3},{2,0},{3,1},{4,6},{5,7},{6,4},{7,5},{8,10},{9,11},{10,... | collective-permute-start | bytes 589832 | tf_op jit(solution)/shard_map/ppermute | solution.py:39
  28.1 6.6 %collective-permute-start.3 = (f32[32,768]{1,0:T(8,128)S(1)}, f32[32,768]{1,0:T(8,128)S(1)}, u32[]{:S(2)}, u32[]{:S(2)}) collective-permute-start(f32[32,768]{1,0:T(8,128)S(1)} %bitcast.8), channel_id=1, source_target_pairs={{0,16},{2,18},{4,20},{6,22},{8,24},{10,26},{12,28},{14,30},{16,0},... | collective-permute-start | bytes 294920 | tf_op jit(solution)/shard_map/ppermute | solution.py:43
  32.3 4.7 %collective-permute-start.9 = (f32[1,32,768]{2,1,0:T(8,128)S(1)}, f32[1,32,768]{2,1,0:T(8,128)S(1)}, u32[]{:S(2)}, u32[]{:S(2)}) collective-permute-start(f32[1,32,768]{2,1,0:T(8,128)S(1)} %slice_add_fusion.4), channel_id=1, source_target_pairs={{0,4},{1,5},{2,6},{3,7},{4,0},{5,1},{6,2},{7,3},{8,12},{9,13},{10,... | collective-permute-start | bytes 294920 | tf_op jit(solution)/shard_map/ppermute | solution.py:39
  34.8 9.2 %collective-permute-start.4 = (f32[1,2,32,768]{3,2,1,0:T(8,128)S(1)}, f32[1,2,32,768]{3,2,1,0:T(8,128)S(1)}, u32[]{:S(2)}, u32[]{:S(2)}) collective-permute-start(f32[1,2,32,768]{3,2,1,0:T(8,128)S(1)} %maximum_bitcast_fusion), channel_id=1, source_target_pairs={{0,8},{1,3},{2,10},{3,1},{4,12},{5,7},{6,14},{7,5},{8,0},{9,11},{1... | collective-permute-start | bytes 589832 | tf_op jit(solution)/shard_map/ppermute | solution.py:39
  37.1 8.4 %collective-permute-start.10 = (f32[32,768]{1,0:T(8,128)S(1)}, f32[32,768]{1,0:T(8,128)S(1)}, u32[]{:S(2)}, u32[]{:S(2)}) collective-permute-start(f32[32,768]{1,0:T(8,128)S(1)} %fusion.1), channel_id=1, source_target_pairs={{0,16},{2,18},{4,20},{6,22},{8,24},{10,26},{12,28},{14,30},{16,0},... | collective-permute-start | bytes 294920 | tf_op jit(solution)/shard_map/ppermute | solution.py:43
  44.1 13.2 %collective-permute-start.5 = (f32[2,2,32,768]{3,2,1,0:T(8,128)S(1)}, f32[2,2,32,768]{3,2,1,0:T(8,128)S(1)}, u32[]{:S(2)}, u32[]{:S(2)}) collective-permute-start(f32[2,2,32,768]{3,2,1,0:T(8,128)S(1)} %pad_maximum_fusion.2), channel_id=1, source_target_pairs={{0,4},{1,9},{2,6},{3,11},{4,0},{5,13},{6,2},{7,15},{8,12},{9,1},{1... | collective-permute-start | bytes 1179656 | tf_op jit(solution)/shard_map/ppermute | solution.py:39
  45.5 11.7 %collective-permute-start.11 = (f32[1,32,1024]{2,1,0:T(8,128)S(1)}, f32[1,32,1024]{2,1,0:T(8,128)S(1)}, u32[]{:S(2)}, u32[]{:S(2)}) collective-permute-start(f32[1,32,1024]{2,1,0:T(8,128)S(1)} %maximum_bitcast_fusion.1), channel_id=1, source_target_pairs={{0,4},{1,5},{2,6},{3,7},{4,0},{5,1},{6,2},{7,3},{8,12},{9,13},{10,... | collective-permute-start | bytes 393224 | tf_op jit(solution)/shard_map/ppermute | solution.py:39
  57.2 6.4 %collective-permute-start.12 = (f32[2,32,1024]{2,1,0:T(8,128)S(1)}, f32[2,32,1024]{2,1,0:T(8,128)S(1)}, u32[]{:S(2)}, u32[]{:S(2)}) collective-permute-start(f32[2,32,1024]{2,1,0:T(8,128)S(1)} %pad_maximum_fusion.3), channel_id=1, source_target_pairs={{0,2},{1,3},{2,0},{3,1},{4,6},{5,7},{6,4},{7,5},{8,10},{9,11},{10,... | collective-permute-start | bytes 786440 | tf_op jit(solution)/shard_map/ppermute | solution.py:39
  57.3 14.7 %collective-permute-start.6 = (f32[4,2,32,768]{3,2,1,0:T(8,128)S(1)}, f32[4,2,32,768]{3,2,1,0:T(8,128)S(1)}, u32[]{:S(2)}, u32[]{:S(2)}) collective-permute-start(f32[4,2,32,768]{3,2,1,0:T(8,128)S(1)} %pad_maximum_fusion.first_ref), channel_id=1, source_target_pairs={{0,2},{1,5},{2,0},{3,7},{4,6},{5,1},{6,4},{7,3},{8,10},{9,13},{10,... | collective-permute-start | bytes 2359304 | tf_op jit(solution)/shard_map/ppermute | solution.py:39
  63.7 10.5 %collective-permute-start.13 = (f32[4,32,1024]{2,1,0:T(8,128)S(1)}, f32[4,32,1024]{2,1,0:T(8,128)S(1)}, u32[]{:S(2)}, u32[]{:S(2)}) collective-permute-start(f32[4,32,1024]{2,1,0:T(8,128)S(1)} %pad_maximum_fusion.1.first_ref), channel_id=1, source_target_pairs={{0,8},{1,9},{2,10},{3,11},{4,12},{5,13},{6,14},{7,15},{8,0},{9,1},... | collective-permute-start | bytes 1572872 | tf_op jit(solution)/shard_map/ppermute | solution.py:39
  74.1 1.0 %copy-start.3 = (f32[512,256]{1,0:T(8,128)S(1)}, f32[512,256]{1,0:T(8,128)}, u32[]{:S(2)}) copy-start(f32[512,256]{1,0:T(8,128)} %y_ref.5) | copy-start | bytes 1572868
  74.8 2.0 %collective-permute-start.14 = (f32[256,512]{1,0:T(8,128)S(1)}, f32[256,512]{1,0:T(8,128)S(1)}, u32[]{:S(2)}, u32[]{:S(2)}) collective-permute-start(f32[256,512]{1,0:T(8,128)S(1)} %shard_map.63.mine_ref), channel_id=1, source_target_pairs={{0,1},{1,0},{2,3},{3,2},{4,5},{5,4},{6,7},{7,6},{8,9},{9,8},{10,11... | collective-permute-start | bytes 1572872 | tf_op jit(solution)/shard_map/ppermute | solution.py:43
  76.8 1.0 %copy-start.4 = (f32[512,256]{1,0:T(8,128)S(1)}, f32[512,256]{1,0:T(8,128)}, u32[]{:S(2)}) copy-start(f32[512,256]{1,0:T(8,128)} %get-tuple-element.6.pair_ref) | copy-start | bytes 1572868

commit v4 on v3

--- a/solution.py
+++ b/solution.py
@@ -11,12 +11,14 @@
 
 
 def axis_order(chain, core, bits, stage):
+    pair, rest = [core, 1 - core], list(range(2, bits))
     if chain == "low":
-        first = core
-    else:
-        first = 2
-    order = [(first + t) % bits for t in range(bits)]
-    return order if stage == "scatter" else order[::-1]
+        if stage == "scatter":
+            return pair + rest
+        return (rest + [1, 0]) if core == 0 else ([0] + rest + [1])
+    if stage == "scatter":
+        return rest + pair
+    return [core] + rest + [1 - core]
 
 
 def relative_bits(order, r, first_is_high):
@@ -64,18 +66,46 @@
     return lax.bitwise_xor(own, jnp.where(core == 0, moves[0], moves[1]))
 
 
-def local_kernel(chain, bits, basis_ref, y_ref, z_ref, send_ref, keep_ref, sums):
-    rank = y_ref.shape[1]
+def local_kernel(bits, *refs):
+    inputs, outputs = refs[:4], refs[4:8]
+    loaded, (joined, sums), (in_sems,) = refs[8:12], refs[12:14], refs[14:]
+    depth, rank = inputs[0].shape
     blocks = 1 << bits
     rows = rank // blocks
+    parts = 2
+    part = depth // parts
+    copies = [
+        [
+            pltpu.make_async_copy(
+                source.at[pl.ds(p * part, part)], target.at[pl.ds(p * part, part)], in_sems.at[p, i]
+            )
+            for i, (source, target) in enumerate(zip(inputs, loaded))
+        ]
+        for p in range(parts)
+    ]
+    for group in copies:
+        for copy in group:
+            copy.start()
+    y, z, low_basis, high_basis = loaded
     dims = (((0,), (0,)), ((), ()))
-    basis = split(basis_ref[...])
-    sums[:, :rank] = dot3(basis, split(y_ref[...]), dims)
-    sums[:, rank:] = dot3(basis, split(z_ref[...]), dims)
-    for r in range(blocks):
-        start = pl.multiple_of(block_of(r, chain, bits, "scatter") * rows, rows)
-        target = send_ref if r >= blocks // 2 else keep_ref
-        target[r % (blocks // 2)] = sums[pl.ds(start, rows), :]
+    for p in range(parts):
+        span = pl.ds(p * part, part)
+        for copy in copies[p][:3]:
+            copy.wait()
+        for source, columns in ((y, pl.ds(0, rank)), (z, pl.ds(rank, 2 * rank))):
+            high, low = split(source[span, :])
+            joined[0, span, columns] = high
+            joined[1, span, columns] = low
+        term = dot3(split(low_basis[span, :]), (joined[0, span, :], joined[1, span, :]), dims)
+        sums[0] = term if p == 0 else sums[0] + term
+    for p in range(parts):
+        copies[p][3].wait()
+    sums[1] = dot3(split(high_basis[...]), (joined[0], joined[1]), dims)
+    for i, chain in enumerate(("low", "high")):
+        for r in range(blocks):
+            start = pl.multiple_of(block_of(r, chain, bits, "scatter") * rows, rows)
+            target = outputs[2 * i + (0 if r >= blocks // 2 else 1)]
+            target[r % (blocks // 2)] = sums[i, pl.ds(start, rows), :]
 
 
 def place(parts, chain, bits, target):
@@ -109,37 +139,43 @@
     total_ref[...] = total
 
 
-def middle_kernel(y_ref, z_ref, update_ref, pair_ref, next_ref):
+def middle_kernel(y_ref, z_ref, update_ref, pair_ref, halves_ref, next_ref):
     rank = y_ref.shape[1]
     middle = z_ref[...] - dot3(split(y_ref[...]), split(update_ref[0]))
-    pair_ref[...] = middle[:, :rank]
+    pair = middle[:, :rank]
+    pair_ref[...] = pair
+    halves_ref[0], halves_ref[1] = split(pair)
     next_ref[...] = middle[:, rank:]
 
 
-def final_kernel(mine_ref, other_ref, pair_ref, next_ref, out_ref):
+def final_kernel(mine_ref, other_ref, halves_ref, next_ref, out_ref):
     rank = mine_ref.shape[0]
     mine = split(mine_ref[:, :rank])
     other = split(other_ref[:, :rank])
     start = other_ref[:, rank:] - dot3(other, split(mine_ref[:, rank:]))
     update = start + dot3(other, split(dot3(mine, split(start))))
-    out_ref[...] = next_ref[...] - dot3(split(pair_ref[...]), split(update))
-
-
-def run(kernel, shapes, args, scratch=(), flops=0):
+    out_ref[...] = next_ref[...] - dot3((halves_ref[0], halves_ref[1]), split(update))
+
+
+def run(kernel, shapes, args, scratch=(), flops=0, space=pltpu.VMEM, limit=24 << 20):
     bytes_moved = sum(a.size * 4 for a in args) + sum(4 * s.size for s in shapes)
     return pl.pallas_call(
         kernel,
         out_shape=shapes,
-        in_specs=[pl.BlockSpec(memory_space=pltpu.VMEM)] * len(args),
+        in_specs=[pl.BlockSpec(memory_space=space)] * len(args),
         out_specs=[pl.BlockSpec(memory_space=pltpu.VMEM)] * len(shapes),
         scratch_shapes=list(scratch),
-        compiler_params=pltpu.CompilerParams(vmem_limit_bytes=24 * 1024 * 1024),
+        compiler_params=pltpu.CompilerParams(vmem_limit_bytes=limit),
         cost_estimate=pl.CostEstimate(flops=flops, bytes_accessed=bytes_moved, transcendentals=0),
     )(*args)
 
 
-def array(*shape):
-    return jax.ShapeDtypeStruct(shape, jnp.float32)
+def array(*shape, dtype=jnp.float32):
+    return jax.ShapeDtypeStruct(shape, dtype)
+
+
+def after(x, *others):
+    return lax.optimization_barrier((x, *others))[0]
 
 
 def body(low_solved, low_basis, upper_solved, upper_basis):
@@ -150,43 +186,54 @@
     rows = rank // blocks
     unit = 6 * rank * rank
 
-    def scatter_terms(chain, basis):
-        half = array(blocks // 2, rows, 3 * rank)
-        return run(
-            functools.partial(local_kernel, chain, bits),
-            [half, half],
-            [basis, low_solved, upper_solved],
-            [pltpu.VMEM((rank, 3 * rank), jnp.float32)],
-            flops=3 * unit * depth,
-        )
-
-    def scatter(chain, send, keep):
+    half = array(blocks // 2, rows, 3 * rank)
+    low_send, low_keep, high_send, high_keep = run(
+        functools.partial(local_kernel, bits),
+        [half] * 4,
+        [low_solved, upper_solved, low_basis, upper_basis],
+        [
+            pltpu.VMEM((depth, rank), jnp.float32),
+            pltpu.VMEM((depth, 2 * rank), jnp.float32),
+            pltpu.VMEM((depth, rank), jnp.float32),
+            pltpu.VMEM((depth, rank), jnp.float32),
+            pltpu.VMEM((2, depth, 3 * rank), jnp.bfloat16),
+            pltpu.VMEM((2, rank, 3 * rank), jnp.float32),
+            pltpu.SemaphoreType.DMA((2, 4)),
+        ],
+        flops=6 * unit * depth,
+        space=pltpu.HBM,
+        limit=(62 << 20) + (1 << 18),
+    )
+
+    def rounds(chain, send, keep):
         for t in range(bits):
-            got = step(send, chain, t, bits, "scatter")
-            if t == bits - 1:
-                return keep[0] + got[0]
+            got = yield send, functools.partial(step, chain=chain, t=t, bits=bits, stage="scatter")
             half = keep.shape[0] // 2
-            send = keep[half:] + got[half:]
-            keep = keep[:half] + got[:half]
-
-    def gather(chain, x):
+            if t < bits - 1:
+                send = keep[half:] + got[half:]
+                keep = keep[:half] + got[:half]
+        mine = keep[0] + got[0]
+        other = yield mine, functools.partial(flip, axis="leaf", bit=bits)
+        if chain == "low":
+            grown = jnp.stack([mine, other])[None]
+        else:
+            both = [mine[:, :rank], other[:, :rank], mine[:, rank:] + other[:, rank:]]
+            grown = jnp.concatenate(both, axis=1)[None]
         for t in range(bits):
-            got = step(x, chain, t, bits, "gather")
-            if t == bits - 1:
-                return x, got
-            x = jnp.concatenate([x, got], axis=0)
-
-    low_mine = scatter("low", *scatter_terms("low", low_basis))
-    low_other = flip(low_mine, "leaf", bits)
-    low_parts = gather("low", jnp.stack([low_mine, low_other])[None])
-
-    high_mine = scatter("high", *scatter_terms("high", upper_basis))
-    high_other = flip(high_mine, "leaf", bits)
-    joined = jnp.concatenate(
-        [high_mine[:, :rank], high_other[:, :rank], high_mine[:, rank:] + high_other[:, rank:]],
-        axis=1,
-    )
-    high_parts = gather("high", joined[None])
+            got = yield grown, functools.partial(step, chain=chain, t=t, bits=bits, stage="gather")
+            if t < bits - 1:
+                grown = jnp.concatenate([grown, got], axis=0)
+        yield (grown, got), None
+
+    low, high = rounds("low", low_send, low_keep), rounds("high", high_send, high_keep)
+    (low_out, low_move), (high_out, high_move) = next(low), next(high)
+    while low_move is not None:
+        low_got, high_got = low_move(low_out), high_move(high_out)
+        low_out, low_move = low.send(after(low_got, high_out))
+        if low_move is not None:
+            high_got = after(high_got, low_out)
+        high_out, high_move = high.send(high_got)
+    low_parts, high_parts = low_out, high_out
 
     (update,) = run(
         functools.partial(solve_kernel, bits),
@@ -203,16 +250,16 @@
         flops=4 * unit * rank,
     )
     sibling = flip(total, "group", 0)
-    pair_solved, next_terms = run(
+    pair_solved, halves, next_terms = run(
         middle_kernel,
-        [array(depth, rank), array(depth, rank)],
+        [array(depth, rank), array(2, depth, rank, dtype=jnp.bfloat16), array(depth, rank)],
         [low_solved, upper_solved, update],
         flops=2 * unit * depth,
     )
     (next_solved,) = run(
         final_kernel,
         [array(depth, rank)],
-        [total, sibling, pair_solved, next_terms],
+        [total, sibling, halves, next_terms],
         flops=3 * unit * rank + unit * depth,
     )
     return pair_solved, next_solved

time: 80.4 us -> 75 us (0.933)
  waiting for transfers between devices: 43.2 us -> 33.4 us
  local copies, waits for them, and re-layouts: 4.64 us -> 0.59 us
  starting transfers between devices: 23 us -> 26.8 us
  Pallas kernels: 8.09 us -> 11.6 us
  other arithmetic: 0.32 us -> 1.4 us
    ppermute x12, waiting for transfers between devices: 42.6 us -> 30.1 us  [step(): return lax.ppermute(x, AXES, pairs)]
    ppermute x12, starting transfers between devices: 17.6 us -> 21.7 us  [step(): return lax.ppermute(x, AXES, pairs)]
    unnamed x14 -> x6, local copies, waits for them, and re-layouts: 4.63 us -> 0.58 us
    pallas_call x6 -> x5, Pallas kernels: 8.09 us -> 11.6 us  [run(): pl.pallas_call(kernel, out_shape=shapes, in_specs=[pl.BlockSpec(memory_sp...]
    ppermute x3, waiting for transfers between devices: 0.58 us -> 3.37 us  [flip(): lax.ppermute(x, axis, [(i, i ^ 1 << bit) for i in range(lax.axis_size(axi...]
    add x7, other arithmetic: 0.16 us -> 1.24 us  [the longest x3 1.16 us: rounds(): send = keep[half:] + got[half:]]
  transfers between devices with their start and end apart: 15 -> 15, of which waited for: 11 -> 12; matrix products, arithmetic and copies ran while one was open for 0% -> 2% of each run, Pallas kernels for 5% -> 5%
where the time goes in v4:
time: 75 us; the launch traced here: 74.6 us
  waiting for transfers between devices  33.4 us (45%)
  starting transfers between devices  26.8 us (36%)
  Pallas kernels  11.6 us (15%)
  other arithmetic  1.4 us (2%)
  between operations  0.77 us (1%)
    ppermute x12, waiting for transfers between devices, step(): return lax.ppermute(x, AXES, pairs)  30.1 us
    ppermute x12, starting transfers between devices, step(): return lax.ppermute(x, AXES, pairs)  21.7 us
    pallas_call x5, Pallas kernels, run(): pl.pallas_call(kernel, out_shape=shapes, in_specs=[pl.BlockSpec(memory_sp...  11.6 us
    ppermute x3, starting transfers between devices, flip(): lax.ppermute(x, axis, [(i, i ^ 1 << bit) for i in range(lax.axis_size(axi...  5.08 us
    ppermute x3, waiting for transfers between devices, flip(): lax.ppermute(x, axis, [(i, i ^ 1 << bit) for i in range(lax.axis_size(axi...  3.37 us
  transfers between devices with their start and end apart: 15, of which 12 were waited for; matrix products, arithmetic and copies ran while one was open for 2% of the time, Pallas kernels for 5%

profile of v4, /device:TPU:0, one launch (start us, length us, event | category | flops | bytes accessed | tf_op | source)
XLA Modules:
  0.0 74.6 jit_solution(3358070544035938085)
XLA Ops:
  0.6 5.3 %shard_map.59 = (f32[4,32,768]{2,1,0:T(8,128)}, f32[4,32,768]{2,1,0:T(8,128)}, f32[4,32,768]{2,1,0:T(8,128)}, f32[4,32,768]{2,1,0:T(8,128)}) custom-call(f32[512,256]{1,0:T(8,128)} %y_ref.1, f32[512,512]{1,0:T(8,128)} %z_ref.1, f32[512,256]{1,0:T(8,128)} %refs_2_.1, f32[512,256]{1,0:T(8,128)} %refs_3_.1), custom_call_target="tpu_custom_call" | custom-call | flops 1207959552 | bytes 4194304 | tf_op jit(solution)/shard_map/pallas_call | solution.py:162
  5.9 3.0 %collective-permute-start = (f32[4,32,768]{2,1,0:T(8,128)}, f32[4,32,768]{2,1,0:T(8,128)S(1)}, u32[]{:S(2)}, u32[]{:S(2)}) collective-permute-start(f32[4,32,768]{2,1,0:T(8,128)} %get-tuple-element.23), channel_id=1, source_target_pairs={{0,2},{1,5},{2,0},{3,7},{4,6},{5,1},{6,4},{7,3},{8,10},{9,13},{10,... | collective-permute-start | bytes 1179656 | tf_op jit(solution)/shard_map/ppermute | solution.py:41
  8.9 1.6 %collective-permute-start.2 = (f32[4,32,768]{2,1,0:T(8,128)}, f32[4,32,768]{2,1,0:T(8,128)S(1)}, u32[]{:S(2)}, u32[]{:S(2)}) collective-permute-start(f32[4,32,768]{2,1,0:T(8,128)} %get-tuple-element.24), channel_id=1, source_target_pairs={{0,8},{1,9},{2,10},{3,11},{4,12},{5,13},{6,14},{7,15},{8,0},{9,1},... | collective-permute-start | bytes 1179656 | tf_op jit(solution)/shard_map/ppermute | solution.py:41
  10.5 4.4 %collective-permute-done = f32[4,32,768]{2,1,0:T(8,128)S(1)} collective-permute-done((f32[4,32,768]{2,1,0:T(8,128)}, f32[4,32,768]{2,1,0:T(8,128)S(1)}, u32[]{:S(2)}, u32[]{:S(2)}) %collective-permute-start) | collective-permute-done | bytes 393248 | tf_op jit(solution)/shard_map/ppermute | solution.py:41
  14.9 0.0 copy-start.2
  14.9 1.1 %slice_add_fusion.2 = (f32[2,32,768]{2,1,0:T(8,128)S(1)}, f32[2,32,768]{2,1,0:T(8,128)S(1)}) fusion(f32[4,32,768]{2,1,0:T(8,128)S(1)} %collective-permute-done, f32[4,32,768]{2,1,0:T(8,128)} %get-tuple-element.22), kind=kLoop, calls=%fused_computation.7 | loop fusion | flops 98304 | bytes 1179648 | tf_op jit(solution)/shard_map/add | solution.py:213
  16.0 2.1 %collective-permute-start.1 = (f32[2,32,768]{2,1,0:T(8,128)S(1)}, f32[2,32,768]{2,1,0:T(8,128)S(1)}, u32[]{:S(2)}, u32[]{:S(2)}) collective-permute-start(f32[2,32,768]{2,1,0:T(8,128)S(1)} %get-tuple-element.44), channel_id=1, source_target_pairs={{0,4},{1,3},{2,6},{3,1},{4,0},{5,7},{6,2},{7,5},{8,12},{9,11},{10,... | collective-permute-start | bytes 589832 | tf_op jit(solution)/shard_map/ppermute | solution.py:41
  18.1 1.6 %collective-permute-done.2 = f32[4,32,768]{2,1,0:T(8,128)S(1)} collective-permute-done((f32[4,32,768]{2,1,0:T(8,128)}, f32[4,32,768]{2,1,0:T(8,128)S(1)}, u32[]{:S(2)}, u32[]{:S(2)}) %collective-permute-start.2) | collective-permute-done | bytes 393248 | tf_op jit(solution)/shard_map/ppermute | solution.py:41
  19.7 0.0 copy-done.2
  19.8 1.5 %collective-permute-start.4 = (f32[2,32,768]{2,1,0:T(8,128)S(1)}, f32[2,32,768]{2,1,0:T(8,128)S(1)}, u32[]{:S(2)}, u32[]{:S(2)}) collective-permute-start(f32[2,32,768]{2,1,0:T(8,128)S(1)} %get-tuple-element.43), channel_id=1, source_target_pairs={{0,2},{1,5},{2,0},{3,7},{4,6},{5,1},{6,4},{7,3},{8,10},{9,13},{10,... | collective-permute-start | bytes 589832 | tf_op jit(solution)/shard_map/ppermute | solution.py:41
  21.3 1.8 %collective-permute-done.1 = f32[2,32,768]{2,1,0:T(8,128)S(1)} collective-permute-done((f32[2,32,768]{2,1,0:T(8,128)S(1)}, f32[2,32,768]{2,1,0:T(8,128)S(1)}, u32[]{:S(2)}, u32[]{:S(2)}) %collective-permute-start.1) | collective-permute-done | bytes 196640 | tf_op jit(solution)/shard_map/ppermute | solution.py:41
  23.1 2.0 %collective-permute-start.3 = (f32[1,32,768]{2,1,0:T(8,128)S(1)}, f32[1,32,768]{2,1,0:T(8,128)S(1)}, u32[]{:S(2)}, u32[]{:S(2)}) collective-permute-start(f32[1,32,768]{2,1,0:T(8,128)S(1)} %slice_add_fusion.6), channel_id=1, source_target_pairs={{0,8},{1,9},{2,10},{3,11},{4,12},{5,13},{6,14},{7,15},{8,0},{9,1},... | collective-permute-start | bytes 294920 | tf_op jit(solution)/shard_map/ppermute | solution.py:41
  25.1 0.4 collective-permute-done.4
  25.5 1.8 %collective-permute-start.6 = (f32[1,32,768]{2,1,0:T(8,128)S(1)}, f32[1,32,768]{2,1,0:T(8,128)S(1)}, u32[]{:S(2)}, u32[]{:S(2)}) collective-permute-start(f32[1,32,768]{2,1,0:T(8,128)S(1)} %slice_add_fusion.5), channel_id=1, source_target_pairs={{0,4},{1,3},{2,6},{3,1},{4,0},{5,7},{6,2},{7,5},{8,12},{9,11},{10,... | collective-permute-start | bytes 294920 | tf_op jit(solution)/shard_map/ppermute | solution.py:41
  27.3 0.5 collective-permute-done.3
  27.8 3.0 %collective-permute-start.5 = (f32[32,768]{1,0:T(8,128)S(1)}, f32[32,768]{1,0:T(8,128)S(1)}, u32[]{:S(2)}, u32[]{:S(2)}) collective-permute-start(f32[32,768]{1,0:T(8,128)S(1)} %bitcast.8), channel_id=1, source_target_pairs={{0,16},{2,18},{4,20},{6,22},{8,24},{10,26},{12,28},{14,30},{16,0},... | collective-permute-start | bytes 294920 | tf_op jit(solution)/shard_map/ppermute | solution.py:45
  30.8 0.0 collective-permute-done.6
  30.9 2.0 %collective-permute-start.8 = (f32[32,768]{1,0:T(8,128)S(1)}, f32[32,768]{1,0:T(8,128)S(1)}, u32[]{:S(2)}, u32[]{:S(2)}) collective-permute-start(f32[32,768]{1,0:T(8,128)S(1)} %fusion.1), channel_id=1, source_target_pairs={{0,16},{2,18},{4,20},{6,22},{8,24},{10,26},{12,28},{14,30},{16,0},... | collective-permute-start | bytes 294920 | tf_op jit(solution)/shard_map/ppermute | solution.py:45
  32.9 3.1 %collective-permute-done.5 = f32[32,768]{1,0:T(8,128)S(1)} collective-permute-done((f32[32,768]{1,0:T(8,128)S(1)}, f32[32,768]{1,0:T(8,128)S(1)}, u32[]{:S(2)}, u32[]{:S(2)}) %collective-permute-start.5) | collective-permute-done | bytes 98336 | tf_op jit(solution)/shard_map/ppermute | solution.py:45
  36.0 1.8 %collective-permute-start.7 = (f32[1,2,32,768]{3,2,1,0:T(8,128)S(1)}, f32[1,2,32,768]{3,2,1,0:T(8,128)S(1)}, u32[]{:S(2)}, u32[]{:S(2)}) collective-permute-start(f32[1,2,32,768]{3,2,1,0:T(8,128)S(1)} %maximum_bitcast_fusion), channel_id=1, source_target_pairs={{0,8},{1,3},{2,10},{3,1},{4,12},{5,7},{6,14},{7,5},{8,0},{9,11},{1... | collective-permute-start | bytes 589832 | tf_op jit(solution)/shard_map/ppermute | solution.py:41
  37.9 0.2 collective-permute-done.8
  38.2 5.6 %collective-permute-done.7 = f32[1,2,32,768]{3,2,1,0:T(8,128)S(1)} collective-permute-done((f32[1,2,32,768]{3,2,1,0:T(8,128)S(1)}, f32[1,2,32,768]{3,2,1,0:T(8,128)S(1)}, u32[]{:S(2)}, u32[]{:S(2)}) %collective-permute-start.7) | collective-permute-done | bytes 196640 | tf_op jit(solution)/shard_map/ppermute | solution.py:41
  43.8 1.8 %collective-permute-start.9 = (f32[2,2,32,768]{3,2,1,0:T(8,128)S(1)}, f32[2,2,32,768]{3,2,1,0:T(8,128)S(1)}, u32[]{:S(2)}, u32[]{:S(2)}) collective-permute-start(f32[2,2,32,768]{3,2,1,0:T(8,128)S(1)} %pad_maximum_fusion.2), channel_id=1, source_target_pairs={{0,4},{1,9},{2,6},{3,11},{4,0},{5,13},{6,2},{7,15},{8,12},{9,1},{1... | collective-permute-start | bytes 1179656 | tf_op jit(solution)/shard_map/ppermute | solution.py:41
  45.6 1.4 %collective-permute-start.10 = (f32[1,32,1024]{2,1,0:T(8,128)S(1)}, f32[1,32,1024]{2,1,0:T(8,128)S(1)}, u32[]{:S(2)}, u32[]{:S(2)}) collective-permute-start(f32[1,32,1024]{2,1,0:T(8,128)S(1)} %maximum_bitcast_fusion.1), channel_id=1, source_target_pairs={{0,2},{1,5},{2,0},{3,7},{4,6},{5,1},{6,4},{7,3},{8,10},{9,13},{10,... | collective-permute-start | bytes 393224 | tf_op jit(solution)/shard_map/ppermute | solution.py:41
  47.0 3.5 %collective-permute-done.10 = f32[1,32,1024]{2,1,0:T(8,128)S(1)} collective-permute-done((f32[1,32,1024]{2,1,0:T(8,128)S(1)}, f32[1,32,1024]{2,1,0:T(8,128)S(1)}, u32[]{:S(2)}, u32[]{:S(2)}) %collective-permute-start.10) | collective-permute-done | bytes 131104 | tf_op jit(solution)/shard_map/ppermute | solution.py:41
  50.6 1.6 %collective-permute-start.12 = (f32[2,32,1024]{2,1,0:T(8,128)S(1)}, f32[2,32,1024]{2,1,0:T(8,128)S(1)}, u32[]{:S(2)}, u32[]{:S(2)}) collective-permute-start(f32[2,32,1024]{2,1,0:T(8,128)S(1)} %pad_maximum_fusion.3), channel_id=1, source_target_pairs={{0,8},{1,9},{2,10},{3,11},{4,12},{5,13},{6,14},{7,15},{8,0},{9,1},... | collective-permute-start | bytes 786440 | tf_op jit(solution)/shard_map/ppermute | solution.py:41
  52.2 3.2 %collective-permute-done.9 = f32[2,2,32,768]{3,2,1,0:T(8,128)S(1)} collective-permute-done((f32[2,2,32,768]{3,2,1,0:T(8,128)S(1)}, f32[2,2,32,768]{3,2,1,0:T(8,128)S(1)}, u32[]{:S(2)}, u32[]{:S(2)}) %collective-permute-start.9) | collective-permute-done | bytes 393248 | tf_op jit(solution)/shard_map/ppermute | solution.py:41
  55.4 0.1 pad_maximum_fusion.first_ref
  55.5 1.0 %collective-permute-start.11 = (f32[4,2,32,768]{3,2,1,0:T(8,128)S(1)}, f32[4,2,32,768]{3,2,1,0:T(8,128)S(1)}, u32[]{:S(2)}, u32[]{:S(2)}) collective-permute-start(f32[4,2,32,768]{3,2,1,0:T(8,128)S(1)} %pad_maximum_fusion.first_ref), channel_id=1, source_target_pairs={{0,2},{1,5},{2,0},{3,7},{4,6},{5,1},{6,4},{7,3},{8,10},{9,13},{10,... | collective-permute-start | bytes 2359304 | tf_op jit(solution)/shard_map/ppermute | solution.py:41
  56.5 0.5 collective-permute-done.12
  57.1 2.0 %collective-permute-start.13 = (f32[4,32,1024]{2,1,0:T(8,128)S(1)}, f32[4,32,1024]{2,1,0:T(8,128)S(1)}, u32[]{:S(2)}, u32[]{:S(2)}) collective-permute-start(f32[4,32,1024]{2,1,0:T(8,128)S(1)} %pad_maximum_fusion.1.first_ref), channel_id=1, source_target_pairs={{0,4},{1,3},{2,6},{3,1},{4,0},{5,7},{6,2},{7,5},{8,12},{9,11},{10,... | collective-permute-start | bytes 1572872 | tf_op jit(solution)/shard_map/ppermute | solution.py:41
  59.1 8.4 %collective-permute-done.11.second_ref = f32[4,2,32,768]{3,2,1,0:T(8,128)S(1)} collective-permute-done((f32[4,2,32,768]{3,2,1,0:T(8,128)S(1)}, f32[4,2,32,768]{3,2,1,0:T(8,128)S(1)}, u32[]{:S(2)}, u32[]{:S(2)}) %collective-permute-start.11) | collective-permute-done | bytes 786464 | tf_op jit(solution)/shard_map/ppermute | solution.py:41
  67.5 2.1 %shard_map.60.update_ref = f32[2,256,512]{2,1,0:T(8,128)S(1)} custom-call(f32[4,2,32,768]{3,2,1,0:T(8,128)S(1)} %pad_maximum_fusion.first_ref, f32[4,2,32,768]{3,2,1,0:T(8,128)S(1)} %collective-permute-done.11.second_ref), custom_call_target="tpu_custom_call" | custom-call | flops 1207959552 | bytes 2621440 | tf_op jit(solution)/shard_map/pallas_call | solution.py:162
  69.6 0.0 copy-start
  69.6 0.0 copy-start.1
  69.6 0.0 collective-permute-done.13.second_ref
  69.7 0.7 shard_map.62.mine_ref
  70.3 0.1 collective-permute-start.14
  70.4 0.4 copy-done
  70.9 0.1 copy-done.1
  71.0 1.4 %shard_map.61 = (f32[512,256]{1,0:T(8,128)}, bf16[2,512,256]{2,1,0:T(8,128)(2,1)S(1)}, f32[512,256]{1,0:T(8,128)S(1)}) custom-call(f32[512,256]{1,0:T(8,128)S(1)} %copy-done.1, f32[512,512]{1,0:T(8,128)S(1)} %copy-done, f32[2,256,512]{2,1,0:T(8,128)S(1)} %shard_map.60.update_ref), custom_call_target="tpu_custom_call" | custom-call | flops 402653184 | bytes 4718592 | tf_op jit(solution)/shard_map/pallas_call | solution.py:162
  72.4 0.0 collective-permute-done.14.other_ref
  72.4 2.2 %shard_map.63 = f32[512,256]{1,0:T(8,128)} custom-call(f32[256,512]{1,0:T(8,128)S(1)} %shard_map.62.mine_ref, f32[256,512]{1,0:T(8,128)S(1)} %collective-permute-done.14.other_ref, bf16[2,512,256]{2,1,0:T(8,128)(2,1)S(1)} %get-tuple-element.40.halves_ref, f32[512,256]{1,0:T(8,128)S(1)} %get-tuple-element.41.next_ref), custom_call_target="tpu_custom_call" | custom-call | flops 503316480 | bytes 3145728 | tf_op jit(solution)/shard_map/pallas_call | solution.py:162
  (13 shorter events, 0.2 us)
Async XLA Ops:
  5.9 9.0 %collective-permute-start = (f32[4,32,768]{2,1,0:T(8,128)}, f32[4,32,768]{2,1,0:T(8,128)S(1)}, u32[]{:S(2)}, u32[]{:S(2)}) collective-permute-start(f32[4,32,768]{2,1,0:T(8,128)} %get-tuple-element.23), channel_id=1, source_target_pairs={{0,2},{1,5},{2,0},{3,7},{4,6},{5,1},{6,4},{7,3},{8,10},{9,13},{10,... | collective-permute-start | bytes 1179656 | tf_op jit(solution)/shard_map/ppermute | solution.py:41
  8.9 10.8 %collective-permute-start.2 = (f32[4,32,768]{2,1,0:T(8,128)}, f32[4,32,768]{2,1,0:T(8,128)S(1)}, u32[]{:S(2)}, u32[]{:S(2)}) collective-permute-start(f32[4,32,768]{2,1,0:T(8,128)} %get-tuple-element.24), channel_id=1, source_target_pairs={{0,8},{1,9},{2,10},{3,11},{4,12},{5,13},{6,14},{7,15},{8,0},{9,1},... | collective-permute-start | bytes 1179656 | tf_op jit(solution)/shard_map/ppermute | solution.py:41
  14.9 4.8 %copy-start.2 = (f32[4,32,768]{2,1,0:T(8,128)S(1)}, f32[4,32,768]{2,1,0:T(8,128)}, u32[]{:S(2)}) copy-start(f32[4,32,768]{2,1,0:T(8,128)} %get-tuple-element.26) | copy-start | bytes 1179652
  16.0 7.1 %collective-permute-start.1 = (f32[2,32,768]{2,1,0:T(8,128)S(1)}, f32[2,32,768]{2,1,0:T(8,128)S(1)}, u32[]{:S(2)}, u32[]{:S(2)}) collective-permute-start(f32[2,32,768]{2,1,0:T(8,128)S(1)} %get-tuple-element.44), channel_id=1, source_target_pairs={{0,4},{1,3},{2,6},{3,1},{4,0},{5,7},{6,2},{7,5},{8,12},{9,11},{10,... | collective-permute-start | bytes 589832 | tf_op jit(solution)/shard_map/ppermute | solution.py:41
  19.8 5.7 %collective-permute-start.4 = (f32[2,32,768]{2,1,0:T(8,128)S(1)}, f32[2,32,768]{2,1,0:T(8,128)S(1)}, u32[]{:S(2)}, u32[]{:S(2)}) collective-permute-start(f32[2,32,768]{2,1,0:T(8,128)S(1)} %get-tuple-element.43), channel_id=1, source_target_pairs={{0,2},{1,5},{2,0},{3,7},{4,6},{5,1},{6,4},{7,3},{8,10},{9,13},{10,... | collective-permute-start | bytes 589832 | tf_op jit(solution)/shard_map/ppermute | solution.py:41
  23.1 4.7 %collective-permute-start.3 = (f32[1,32,768]{2,1,0:T(8,128)S(1)}, f32[1,32,768]{2,1,0:T(8,128)S(1)}, u32[]{:S(2)}, u32[]{:S(2)}) collective-permute-start(f32[1,32,768]{2,1,0:T(8,128)S(1)} %slice_add_fusion.6), channel_id=1, source_target_pairs={{0,8},{1,9},{2,10},{3,11},{4,12},{5,13},{6,14},{7,15},{8,0},{9,1},... | collective-permute-start | bytes 294920 | tf_op jit(solution)/shard_map/ppermute | solution.py:41
  25.5 5.3 %collective-permute-start.6 = (f32[1,32,768]{2,1,0:T(8,128)S(1)}, f32[1,32,768]{2,1,0:T(8,128)S(1)}, u32[]{:S(2)}, u32[]{:S(2)}) collective-permute-start(f32[1,32,768]{2,1,0:T(8,128)S(1)} %slice_add_fusion.5), channel_id=1, source_target_pairs={{0,4},{1,3},{2,6},{3,1},{4,0},{5,7},{6,2},{7,5},{8,12},{9,11},{10,... | collective-permute-start | bytes 294920 | tf_op jit(solution)/shard_map/ppermute | solution.py:41
  27.8 8.2 %collective-permute-start.5 = (f32[32,768]{1,0:T(8,128)S(1)}, f32[32,768]{1,0:T(8,128)S(1)}, u32[]{:S(2)}, u32[]{:S(2)}) collective-permute-start(f32[32,768]{1,0:T(8,128)S(1)} %bitcast.8), channel_id=1, source_target_pairs={{0,16},{2,18},{4,20},{6,22},{8,24},{10,26},{12,28},{14,30},{16,0},... | collective-permute-start | bytes 294920 | tf_op jit(solution)/shard_map/ppermute | solution.py:45
  30.9 7.3 %collective-permute-start.8 = (f32[32,768]{1,0:T(8,128)S(1)}, f32[32,768]{1,0:T(8,128)S(1)}, u32[]{:S(2)}, u32[]{:S(2)}) collective-permute-start(f32[32,768]{1,0:T(8,128)S(1)} %fusion.1), channel_id=1, source_target_pairs={{0,16},{2,18},{4,20},{6,22},{8,24},{10,26},{12,28},{14,30},{16,0},... | collective-permute-start | bytes 294920 | tf_op jit(solution)/shard_map/ppermute | solution.py:45
  36.0 7.8 %collective-permute-start.7 = (f32[1,2,32,768]{3,2,1,0:T(8,128)S(1)}, f32[1,2,32,768]{3,2,1,0:T(8,128)S(1)}, u32[]{:S(2)}, u32[]{:S(2)}) collective-permute-start(f32[1,2,32,768]{3,2,1,0:T(8,128)S(1)} %maximum_bitcast_fusion), channel_id=1, source_target_pairs={{0,8},{1,3},{2,10},{3,1},{4,12},{5,7},{6,14},{7,5},{8,0},{9,11},{1... | collective-permute-start | bytes 589832 | tf_op jit(solution)/shard_map/ppermute | solution.py:41
  43.8 11.6 %collective-permute-start.9 = (f32[2,2,32,768]{3,2,1,0:T(8,128)S(1)}, f32[2,2,32,768]{3,2,1,0:T(8,128)S(1)}, u32[]{:S(2)}, u32[]{:S(2)}) collective-permute-start(f32[2,2,32,768]{3,2,1,0:T(8,128)S(1)} %pad_maximum_fusion.2), channel_id=1, source_target_pairs={{0,4},{1,9},{2,6},{3,11},{4,0},{5,13},{6,2},{7,15},{8,12},{9,1},{1... | collective-permute-start | bytes 1179656 | tf_op jit(solution)/shard_map/ppermute | solution.py:41
  45.6 5.0 %collective-permute-start.10 = (f32[1,32,1024]{2,1,0:T(8,128)S(1)}, f32[1,32,1024]{2,1,0:T(8,128)S(1)}, u32[]{:S(2)}, u32[]{:S(2)}) collective-permute-start(f32[1,32,1024]{2,1,0:T(8,128)S(1)} %maximum_bitcast_fusion.1), channel_id=1, source_target_pairs={{0,2},{1,5},{2,0},{3,7},{4,6},{5,1},{6,4},{7,3},{8,10},{9,13},{10,... | collective-permute-start | bytes 393224 | tf_op jit(solution)/shard_map/ppermute | solution.py:41
  50.6 6.4 %collective-permute-start.12 = (f32[2,32,1024]{2,1,0:T(8,128)S(1)}, f32[2,32,1024]{2,1,0:T(8,128)S(1)}, u32[]{:S(2)}, u32[]{:S(2)}) collective-permute-start(f32[2,32,1024]{2,1,0:T(8,128)S(1)} %pad_maximum_fusion.3), channel_id=1, source_target_pairs={{0,8},{1,9},{2,10},{3,11},{4,12},{5,13},{6,14},{7,15},{8,0},{9,1},... | collective-permute-start | bytes 786440 | tf_op jit(solution)/shard_map/ppermute | solution.py:41
  55.5 12.1 %collective-permute-start.11 = (f32[4,2,32,768]{3,2,1,0:T(8,128)S(1)}, f32[4,2,32,768]{3,2,1,0:T(8,128)S(1)}, u32[]{:S(2)}, u32[]{:S(2)}) collective-permute-start(f32[4,2,32,768]{3,2,1,0:T(8,128)S(1)} %pad_maximum_fusion.first_ref), channel_id=1, source_target_pairs={{0,2},{1,5},{2,0},{3,7},{4,6},{5,1},{6,4},{7,3},{8,10},{9,13},{10,... | collective-permute-start | bytes 2359304 | tf_op jit(solution)/shard_map/ppermute | solution.py:41
  57.1 12.6 %collective-permute-start.13 = (f32[4,32,1024]{2,1,0:T(8,128)S(1)}, f32[4,32,1024]{2,1,0:T(8,128)S(1)}, u32[]{:S(2)}, u32[]{:S(2)}) collective-permute-start(f32[4,32,1024]{2,1,0:T(8,128)S(1)} %pad_maximum_fusion.1.first_ref), channel_id=1, source_target_pairs={{0,4},{1,3},{2,6},{3,1},{4,0},{5,7},{6,2},{7,5},{8,12},{9,11},{10,... | collective-permute-start | bytes 1572872 | tf_op jit(solution)/shard_map/ppermute | solution.py:41
  69.6 1.2 %copy-start = (f32[512,512]{1,0:T(8,128)S(1)}, f32[512,512]{1,0:T(8,128)}, u32[]{:S(2)}) copy-start(f32[512,512]{1,0:T(8,128)} %z_ref.1) | copy-start | bytes 3145732
  69.6 1.3 %copy-start.1 = (f32[512,256]{1,0:T(8,128)S(1)}, f32[512,256]{1,0:T(8,128)}, u32[]{:S(2)}) copy-start(f32[512,256]{1,0:T(8,128)} %y_ref.1) | copy-start | bytes 1572868
  70.3 2.0 %collective-permute-start.14 = (f32[256,512]{1,0:T(8,128)S(1)}, f32[256,512]{1,0:T(8,128)S(1)}, u32[]{:S(2)}, u32[]{:S(2)}) collective-permute-start(f32[256,512]{1,0:T(8,128)S(1)} %shard_map.62.mine_ref), channel_id=1, source_target_pairs={{0,1},{1,0},{2,3},{3,2},{4,5},{5,4},{6,7},{7,6},{8,9},{9,8},{10,11... | collective-permute-start | bytes 1572872 | tf_op jit(solution)/shard_map/ppermute | solution.py:45

commit v5 on v4

--- a/solution.py
+++ b/solution.py
@@ -11,14 +11,11 @@
 
 
 def axis_order(chain, core, bits, stage):
+    if stage == "gather":
+        first = core if chain == "low" else 2
+        return [(first + t) % bits for t in range(bits)]
     pair, rest = [core, 1 - core], list(range(2, bits))
-    if chain == "low":
-        if stage == "scatter":
-            return pair + rest
-        return (rest + [1, 0]) if core == 0 else ([0] + rest + [1])
-    if stage == "scatter":
-        return rest + pair
-    return [core] + rest + [1 - core]
+    return pair + rest if chain == "low" else rest + pair
 
 
 def relative_bits(order, r, first_is_high):
@@ -110,33 +107,29 @@
 
 def place(parts, chain, bits, target):
     blocks = 1 << bits
-    rows = target.shape[-2] // blocks
+    rows = target.shape[0] // blocks
     for r in range(blocks):
         start = pl.multiple_of(block_of(r, chain, bits, "gather") * rows, rows)
-        piece = parts[r // (blocks // 2)][r % (blocks // 2)]
-        if len(target.shape) == 3:
-            target[:, pl.ds(start, rows), :] = piece
-        else:
-            target[pl.ds(start, rows), :] = piece
-
-
-def solve_kernel(bits, first_ref, second_ref, update_ref, terms):
+        target[pl.ds(start, rows), :] = parts[r // (blocks // 2)][r % (blocks // 2)]
+
+
+def solve_kernel(bits, first_ref, second_ref, update_ref, share_ref, terms):
     rank = update_ref.shape[1]
     place((first_ref, second_ref), "low", bits, terms)
-    couples = [split(terms[i, :, :rank]) for i in range(2)]
+    couples = [split(terms[:, 3 * i * rank : (3 * i + 1) * rank]) for i in range(2)]
+    sides = [terms[:, (3 * i + 1) * rank : (3 * i + 3) * rank] for i in range(2)]
     for i in range(2):
         mine, other = couples[i], couples[1 - i]
-        start = terms[1 - i, :, rank:] - dot3(other, split(terms[i, :, rank:]))
+        start = sides[1 - i] - dot3(other, split(sides[i]))
         update_ref[i] = start + dot3(other, split(dot3(mine, split(start))))
-
-
-def total_kernel(bits, first_ref, second_ref, update_ref, total_ref, terms):
+    share_ref[...] = dot3(split(terms[:, 6 * rank :]), split(update_ref[0]))
+
+
+def total_kernel(bits, first_ref, second_ref, update_ref, share_ref, total_ref, terms):
     rank = total_ref.shape[0]
     place((first_ref, second_ref), "high", bits, terms)
-    total = terms[:, 2 * rank :]
-    for i in range(2):
-        total = total - dot3(split(terms[:, i * rank : (i + 1) * rank]), split(update_ref[i]))
-    total_ref[...] = total
+    share = dot3(split(terms[:, :rank]), split(update_ref[1]))
+    total_ref[...] = terms[:, rank:] - share_ref[...] - share
 
 
 def middle_kernel(y_ref, z_ref, update_ref, pair_ref, halves_ref, next_ref):
@@ -205,6 +198,8 @@
         limit=(62 << 20) + (1 << 18),
     )
 
+    own = {}
+
     def rounds(chain, send, keep):
         for t in range(bits):
             got = yield send, functools.partial(step, chain=chain, t=t, bits=bits, stage="scatter")
@@ -213,12 +208,13 @@
                 send = keep[half:] + got[half:]
                 keep = keep[:half] + got[:half]
         mine = keep[0] + got[0]
+        own[chain] = mine
         other = yield mine, functools.partial(flip, axis="leaf", bit=bits)
         if chain == "low":
-            grown = jnp.stack([mine, other])[None]
+            both = [mine, other, own["high"][:, :rank]]
         else:
-            both = [mine[:, :rank], other[:, :rank], mine[:, rank:] + other[:, rank:]]
-            grown = jnp.concatenate(both, axis=1)[None]
+            both = [other[:, :rank], mine[:, rank:] + other[:, rank:]]
+        grown = jnp.concatenate(both, axis=1)[None]
         for t in range(bits):
             got = yield grown, functools.partial(step, chain=chain, t=t, bits=bits, stage="gather")
             if t < bits - 1:
@@ -235,19 +231,19 @@
         high_out, high_move = high.send(high_got)
     low_parts, high_parts = low_out, high_out
 
-    (update,) = run(
+    update, share = run(
         functools.partial(solve_kernel, bits),
-        [array(2, rank, 2 * rank)],
+        [array(2, rank, 2 * rank), array(rank, 2 * rank)],
         low_parts,
-        [pltpu.VMEM((2, rank, 3 * rank), jnp.float32)],
-        flops=12 * unit * rank,
+        [pltpu.VMEM((rank, 7 * rank), jnp.float32)],
+        flops=14 * unit * rank,
     )
     (total,) = run(
         functools.partial(total_kernel, bits),
         [array(rank, 2 * rank)],
-        [*high_parts, update],
-        [pltpu.VMEM((rank, 4 * rank), jnp.float32)],
-        flops=4 * unit * rank,
+        [*high_parts, update, share],
+        [pltpu.VMEM((rank, 3 * rank), jnp.float32)],
+        flops=2 * unit * rank,
     )
     sibling = flip(total, "group", 0)
     pair_solved, halves, next_terms = run(

time: 75 us -> 77.1 us (1.028)
  waiting for transfers between devices: 33.4 us -> 35.8 us
    ppermute x12, waiting for transfers between devices: 30.1 us -> 31.5 us  [step(): return lax.ppermute(x, AXES, pairs)]
    ppermute x3, starting transfers between devices: 5.08 us -> 6.27 us  [flip(): lax.ppermute(x, axis, [(i, i ^ 1 << bit) for i in range(lax.axis_size(axi...]
    add x1, other arithmetic: 0.04 us -> 1.13 us  [rounds(): keep = keep[:half] + got[:half]]
    add x3, other arithmetic: 1.16 us -> 0.07 us  [rounds(): send = keep[half:] + got[half:]]
    ppermute x3, waiting for transfers between devices: 3.37 us -> 4.32 us  [flip(): lax.ppermute(x, axis, [(i, i ^ 1 << bit) for i in range(lax.axis_size(axi...]
    ppermute x12, starting transfers between devices: 21.7 us -> 20.8 us  [step(): return lax.ppermute(x, AXES, pairs)]
  transfers between devices with their start and end apart: 15 -> 15, of which waited for: 12 -> 14; matrix products, arithmetic and copies ran while one was open for 2% -> 2% of each run, Pallas kernels for 5% -> 5%
where the time goes in v5:
time: 77.1 us; the launch traced here: 76.6 us
  waiting for transfers between devices  35.8 us (46%)
  starting transfers between devices  27 us (35%)
  Pallas kernels  11.6 us (15%)
  other arithmetic  1.4 us (2%)
    ppermute x12, waiting for transfers between devices, step(): return lax.ppermute(x, AXES, pairs)  31.5 us
    ppermute x12, starting transfers between devices, step(): return lax.ppermute(x, AXES, pairs)  20.8 us
    pallas_call x5, Pallas kernels, run(): pl.pallas_call(kernel, out_shape=shapes, in_specs=[pl.BlockSpec(memory_sp...  11.6 us
    ppermute x3, starting transfers between devices, flip(): lax.ppermute(x, axis, [(i, i ^ 1 << bit) for i in range(lax.axis_size(axi...  6.27 us
    ppermute x3, waiting for transfers between devices, flip(): lax.ppermute(x, axis, [(i, i ^ 1 << bit) for i in range(lax.axis_size(axi...  4.32 us
  transfers between devices with their start and end apart: 15, of which 14 were waited for; matrix products, arithmetic and copies ran while one was open for 2% of the time, Pallas kernels for 5%

profile of v5, /device:TPU:0, one launch (start us, length us, event | category | flops | bytes accessed | tf_op | source)
XLA Modules:
  0.0 76.6 jit_solution(12835687331241045863)
XLA Ops:
  0.6 5.3 %shard_map.59 = (f32[4,32,768]{2,1,0:T(8,128)}, f32[4,32,768]{2,1,0:T(8,128)}, f32[4,32,768]{2,1,0:T(8,128)}, f32[4,32,768]{2,1,0:T(8,128)}) custom-call(f32[512,256]{1,0:T(8,128)} %y_ref.1, f32[512,512]{1,0:T(8,128)} %z_ref.1, f32[512,256]{1,0:T(8,128)} %refs_2_.1, f32[512,256]{1,0:T(8,128)} %refs_3_.1), custom_call_target="tpu_custom_call" | custom-call | flops 1207959552 | bytes 4194304 | tf_op jit(solution)/shard_map/pallas_call | solution.py:155
  5.9 3.0 %collective-permute-start = (f32[4,32,768]{2,1,0:T(8,128)}, f32[4,32,768]{2,1,0:T(8,128)S(1)}, u32[]{:S(2)}, u32[]{:S(2)}) collective-permute-start(f32[4,32,768]{2,1,0:T(8,128)} %get-tuple-element.25), channel_id=1, source_target_pairs={{0,2},{1,5},{2,0},{3,7},{4,6},{5,1},{6,4},{7,3},{8,10},{9,13},{10,... | collective-permute-start | bytes 1179656 | tf_op jit(solution)/shard_map/ppermute | solution.py:38
  8.9 1.6 %collective-permute-start.2 = (f32[4,32,768]{2,1,0:T(8,128)}, f32[4,32,768]{2,1,0:T(8,128)S(1)}, u32[]{:S(2)}, u32[]{:S(2)}) collective-permute-start(f32[4,32,768]{2,1,0:T(8,128)} %get-tuple-element.26), channel_id=1, source_target_pairs={{0,8},{1,9},{2,10},{3,11},{4,12},{5,13},{6,14},{7,15},{8,0},{9,1},... | collective-permute-start | bytes 1179656 | tf_op jit(solution)/shard_map/ppermute | solution.py:38
  10.5 4.4 %collective-permute-done = f32[4,32,768]{2,1,0:T(8,128)S(1)} collective-permute-done((f32[4,32,768]{2,1,0:T(8,128)}, f32[4,32,768]{2,1,0:T(8,128)S(1)}, u32[]{:S(2)}, u32[]{:S(2)}) %collective-permute-start) | collective-permute-done | bytes 393248 | tf_op jit(solution)/shard_map/ppermute | solution.py:38
  14.9 0.0 copy-start.2
  14.9 1.1 %slice_add_fusion.3 = (f32[2,32,768]{2,1,0:T(8,128)S(1)}, f32[2,32,768]{2,1,0:T(8,128)S(1)}) fusion(f32[4,32,768]{2,1,0:T(8,128)S(1)} %collective-permute-done, f32[4,32,768]{2,1,0:T(8,128)} %get-tuple-element.24), kind=kLoop, calls=%fused_computation.8 | loop fusion | flops 98304 | bytes 1179648 | tf_op jit(solution)/shard_map/add | solution.py:209
  16.0 2.1 %collective-permute-start.1 = (f32[2,32,768]{2,1,0:T(8,128)S(1)}, f32[2,32,768]{2,1,0:T(8,128)S(1)}, u32[]{:S(2)}, u32[]{:S(2)}) collective-permute-start(f32[2,32,768]{2,1,0:T(8,128)S(1)} %get-tuple-element.47), channel_id=1, source_target_pairs={{0,4},{1,3},{2,6},{3,1},{4,0},{5,7},{6,2},{7,5},{8,12},{9,11},{10,... | collective-permute-start | bytes 589832 | tf_op jit(solution)/shard_map/ppermute | solution.py:38
  18.1 1.6 %collective-permute-done.2 = f32[4,32,768]{2,1,0:T(8,128)S(1)} collective-permute-done((f32[4,32,768]{2,1,0:T(8,128)}, f32[4,32,768]{2,1,0:T(8,128)S(1)}, u32[]{:S(2)}, u32[]{:S(2)}) %collective-permute-start.2) | collective-permute-done | bytes 393248 | tf_op jit(solution)/shard_map/ppermute | solution.py:38
  19.7 0.0 copy-done.2
  19.8 1.5 %collective-permute-start.4 = (f32[2,32,768]{2,1,0:T(8,128)S(1)}, f32[2,32,768]{2,1,0:T(8,128)S(1)}, u32[]{:S(2)}, u32[]{:S(2)}) collective-permute-start(f32[2,32,768]{2,1,0:T(8,128)S(1)} %get-tuple-element.48), channel_id=1, source_target_pairs={{0,2},{1,5},{2,0},{3,7},{4,6},{5,1},{6,4},{7,3},{8,10},{9,13},{10,... | collective-permute-start | bytes 589832 | tf_op jit(solution)/shard_map/ppermute | solution.py:38
  21.3 1.8 %collective-permute-done.1 = f32[2,32,768]{2,1,0:T(8,128)S(1)} collective-permute-done((f32[2,32,768]{2,1,0:T(8,128)S(1)}, f32[2,32,768]{2,1,0:T(8,128)S(1)}, u32[]{:S(2)}, u32[]{:S(2)}) %collective-permute-start.1) | collective-permute-done | bytes 196640 | tf_op jit(solution)/shard_map/ppermute | solution.py:38
  23.1 2.0 %collective-permute-start.3 = (f32[1,32,768]{2,1,0:T(8,128)S(1)}, f32[1,32,768]{2,1,0:T(8,128)S(1)}, u32[]{:S(2)}, u32[]{:S(2)}) collective-permute-start(f32[1,32,768]{2,1,0:T(8,128)S(1)} %slice_add_fusion.6), channel_id=1, source_target_pairs={{0,8},{1,9},{2,10},{3,11},{4,12},{5,13},{6,14},{7,15},{8,0},{9,1},... | collective-permute-start | bytes 294920 | tf_op jit(solution)/shard_map/ppermute | solution.py:38
  25.1 0.4 collective-permute-done.4
  25.5 1.8 %collective-permute-start.6 = (f32[1,32,768]{2,1,0:T(8,128)S(1)}, f32[1,32,768]{2,1,0:T(8,128)S(1)}, u32[]{:S(2)}, u32[]{:S(2)}) collective-permute-start(f32[1,32,768]{2,1,0:T(8,128)S(1)} %slice_add_fusion.5), channel_id=1, source_target_pairs={{0,4},{1,3},{2,6},{3,1},{4,0},{5,7},{6,2},{7,5},{8,12},{9,11},{10,... | collective-permute-start | bytes 294920 | tf_op jit(solution)/shard_map/ppermute | solution.py:38
  27.4 0.5 collective-permute-done.3
  27.8 3.0 %collective-permute-start.5 = (f32[32,768]{1,0:T(8,128)S(1)}, f32[32,768]{1,0:T(8,128)S(1)}, u32[]{:S(2)}, u32[]{:S(2)}) collective-permute-start(f32[32,768]{1,0:T(8,128)S(1)} %fusion.3), channel_id=1, source_target_pairs={{0,16},{2,18},{4,20},{6,22},{8,24},{10,26},{12,28},{14,30},{16,0},... | collective-permute-start | bytes 294920 | tf_op jit(solution)/shard_map/ppermute | solution.py:42
  30.8 0.0 collective-permute-done.6
  30.9 2.0 %collective-permute-start.8 = (f32[32,768]{1,0:T(8,128)S(1)}, f32[32,768]{1,0:T(8,128)S(1)}, u32[]{:S(2)}, u32[]{:S(2)}) collective-permute-start(f32[32,768]{1,0:T(8,128)S(1)} %fusion.1), channel_id=1, source_target_pairs={{0,16},{2,18},{4,20},{6,22},{8,24},{10,26},{12,28},{14,30},{16,0},... | collective-permute-start | bytes 294920 | tf_op jit(solution)/shard_map/ppermute | solution.py:42
  32.9 3.1 %collective-permute-done.5 = f32[32,768]{1,0:T(8,128)S(1)} collective-permute-done((f32[32,768]{1,0:T(8,128)S(1)}, f32[32,768]{1,0:T(8,128)S(1)}, u32[]{:S(2)}, u32[]{:S(2)}) %collective-permute-start.5) | collective-permute-done | bytes 98336 | tf_op jit(solution)/shard_map/ppermute | solution.py:42
  36.0 1.0 %collective-permute-start.7 = (f32[1,32,1792]{2,1,0:T(8,128)S(1)}, f32[1,32,1792]{2,1,0:T(8,128)S(1)}, u32[]{:S(2)}, u32[]{:S(2)}) collective-permute-start(f32[1,32,1792]{2,1,0:T(8,128)S(1)} %maximum_bitcast_fusion), channel_id=1, source_target_pairs={{0,2},{1,5},{2,0},{3,7},{4,6},{5,1},{6,4},{7,3},{8,10},{9,13},{10,... | collective-permute-start | bytes 688136 | tf_op jit(solution)/shard_map/ppermute | solution.py:38
  37.1 1.1 %collective-permute-done.8 = f32[32,768]{1,0:T(8,128)S(1)} collective-permute-done((f32[32,768]{1,0:T(8,128)S(1)}, f32[32,768]{1,0:T(8,128)S(1)}, u32[]{:S(2)}, u32[]{:S(2)}) %collective-permute-start.8) | collective-permute-done | bytes 98336 | tf_op jit(solution)/shard_map/ppermute | solution.py:42
  38.2 4.0 %collective-permute-done.7 = f32[1,32,1792]{2,1,0:T(8,128)S(1)} collective-permute-done((f32[1,32,1792]{2,1,0:T(8,128)S(1)}, f32[1,32,1792]{2,1,0:T(8,128)S(1)}, u32[]{:S(2)}, u32[]{:S(2)}) %collective-permute-start.7) | collective-permute-done | bytes 229408 | tf_op jit(solution)/shard_map/ppermute | solution.py:38
  42.2 1.6 %collective-permute-start.9 = (f32[2,32,1792]{2,1,0:T(8,128)S(1)}, f32[2,32,1792]{2,1,0:T(8,128)S(1)}, u32[]{:S(2)}, u32[]{:S(2)}) collective-permute-start(f32[2,32,1792]{2,1,0:T(8,128)S(1)} %pad_maximum_fusion.1), channel_id=1, source_target_pairs={{0,4},{1,9},{2,6},{3,11},{4,0},{5,13},{6,2},{7,15},{8,12},{9,1},{1... | collective-permute-start | bytes 1376264 | tf_op jit(solution)/shard_map/ppermute | solution.py:38
  43.8 1.5 %collective-permute-start.10 = (f32[1,32,768]{2,1,0:T(8,128)S(1)}, f32[1,32,768]{2,1,0:T(8,128)S(1)}, u32[]{:S(2)}, u32[]{:S(2)}) collective-permute-start(f32[1,32,768]{2,1,0:T(8,128)S(1)} %maximum_bitcast_fusion.1), channel_id=1, source_target_pairs={{0,8},{1,9},{2,10},{3,11},{4,12},{5,13},{6,14},{7,15},{8,0},{9,1},... | collective-permute-start | bytes 294920 | tf_op jit(solution)/shard_map/ppermute | solution.py:38
  45.4 3.1 %collective-permute-done.10 = f32[1,32,768]{2,1,0:T(8,128)S(1)} collective-permute-done((f32[1,32,768]{2,1,0:T(8,128)S(1)}, f32[1,32,768]{2,1,0:T(8,128)S(1)}, u32[]{:S(2)}, u32[]{:S(2)}) %collective-permute-start.10) | collective-permute-done | bytes 98336 | tf_op jit(solution)/shard_map/ppermute | solution.py:38
  48.4 2.3 %collective-permute-done.9 = f32[2,32,1792]{2,1,0:T(8,128)S(1)} collective-permute-done((f32[2,32,1792]{2,1,0:T(8,128)S(1)}, f32[2,32,1792]{2,1,0:T(8,128)S(1)}, u32[]{:S(2)}, u32[]{:S(2)}) %collective-permute-start.9) | collective-permute-done | bytes 458784 | tf_op jit(solution)/shard_map/ppermute | solution.py:38
  50.7 0.1 pad_maximum_fusion.first_ref
  50.8 1.8 %collective-permute-start.11 = (f32[4,32,1792]{2,1,0:T(8,128)S(1)}, f32[4,32,1792]{2,1,0:T(8,128)S(1)}, u32[]{:S(2)}, u32[]{:S(2)}) collective-permute-start(f32[4,32,1792]{2,1,0:T(8,128)S(1)} %pad_maximum_fusion.first_ref), channel_id=1, source_target_pairs={{0,8},{1,3},{2,10},{3,1},{4,12},{5,7},{6,14},{7,5},{8,0},{9,11},{1... | collective-permute-start | bytes 2752520 | tf_op jit(solution)/shard_map/ppermute | solution.py:38
  52.6 1.3 %collective-permute-start.12 = (f32[2,32,768]{2,1,0:T(8,128)S(1)}, f32[2,32,768]{2,1,0:T(8,128)S(1)}, u32[]{:S(2)}, u32[]{:S(2)}) collective-permute-start(f32[2,32,768]{2,1,0:T(8,128)S(1)} %pad_maximum_fusion.3), channel_id=1, source_target_pairs={{0,2},{1,3},{2,0},{3,1},{4,6},{5,7},{6,4},{7,5},{8,10},{9,11},{10,... | collective-permute-start | bytes 589832 | tf_op jit(solution)/shard_map/ppermute | solution.py:38
  53.9 6.5 %collective-permute-done.12 = f32[2,32,768]{2,1,0:T(8,128)S(1)} collective-permute-done((f32[2,32,768]{2,1,0:T(8,128)S(1)}, f32[2,32,768]{2,1,0:T(8,128)S(1)}, u32[]{:S(2)}, u32[]{:S(2)}) %collective-permute-start.12) | collective-permute-done | bytes 196640 | tf_op jit(solution)/shard_map/ppermute | solution.py:38
  60.5 1.4 %collective-permute-start.13 = (f32[4,32,768]{2,1,0:T(8,128)S(1)}, f32[4,32,768]{2,1,0:T(8,128)S(1)}, u32[]{:S(2)}, u32[]{:S(2)}) collective-permute-start(f32[4,32,768]{2,1,0:T(8,128)S(1)} %pad_maximum_fusion.2.first_ref), channel_id=1, source_target_pairs={{0,4},{1,5},{2,6},{3,7},{4,0},{5,1},{6,2},{7,3},{8,12},{9,13},{10,... | collective-permute-start | bytes 1179656 | tf_op jit(solution)/shard_map/ppermute | solution.py:38
  61.9 2.3 %collective-permute-done.11.second_ref = f32[4,32,1792]{2,1,0:T(8,128)S(1)} collective-permute-done((f32[4,32,1792]{2,1,0:T(8,128)S(1)}, f32[4,32,1792]{2,1,0:T(8,128)S(1)}, u32[]{:S(2)}, u32[]{:S(2)}) %collective-permute-start.11) | collective-permute-done | bytes 917536 | tf_op jit(solution)/shard_map/ppermute | solution.py:38
  64.2 2.3 %shard_map.60 = (f32[2,256,512]{2,1,0:T(8,128)S(1)}, f32[256,512]{1,0:T(8,128)S(1)}) custom-call(f32[4,32,1792]{2,1,0:T(8,128)S(1)} %pad_maximum_fusion.first_ref, f32[4,32,1792]{2,1,0:T(8,128)S(1)} %collective-permute-done.11.second_ref), custom_call_target="tpu_custom_call" | custom-call | flops 1409286144 | bytes 3407872 | tf_op jit(solution)/shard_map/pallas_call | solution.py:155
  66.6 4.6 %collective-permute-done.13.second_ref = f32[4,32,768]{2,1,0:T(8,128)S(1)} collective-permute-done((f32[4,32,768]{2,1,0:T(8,128)S(1)}, f32[4,32,768]{2,1,0:T(8,128)S(1)}, u32[]{:S(2)}, u32[]{:S(2)}) %collective-permute-start.13) | collective-permute-done | bytes 393248 | tf_op jit(solution)/shard_map/ppermute | solution.py:38
  71.2 0.0 copy-start
  71.2 0.0 copy-start.1
  71.2 0.4 shard_map.62.mine_ref
  71.6 1.3 %collective-permute-start.14 = (f32[256,512]{1,0:T(8,128)S(1)}, f32[256,512]{1,0:T(8,128)S(1)}, u32[]{:S(2)}, u32[]{:S(2)}) collective-permute-start(f32[256,512]{1,0:T(8,128)S(1)} %shard_map.62.mine_ref), channel_id=1, source_target_pairs={{0,1},{1,0},{2,3},{3,2},{4,5},{5,4},{6,7},{7,6},{8,9},{9,8},{10,11... | collective-permute-start | bytes 1572872 | tf_op jit(solution)/shard_map/ppermute | solution.py:42
  72.9 0.0 copy-done
  72.9 0.0 copy-done.1
  72.9 1.4 %shard_map.61 = (f32[512,256]{1,0:T(8,128)}, bf16[2,512,256]{2,1,0:T(8,128)(2,1)S(1)}, f32[512,256]{1,0:T(8,128)S(1)}) custom-call(f32[512,256]{1,0:T(8,128)S(1)} %copy-done.1, f32[512,512]{1,0:T(8,128)S(1)} %copy-done, f32[2,256,512]{2,1,0:T(8,128)S(1)} %get-tuple-element.41.update_ref), custom_call_target="tpu_custom_call" | custom-call | flops 402653184 | bytes 4718592 | tf_op jit(solution)/shard_map/pallas_call | solution.py:155
  74.3 0.1 collective-permute-done.14.other_ref
  74.4 2.2 %shard_map.63 = f32[512,256]{1,0:T(8,128)} custom-call(f32[256,512]{1,0:T(8,128)S(1)} %shard_map.62.mine_ref, f32[256,512]{1,0:T(8,128)S(1)} %collective-permute-done.14.other_ref, bf16[2,512,256]{2,1,0:T(8,128)(2,1)S(1)} %get-tuple-element.44.halves_ref, f32[512,256]{1,0:T(8,128)S(1)} %get-tuple-element.45.next_ref), custom_call_target="tpu_custom_call" | custom-call | flops 503316480 | bytes 3145728 | tf_op jit(solution)/shard_map/pallas_call | solution.py:155
  (13 shorter events, 0.2 us)
Async XLA Ops:
  5.9 9.0 %collective-permute-start = (f32[4,32,768]{2,1,0:T(8,128)}, f32[4,32,768]{2,1,0:T(8,128)S(1)}, u32[]{:S(2)}, u32[]{:S(2)}) collective-permute-start(f32[4,32,768]{2,1,0:T(8,128)} %get-tuple-element.25), channel_id=1, source_target_pairs={{0,2},{1,5},{2,0},{3,7},{4,6},{5,1},{6,4},{7,3},{8,10},{9,13},{10,... | collective-permute-start | bytes 1179656 | tf_op jit(solution)/shard_map/ppermute | solution.py:38
  8.9 10.8 %collective-permute-start.2 = (f32[4,32,768]{2,1,0:T(8,128)}, f32[4,32,768]{2,1,0:T(8,128)S(1)}, u32[]{:S(2)}, u32[]{:S(2)}) collective-permute-start(f32[4,32,768]{2,1,0:T(8,128)} %get-tuple-element.26), channel_id=1, source_target_pairs={{0,8},{1,9},{2,10},{3,11},{4,12},{5,13},{6,14},{7,15},{8,0},{9,1},... | collective-permute-start | bytes 1179656 | tf_op jit(solution)/shard_map/ppermute | solution.py:38
  14.9 4.8 %copy-start.2 = (f32[4,32,768]{2,1,0:T(8,128)S(1)}, f32[4,32,768]{2,1,0:T(8,128)}, u32[]{:S(2)}) copy-start(f32[4,32,768]{2,1,0:T(8,128)} %get-tuple-element.28) | copy-start | bytes 1179652
  16.0 7.1 %collective-permute-start.1 = (f32[2,32,768]{2,1,0:T(8,128)S(1)}, f32[2,32,768]{2,1,0:T(8,128)S(1)}, u32[]{:S(2)}, u32[]{:S(2)}) collective-permute-start(f32[2,32,768]{2,1,0:T(8,128)S(1)} %get-tuple-element.47), channel_id=1, source_target_pairs={{0,4},{1,3},{2,6},{3,1},{4,0},{5,7},{6,2},{7,5},{8,12},{9,11},{10,... | collective-permute-start | bytes 589832 | tf_op jit(solution)/shard_map/ppermute | solution.py:38
  19.8 5.7 %collective-permute-start.4 = (f32[2,32,768]{2,1,0:T(8,128)S(1)}, f32[2,32,768]{2,1,0:T(8,128)S(1)}, u32[]{:S(2)}, u32[]{:S(2)}) collective-permute-start(f32[2,32,768]{2,1,0:T(8,128)S(1)} %get-tuple-element.48), channel_id=1, source_target_pairs={{0,2},{1,5},{2,0},{3,7},{4,6},{5,1},{6,4},{7,3},{8,10},{9,13},{10,... | collective-permute-start | bytes 589832 | tf_op jit(solution)/shard_map/ppermute | solution.py:38
  23.1 4.7 %collective-permute-start.3 = (f32[1,32,768]{2,1,0:T(8,128)S(1)}, f32[1,32,768]{2,1,0:T(8,128)S(1)}, u32[]{:S(2)}, u32[]{:S(2)}) collective-permute-start(f32[1,32,768]{2,1,0:T(8,128)S(1)} %slice_add_fusion.6), channel_id=1, source_target_pairs={{0,8},{1,9},{2,10},{3,11},{4,12},{5,13},{6,14},{7,15},{8,0},{9,1},... | collective-permute-start | bytes 294920 | tf_op jit(solution)/shard_map/ppermute | solution.py:38
  25.5 5.3 %collective-permute-start.6 = (f32[1,32,768]{2,1,0:T(8,128)S(1)}, f32[1,32,768]{2,1,0:T(8,128)S(1)}, u32[]{:S(2)}, u32[]{:S(2)}) collective-permute-start(f32[1,32,768]{2,1,0:T(8,128)S(1)} %slice_add_fusion.5), channel_id=1, source_target_pairs={{0,4},{1,3},{2,6},{3,1},{4,0},{5,7},{6,2},{7,5},{8,12},{9,11},{10,... | collective-permute-start | bytes 294920 | tf_op jit(solution)/shard_map/ppermute | solution.py:38
  27.8 8.2 %collective-permute-start.5 = (f32[32,768]{1,0:T(8,128)S(1)}, f32[32,768]{1,0:T(8,128)S(1)}, u32[]{:S(2)}, u32[]{:S(2)}) collective-permute-start(f32[32,768]{1,0:T(8,128)S(1)} %fusion.3), channel_id=1, source_target_pairs={{0,16},{2,18},{4,20},{6,22},{8,24},{10,26},{12,28},{14,30},{16,0},... | collective-permute-start | bytes 294920 | tf_op jit(solution)/shard_map/ppermute | solution.py:42
  30.9 7.3 %collective-permute-start.8 = (f32[32,768]{1,0:T(8,128)S(1)}, f32[32,768]{1,0:T(8,128)S(1)}, u32[]{:S(2)}, u32[]{:S(2)}) collective-permute-start(f32[32,768]{1,0:T(8,128)S(1)} %fusion.1), channel_id=1, source_target_pairs={{0,16},{2,18},{4,20},{6,22},{8,24},{10,26},{12,28},{14,30},{16,0},... | collective-permute-start | bytes 294920 | tf_op jit(solution)/shard_map/ppermute | solution.py:42
  36.0 6.1 %collective-permute-start.7 = (f32[1,32,1792]{2,1,0:T(8,128)S(1)}, f32[1,32,1792]{2,1,0:T(8,128)S(1)}, u32[]{:S(2)}, u32[]{:S(2)}) collective-permute-start(f32[1,32,1792]{2,1,0:T(8,128)S(1)} %maximum_bitcast_fusion), channel_id=1, source_target_pairs={{0,2},{1,5},{2,0},{3,7},{4,6},{5,1},{6,4},{7,3},{8,10},{9,13},{10,... | collective-permute-start | bytes 688136 | tf_op jit(solution)/shard_map/ppermute | solution.py:38
  42.2 8.5 %collective-permute-start.9 = (f32[2,32,1792]{2,1,0:T(8,128)S(1)}, f32[2,32,1792]{2,1,0:T(8,128)S(1)}, u32[]{:S(2)}, u32[]{:S(2)}) collective-permute-start(f32[2,32,1792]{2,1,0:T(8,128)S(1)} %pad_maximum_fusion.1), channel_id=1, source_target_pairs={{0,4},{1,9},{2,6},{3,11},{4,0},{5,13},{6,2},{7,15},{8,12},{9,1},{1... | collective-permute-start | bytes 1376264 | tf_op jit(solution)/shard_map/ppermute | solution.py:38
  43.8 4.6 %collective-permute-start.10 = (f32[1,32,768]{2,1,0:T(8,128)S(1)}, f32[1,32,768]{2,1,0:T(8,128)S(1)}, u32[]{:S(2)}, u32[]{:S(2)}) collective-permute-start(f32[1,32,768]{2,1,0:T(8,128)S(1)} %maximum_bitcast_fusion.1), channel_id=1, source_target_pairs={{0,8},{1,9},{2,10},{3,11},{4,12},{5,13},{6,14},{7,15},{8,0},{9,1},... | collective-permute-start | bytes 294920 | tf_op jit(solution)/shard_map/ppermute | solution.py:38
  50.8 13.5 %collective-permute-start.11 = (f32[4,32,1792]{2,1,0:T(8,128)S(1)}, f32[4,32,1792]{2,1,0:T(8,128)S(1)}, u32[]{:S(2)}, u32[]{:S(2)}) collective-permute-start(f32[4,32,1792]{2,1,0:T(8,128)S(1)} %pad_maximum_fusion.first_ref), channel_id=1, source_target_pairs={{0,8},{1,3},{2,10},{3,1},{4,12},{5,7},{6,14},{7,5},{8,0},{9,11},{1... | collective-permute-start | bytes 2752520 | tf_op jit(solution)/shard_map/ppermute | solution.py:38
  52.6 7.8 %collective-permute-start.12 = (f32[2,32,768]{2,1,0:T(8,128)S(1)}, f32[2,32,768]{2,1,0:T(8,128)S(1)}, u32[]{:S(2)}, u32[]{:S(2)}) collective-permute-start(f32[2,32,768]{2,1,0:T(8,128)S(1)} %pad_maximum_fusion.3), channel_id=1, source_target_pairs={{0,2},{1,3},{2,0},{3,1},{4,6},{5,7},{6,4},{7,5},{8,10},{9,11},{10,... | collective-permute-start | bytes 589832 | tf_op jit(solution)/shard_map/ppermute | solution.py:38
  60.5 10.7 %collective-permute-start.13 = (f32[4,32,768]{2,1,0:T(8,128)S(1)}, f32[4,32,768]{2,1,0:T(8,128)S(1)}, u32[]{:S(2)}, u32[]{:S(2)}) collective-permute-start(f32[4,32,768]{2,1,0:T(8,128)S(1)} %pad_maximum_fusion.2.first_ref), channel_id=1, source_target_pairs={{0,4},{1,5},{2,6},{3,7},{4,0},{5,1},{6,2},{7,3},{8,12},{9,13},{10,... | collective-permute-start | bytes 1179656 | tf_op jit(solution)/shard_map/ppermute | solution.py:38
  71.2 1.7 %copy-start = (f32[512,512]{1,0:T(8,128)S(1)}, f32[512,512]{1,0:T(8,128)}, u32[]{:S(2)}) copy-start(f32[512,512]{1,0:T(8,128)} %z_ref.1) | copy-start | bytes 3145732
  71.2 1.7 %copy-start.1 = (f32[512,256]{1,0:T(8,128)S(1)}, f32[512,256]{1,0:T(8,128)}, u32[]{:S(2)}) copy-start(f32[512,256]{1,0:T(8,128)} %y_ref.1) | copy-start | bytes 1572868
  71.6 2.8 %collective-permute-start.14 = (f32[256,512]{1,0:T(8,128)S(1)}, f32[256,512]{1,0:T(8,128)S(1)}, u32[]{:S(2)}, u32[]{:S(2)}) collective-permute-start(f32[256,512]{1,0:T(8,128)S(1)} %shard_map.62.mine_ref), channel_id=1, source_target_pairs={{0,1},{1,0},{2,3},{3,2},{4,5},{5,4},{6,7},{7,6},{8,9},{9,8},{10,11... | collective-permute-start | bytes 1572872 | tf_op jit(solution)/shard_map/ppermute | solution.py:42

commit v6 on v4

--- a/solution.py
+++ b/solution.py
@@ -12,13 +12,9 @@
 
 def axis_order(chain, core, bits, stage):
     pair, rest = [core, 1 - core], list(range(2, bits))
-    if chain == "low":
-        if stage == "scatter":
-            return pair + rest
-        return (rest + [1, 0]) if core == 0 else ([0] + rest + [1])
     if stage == "scatter":
-        return rest + pair
-    return [core] + rest + [1 - core]
+        return pair + rest if chain == "low" else rest + pair
+    return [1 - core] + rest + [core] if chain == "low" else pair + rest
 
 
 def relative_bits(order, r, first_is_high):
@@ -190,7 +186,10 @@
     low_send, low_keep, high_send, high_keep = run(
         functools.partial(local_kernel, bits),
         [half] * 4,
-        [low_solved, upper_solved, low_basis, upper_basis],
+        [
+            pltpu.with_memory_space_constraint(x, pltpu.HBM)
+            for x in (low_solved, upper_solved, low_basis, upper_basis)
+        ],
         [
             pltpu.VMEM((depth, rank), jnp.float32),
             pltpu.VMEM((depth, 2 * rank), jnp.float32),
@@ -202,7 +201,6 @@
         ],
         flops=6 * unit * depth,
         space=pltpu.HBM,
-        limit=(62 << 20) + (1 << 18),
     )
 
     def rounds(chain, send, keep):

time: 75 us -> 71 us (0.947)
  starting transfers between devices: 26.8 us -> 24 us
  waiting for transfers between devices: 33.4 us -> 35.1 us
  other arithmetic: 1.4 us -> 0.33 us
  Pallas kernels: 11.6 us -> 10.6 us
    ppermute x12, starting transfers between devices: 21.7 us -> 18.7 us  [step(): return lax.ppermute(x, AXES, pairs)]
    ppermute x3, waiting for transfers between devices: 3.37 us -> 4.68 us  [flip(): lax.ppermute(x, axis, [(i, i ^ 1 << bit) for i in range(lax.axis_size(axi...]
    add x3, other arithmetic: 1.16 us -> 0.08 us  [rounds(): send = keep[half:] + got[half:]]
    pallas_call x5, Pallas kernels: 11.6 us -> 10.6 us  [run(): pl.pallas_call(kernel, out_shape=shapes, in_specs=[pl.BlockSpec(memory_sp...]
  transfers between devices with their start and end apart: 15 -> 15, of which waited for: 12 -> 14; matrix products, arithmetic and copies ran while one was open for 2% -> 0% of each run, Pallas kernels for 5% -> 5%
where the time goes in v6:
time: 71 us; the launch traced here: 70.9 us
  waiting for transfers between devices  35.1 us (49%)
  starting transfers between devices  24 us (34%)
  Pallas kernels  10.6 us (15%)
  between operations  0.78 us (1%)
    ppermute x12, waiting for transfers between devices, step(): return lax.ppermute(x, AXES, pairs)  30.4 us
    ppermute x12, starting transfers between devices, step(): return lax.ppermute(x, AXES, pairs)  18.7 us
    pallas_call x5, Pallas kernels, run(): pl.pallas_call(kernel, out_shape=shapes, in_specs=[pl.BlockSpec(memory_sp...  10.6 us
    ppermute x3, starting transfers between devices, flip(): lax.ppermute(x, axis, [(i, i ^ 1 << bit) for i in range(lax.axis_size(axi...  5.38 us
    ppermute x3, waiting for transfers between devices, flip(): lax.ppermute(x, axis, [(i, i ^ 1 << bit) for i in range(lax.axis_size(axi...  4.68 us
  transfers between devices with their start and end apart: 15, of which 14 were waited for; matrix products, arithmetic and copies ran while one was open for 0% of the time, Pallas kernels for 5%

profile of v6, /device:TPU:0, one launch (start us, length us, event | category | flops | bytes accessed | tf_op | source)
XLA Modules:
  0.0 70.9 jit_solution(8846951759997887568)
XLA Ops:
  0.6 4.2 %shard_map.59 = (f32[4,32,768]{2,1,0:T(8,128)S(1)}, f32[4,32,768]{2,1,0:T(8,128)S(1)}, f32[4,32,768]{2,1,0:T(8,128)S(1)}, f32[4,32,768]{2,1,0:T(8,128)S(1)}) custom-call(f32[512,256]{1,0:T(8,128)} %y_ref.1, f32[512,512]{1,0:T(8,128)} %z_ref.1, f32[512,256]{1,0:T(8,128)} %refs_2_.1, f32[512,256]{1,0:T(8,128)} %refs_3_.1), custom_call_target="tpu_custom_call" | custom-call | flops 1207959552 | bytes 4194304 | tf_op jit(solution)/shard_map/pallas_call | solution.py:158
  4.8 3.0 %collective-permute-start = (f32[4,32,768]{2,1,0:T(8,128)S(1)}, f32[4,32,768]{2,1,0:T(8,128)S(1)}, u32[]{:S(2)}, u32[]{:S(2)}) collective-permute-start(f32[4,32,768]{2,1,0:T(8,128)S(1)} %get-tuple-element.23), channel_id=1, source_target_pairs={{0,2},{1,5},{2,0},{3,7},{4,6},{5,1},{6,4},{7,3},{8,10},{9,13},{10,... | collective-permute-start | bytes 1179656 | tf_op jit(solution)/shard_map/ppermute | solution.py:37
  7.9 1.6 %collective-permute-start.2 = (f32[4,32,768]{2,1,0:T(8,128)S(1)}, f32[4,32,768]{2,1,0:T(8,128)S(1)}, u32[]{:S(2)}, u32[]{:S(2)}) collective-permute-start(f32[4,32,768]{2,1,0:T(8,128)S(1)} %get-tuple-element.24), channel_id=1, source_target_pairs={{0,8},{1,9},{2,10},{3,11},{4,12},{5,13},{6,14},{7,15},{8,0},{9,1},... | collective-permute-start | bytes 1179656 | tf_op jit(solution)/shard_map/ppermute | solution.py:37
  9.4 4.2 %collective-permute-done = f32[4,32,768]{2,1,0:T(8,128)S(1)} collective-permute-done((f32[4,32,768]{2,1,0:T(8,128)S(1)}, f32[4,32,768]{2,1,0:T(8,128)S(1)}, u32[]{:S(2)}, u32[]{:S(2)}) %collective-permute-start) | collective-permute-done | bytes 393248 | tf_op jit(solution)/shard_map/ppermute | solution.py:37
  13.6 0.1 slice_add_fusion.2
  13.7 2.1 %collective-permute-start.1 = (f32[2,32,768]{2,1,0:T(8,128)S(1)}, f32[2,32,768]{2,1,0:T(8,128)S(1)}, u32[]{:S(2)}, u32[]{:S(2)}) collective-permute-start(f32[2,32,768]{2,1,0:T(8,128)S(1)} %get-tuple-element.44), channel_id=1, source_target_pairs={{0,4},{1,3},{2,6},{3,1},{4,0},{5,7},{6,2},{7,5},{8,12},{9,11},{10,... | collective-permute-start | bytes 589832 | tf_op jit(solution)/shard_map/ppermute | solution.py:37
  15.8 2.7 %collective-permute-done.2 = f32[4,32,768]{2,1,0:T(8,128)S(1)} collective-permute-done((f32[4,32,768]{2,1,0:T(8,128)S(1)}, f32[4,32,768]{2,1,0:T(8,128)S(1)}, u32[]{:S(2)}, u32[]{:S(2)}) %collective-permute-start.2) | collective-permute-done | bytes 393248 | tf_op jit(solution)/shard_map/ppermute | solution.py:37
  18.5 0.1 slice_add_fusion
  18.5 1.5 %collective-permute-start.4 = (f32[2,32,768]{2,1,0:T(8,128)S(1)}, f32[2,32,768]{2,1,0:T(8,128)S(1)}, u32[]{:S(2)}, u32[]{:S(2)}) collective-permute-start(f32[2,32,768]{2,1,0:T(8,128)S(1)} %get-tuple-element.43), channel_id=1, source_target_pairs={{0,2},{1,5},{2,0},{3,7},{4,6},{5,1},{6,4},{7,3},{8,10},{9,13},{10,... | collective-permute-start | bytes 589832 | tf_op jit(solution)/shard_map/ppermute | solution.py:37
  20.0 0.3 collective-permute-done.1
  20.3 1.6 %collective-permute-start.3 = (f32[1,32,768]{2,1,0:T(8,128)S(1)}, f32[1,32,768]{2,1,0:T(8,128)S(1)}, u32[]{:S(2)}, u32[]{:S(2)}) collective-permute-start(f32[1,32,768]{2,1,0:T(8,128)S(1)} %slice_add_fusion.6), channel_id=1, source_target_pairs={{0,8},{1,9},{2,10},{3,11},{4,12},{5,13},{6,14},{7,15},{8,0},{9,1},... | collective-permute-start | bytes 294920 | tf_op jit(solution)/shard_map/ppermute | solution.py:37
  22.0 2.3 %collective-permute-done.4 = f32[2,32,768]{2,1,0:T(8,128)S(1)} collective-permute-done((f32[2,32,768]{2,1,0:T(8,128)S(1)}, f32[2,32,768]{2,1,0:T(8,128)S(1)}, u32[]{:S(2)}, u32[]{:S(2)}) %collective-permute-start.4) | collective-permute-done | bytes 196640 | tf_op jit(solution)/shard_map/ppermute | solution.py:37
  24.3 0.4 collective-permute-start.6
  24.7 0.3 collective-permute-done.3
  25.0 2.7 %collective-permute-start.5 = (f32[32,768]{1,0:T(8,128)S(1)}, f32[32,768]{1,0:T(8,128)S(1)}, u32[]{:S(2)}, u32[]{:S(2)}) collective-permute-start(f32[32,768]{1,0:T(8,128)S(1)} %bitcast.8), channel_id=1, source_target_pairs={{0,16},{2,18},{4,20},{6,22},{8,24},{10,26},{12,28},{14,30},{16,0},... | collective-permute-start | bytes 294920 | tf_op jit(solution)/shard_map/ppermute | solution.py:41
  27.7 1.3 %collective-permute-done.6 = f32[1,32,768]{2,1,0:T(8,128)S(1)} collective-permute-done((f32[1,32,768]{2,1,0:T(8,128)S(1)}, f32[1,32,768]{2,1,0:T(8,128)S(1)}, u32[]{:S(2)}, u32[]{:S(2)}) %collective-permute-start.6) | collective-permute-done | bytes 98336 | tf_op jit(solution)/shard_map/ppermute | solution.py:37
  29.0 2.7 %collective-permute-start.8 = (f32[32,768]{1,0:T(8,128)S(1)}, f32[32,768]{1,0:T(8,128)S(1)}, u32[]{:S(2)}, u32[]{:S(2)}) collective-permute-start(f32[32,768]{1,0:T(8,128)S(1)} %fusion.1), channel_id=1, source_target_pairs={{0,16},{2,18},{4,20},{6,22},{8,24},{10,26},{12,28},{14,30},{16,0},... | collective-permute-start | bytes 294920 | tf_op jit(solution)/shard_map/ppermute | solution.py:41
  31.6 2.8 %collective-permute-done.5 = f32[32,768]{1,0:T(8,128)S(1)} collective-permute-done((f32[32,768]{1,0:T(8,128)S(1)}, f32[32,768]{1,0:T(8,128)S(1)}, u32[]{:S(2)}, u32[]{:S(2)}) %collective-permute-start.5) | collective-permute-done | bytes 98336 | tf_op jit(solution)/shard_map/ppermute | solution.py:41
  34.4 1.0 %collective-permute-start.7 = (f32[1,2,32,768]{3,2,1,0:T(8,128)S(1)}, f32[1,2,32,768]{3,2,1,0:T(8,128)S(1)}, u32[]{:S(2)}, u32[]{:S(2)}) collective-permute-start(f32[1,2,32,768]{3,2,1,0:T(8,128)S(1)} %maximum_bitcast_fusion), channel_id=1, source_target_pairs={{0,4},{1,3},{2,6},{3,1},{4,0},{5,7},{6,2},{7,5},{8,12},{9,11},{10,... | collective-permute-start | bytes 589832 | tf_op jit(solution)/shard_map/ppermute | solution.py:37
  35.4 1.4 %collective-permute-done.8 = f32[32,768]{1,0:T(8,128)S(1)} collective-permute-done((f32[32,768]{1,0:T(8,128)S(1)}, f32[32,768]{1,0:T(8,128)S(1)}, u32[]{:S(2)}, u32[]{:S(2)}) %collective-permute-start.8) | collective-permute-done | bytes 98336 | tf_op jit(solution)/shard_map/ppermute | solution.py:41
  36.8 3.3 %collective-permute-done.7 = f32[1,2,32,768]{3,2,1,0:T(8,128)S(1)} collective-permute-done((f32[1,2,32,768]{3,2,1,0:T(8,128)S(1)}, f32[1,2,32,768]{3,2,1,0:T(8,128)S(1)}, u32[]{:S(2)}, u32[]{:S(2)}) %collective-permute-start.7) | collective-permute-done | bytes 196640 | tf_op jit(solution)/shard_map/ppermute | solution.py:37
  40.2 0.7 collective-permute-start.9
  40.9 2.1 %collective-permute-start.10 = (f32[1,32,1024]{2,1,0:T(8,128)S(1)}, f32[1,32,1024]{2,1,0:T(8,128)S(1)}, u32[]{:S(2)}, u32[]{:S(2)}) collective-permute-start(f32[1,32,1024]{2,1,0:T(8,128)S(1)} %maximum_bitcast_fusion.1), channel_id=1, source_target_pairs={{0,2},{1,5},{2,0},{3,7},{4,6},{5,1},{6,4},{7,3},{8,10},{9,13},{10,... | collective-permute-start | bytes 393224 | tf_op jit(solution)/shard_map/ppermute | solution.py:37
  43.0 4.3 %collective-permute-done.10 = f32[1,32,1024]{2,1,0:T(8,128)S(1)} collective-permute-done((f32[1,32,1024]{2,1,0:T(8,128)S(1)}, f32[1,32,1024]{2,1,0:T(8,128)S(1)}, u32[]{:S(2)}, u32[]{:S(2)}) %collective-permute-start.10) | collective-permute-done | bytes 131104 | tf_op jit(solution)/shard_map/ppermute | solution.py:37
  47.4 1.9 %collective-permute-start.12 = (f32[2,32,1024]{2,1,0:T(8,128)S(1)}, f32[2,32,1024]{2,1,0:T(8,128)S(1)}, u32[]{:S(2)}, u32[]{:S(2)}) collective-permute-start(f32[2,32,1024]{2,1,0:T(8,128)S(1)} %pad_maximum_fusion.3), channel_id=1, source_target_pairs={{0,4},{1,3},{2,6},{3,1},{4,0},{5,7},{6,2},{7,5},{8,12},{9,11},{10,... | collective-permute-start | bytes 786440 | tf_op jit(solution)/shard_map/ppermute | solution.py:37
  49.3 0.0 collective-permute-done.9
  49.3 0.1 pad_maximum_fusion.first_ref
  49.3 1.4 %collective-permute-start.11 = (f32[4,2,32,768]{3,2,1,0:T(8,128)S(1)}, f32[4,2,32,768]{3,2,1,0:T(8,128)S(1)}, u32[]{:S(2)}, u32[]{:S(2)}) collective-permute-start(f32[4,2,32,768]{3,2,1,0:T(8,128)S(1)} %pad_maximum_fusion.first_ref), channel_id=1, source_target_pairs={{0,2},{1,5},{2,0},{3,7},{4,6},{5,1},{6,4},{7,3},{8,10},{9,13},{10,... | collective-permute-start | bytes 2359304 | tf_op jit(solution)/shard_map/ppermute | solution.py:37
  50.7 6.0 %collective-permute-done.12 = f32[2,32,1024]{2,1,0:T(8,128)S(1)} collective-permute-done((f32[2,32,1024]{2,1,0:T(8,128)S(1)}, f32[2,32,1024]{2,1,0:T(8,128)S(1)}, u32[]{:S(2)}, u32[]{:S(2)}) %collective-permute-start.12) | collective-permute-done | bytes 262176 | tf_op jit(solution)/shard_map/ppermute | solution.py:37
  56.7 1.4 %collective-permute-start.13 = (f32[4,32,1024]{2,1,0:T(8,128)S(1)}, f32[4,32,1024]{2,1,0:T(8,128)S(1)}, u32[]{:S(2)}, u32[]{:S(2)}) collective-permute-start(f32[4,32,1024]{2,1,0:T(8,128)S(1)} %pad_maximum_fusion.1.first_ref), channel_id=1, source_target_pairs={{0,8},{1,9},{2,10},{3,11},{4,12},{5,13},{6,14},{7,15},{8,0},{9,1},... | collective-permute-start | bytes 1572872 | tf_op jit(solution)/shard_map/ppermute | solution.py:37
  58.1 3.3 %collective-permute-done.11.second_ref = f32[4,2,32,768]{3,2,1,0:T(8,128)S(1)} collective-permute-done((f32[4,2,32,768]{3,2,1,0:T(8,128)S(1)}, f32[4,2,32,768]{3,2,1,0:T(8,128)S(1)}, u32[]{:S(2)}, u32[]{:S(2)}) %collective-permute-start.11) | collective-permute-done | bytes 786464 | tf_op jit(solution)/shard_map/ppermute | solution.py:37
  61.4 2.1 %shard_map.60.update_ref = f32[2,256,512]{2,1,0:T(8,128)S(1)} custom-call(f32[4,2,32,768]{3,2,1,0:T(8,128)S(1)} %pad_maximum_fusion.first_ref, f32[4,2,32,768]{3,2,1,0:T(8,128)S(1)} %collective-permute-done.11.second_ref), custom_call_target="tpu_custom_call" | custom-call | flops 1207959552 | bytes 2621440 | tf_op jit(solution)/shard_map/pallas_call | solution.py:158
  63.5 0.0 copy-start
  63.5 0.0 copy-start.1
  63.5 2.5 %collective-permute-done.13.second_ref = f32[4,32,1024]{2,1,0:T(8,128)S(1)} collective-permute-done((f32[4,32,1024]{2,1,0:T(8,128)S(1)}, f32[4,32,1024]{2,1,0:T(8,128)S(1)}, u32[]{:S(2)}, u32[]{:S(2)}) %collective-permute-start.13) | collective-permute-done | bytes 524320 | tf_op jit(solution)/shard_map/ppermute | solution.py:37
  66.0 0.7 shard_map.62.mine_ref
  66.7 0.1 collective-permute-start.14
  66.7 0.0 copy-done
  66.8 0.0 copy-done.1
  66.8 1.4 %shard_map.61 = (f32[512,256]{1,0:T(8,128)}, bf16[2,512,256]{2,1,0:T(8,128)(2,1)S(1)}, f32[512,256]{1,0:T(8,128)S(1)}) custom-call(f32[512,256]{1,0:T(8,128)S(1)} %copy-done.1, f32[512,512]{1,0:T(8,128)S(1)} %copy-done, f32[2,256,512]{2,1,0:T(8,128)S(1)} %shard_map.60.update_ref), custom_call_target="tpu_custom_call" | custom-call | flops 402653184 | bytes 4718592 | tf_op jit(solution)/shard_map/pallas_call | solution.py:158
  68.1 0.5 collective-permute-done.14.other_ref
  68.6 2.2 %shard_map.63 = f32[512,256]{1,0:T(8,128)} custom-call(f32[256,512]{1,0:T(8,128)S(1)} %shard_map.62.mine_ref, f32[256,512]{1,0:T(8,128)S(1)} %collective-permute-done.14.other_ref, bf16[2,512,256]{2,1,0:T(8,128)(2,1)S(1)} %get-tuple-element.40.halves_ref, f32[512,256]{1,0:T(8,128)S(1)} %get-tuple-element.41.next_ref), custom_call_target="tpu_custom_call" | custom-call | flops 503316480 | bytes 3145728 | tf_op jit(solution)/shard_map/pallas_call | solution.py:158
  (12 shorter events, 0.2 us)
Async XLA Ops:
  4.8 8.8 %collective-permute-start = (f32[4,32,768]{2,1,0:T(8,128)S(1)}, f32[4,32,768]{2,1,0:T(8,128)S(1)}, u32[]{:S(2)}, u32[]{:S(2)}) collective-permute-start(f32[4,32,768]{2,1,0:T(8,128)S(1)} %get-tuple-element.23), channel_id=1, source_target_pairs={{0,2},{1,5},{2,0},{3,7},{4,6},{5,1},{6,4},{7,3},{8,10},{9,13},{10,... | collective-permute-start | bytes 1179656 | tf_op jit(solution)/shard_map/ppermute | solution.py:37
  7.9 10.6 %collective-permute-start.2 = (f32[4,32,768]{2,1,0:T(8,128)S(1)}, f32[4,32,768]{2,1,0:T(8,128)S(1)}, u32[]{:S(2)}, u32[]{:S(2)}) collective-permute-start(f32[4,32,768]{2,1,0:T(8,128)S(1)} %get-tuple-element.24), channel_id=1, source_target_pairs={{0,8},{1,9},{2,10},{3,11},{4,12},{5,13},{6,14},{7,15},{8,0},{9,1},... | collective-permute-start | bytes 1179656 | tf_op jit(solution)/shard_map/ppermute | solution.py:37
  13.7 6.6 %collective-permute-start.1 = (f32[2,32,768]{2,1,0:T(8,128)S(1)}, f32[2,32,768]{2,1,0:T(8,128)S(1)}, u32[]{:S(2)}, u32[]{:S(2)}) collective-permute-start(f32[2,32,768]{2,1,0:T(8,128)S(1)} %get-tuple-element.44), channel_id=1, source_target_pairs={{0,4},{1,3},{2,6},{3,1},{4,0},{5,7},{6,2},{7,5},{8,12},{9,11},{10,... | collective-permute-start | bytes 589832 | tf_op jit(solution)/shard_map/ppermute | solution.py:37
  18.5 5.7 %collective-permute-start.4 = (f32[2,32,768]{2,1,0:T(8,128)S(1)}, f32[2,32,768]{2,1,0:T(8,128)S(1)}, u32[]{:S(2)}, u32[]{:S(2)}) collective-permute-start(f32[2,32,768]{2,1,0:T(8,128)S(1)} %get-tuple-element.43), channel_id=1, source_target_pairs={{0,2},{1,5},{2,0},{3,7},{4,6},{5,1},{6,4},{7,3},{8,10},{9,13},{10,... | collective-permute-start | bytes 589832 | tf_op jit(solution)/shard_map/ppermute | solution.py:37
  20.3 4.7 %collective-permute-start.3 = (f32[1,32,768]{2,1,0:T(8,128)S(1)}, f32[1,32,768]{2,1,0:T(8,128)S(1)}, u32[]{:S(2)}, u32[]{:S(2)}) collective-permute-start(f32[1,32,768]{2,1,0:T(8,128)S(1)} %slice_add_fusion.6), channel_id=1, source_target_pairs={{0,8},{1,9},{2,10},{3,11},{4,12},{5,13},{6,14},{7,15},{8,0},{9,1},... | collective-permute-start | bytes 294920 | tf_op jit(solution)/shard_map/ppermute | solution.py:37
  24.3 4.7 %collective-permute-start.6 = (f32[1,32,768]{2,1,0:T(8,128)S(1)}, f32[1,32,768]{2,1,0:T(8,128)S(1)}, u32[]{:S(2)}, u32[]{:S(2)}) collective-permute-start(f32[1,32,768]{2,1,0:T(8,128)S(1)} %slice_add_fusion.5), channel_id=1, source_target_pairs={{0,4},{1,3},{2,6},{3,1},{4,0},{5,7},{6,2},{7,5},{8,12},{9,11},{10,... | collective-permute-start | bytes 294920 | tf_op jit(solution)/shard_map/ppermute | solution.py:37
  25.0 9.4 %collective-permute-start.5 = (f32[32,768]{1,0:T(8,128)S(1)}, f32[32,768]{1,0:T(8,128)S(1)}, u32[]{:S(2)}, u32[]{:S(2)}) collective-permute-start(f32[32,768]{1,0:T(8,128)S(1)} %bitcast.8), channel_id=1, source_target_pairs={{0,16},{2,18},{4,20},{6,22},{8,24},{10,26},{12,28},{14,30},{16,0},... | collective-permute-start | bytes 294920 | tf_op jit(solution)/shard_map/ppermute | solution.py:41
  29.0 7.8 %collective-permute-start.8 = (f32[32,768]{1,0:T(8,128)S(1)}, f32[32,768]{1,0:T(8,128)S(1)}, u32[]{:S(2)}, u32[]{:S(2)}) collective-permute-start(f32[32,768]{1,0:T(8,128)S(1)} %fusion.1), channel_id=1, source_target_pairs={{0,16},{2,18},{4,20},{6,22},{8,24},{10,26},{12,28},{14,30},{16,0},... | collective-permute-start | bytes 294920 | tf_op jit(solution)/shard_map/ppermute | solution.py:41
  34.4 5.7 %collective-permute-start.7 = (f32[1,2,32,768]{3,2,1,0:T(8,128)S(1)}, f32[1,2,32,768]{3,2,1,0:T(8,128)S(1)}, u32[]{:S(2)}, u32[]{:S(2)}) collective-permute-start(f32[1,2,32,768]{3,2,1,0:T(8,128)S(1)} %maximum_bitcast_fusion), channel_id=1, source_target_pairs={{0,4},{1,3},{2,6},{3,1},{4,0},{5,7},{6,2},{7,5},{8,12},{9,11},{10,... | collective-permute-start | bytes 589832 | tf_op jit(solution)/shard_map/ppermute | solution.py:37
  40.2 9.1 %collective-permute-start.9 = (f32[2,2,32,768]{3,2,1,0:T(8,128)S(1)}, f32[2,2,32,768]{3,2,1,0:T(8,128)S(1)}, u32[]{:S(2)}, u32[]{:S(2)}) collective-permute-start(f32[2,2,32,768]{3,2,1,0:T(8,128)S(1)} %pad_maximum_fusion.2), channel_id=1, source_target_pairs={{0,8},{1,9},{2,10},{3,11},{4,12},{5,13},{6,14},{7,15},{8,0},{9,1},... | collective-permute-start | bytes 1179656 | tf_op jit(solution)/shard_map/ppermute | solution.py:37
  40.9 6.5 %collective-permute-start.10 = (f32[1,32,1024]{2,1,0:T(8,128)S(1)}, f32[1,32,1024]{2,1,0:T(8,128)S(1)}, u32[]{:S(2)}, u32[]{:S(2)}) collective-permute-start(f32[1,32,1024]{2,1,0:T(8,128)S(1)} %maximum_bitcast_fusion.1), channel_id=1, source_target_pairs={{0,2},{1,5},{2,0},{3,7},{4,6},{5,1},{6,4},{7,3},{8,10},{9,13},{10,... | collective-permute-start | bytes 393224 | tf_op jit(solution)/shard_map/ppermute | solution.py:37
  47.4 9.3 %collective-permute-start.12 = (f32[2,32,1024]{2,1,0:T(8,128)S(1)}, f32[2,32,1024]{2,1,0:T(8,128)S(1)}, u32[]{:S(2)}, u32[]{:S(2)}) collective-permute-start(f32[2,32,1024]{2,1,0:T(8,128)S(1)} %pad_maximum_fusion.3), channel_id=1, source_target_pairs={{0,4},{1,3},{2,6},{3,1},{4,0},{5,7},{6,2},{7,5},{8,12},{9,11},{10,... | collective-permute-start | bytes 786440 | tf_op jit(solution)/shard_map/ppermute | solution.py:37
  49.3 12.1 %collective-permute-start.11 = (f32[4,2,32,768]{3,2,1,0:T(8,128)S(1)}, f32[4,2,32,768]{3,2,1,0:T(8,128)S(1)}, u32[]{:S(2)}, u32[]{:S(2)}) collective-permute-start(f32[4,2,32,768]{3,2,1,0:T(8,128)S(1)} %pad_maximum_fusion.first_ref), channel_id=1, source_target_pairs={{0,2},{1,5},{2,0},{3,7},{4,6},{5,1},{6,4},{7,3},{8,10},{9,13},{10,... | collective-permute-start | bytes 2359304 | tf_op jit(solution)/shard_map/ppermute | solution.py:37
  56.7 9.2 %collective-permute-start.13 = (f32[4,32,1024]{2,1,0:T(8,128)S(1)}, f32[4,32,1024]{2,1,0:T(8,128)S(1)}, u32[]{:S(2)}, u32[]{:S(2)}) collective-permute-start(f32[4,32,1024]{2,1,0:T(8,128)S(1)} %pad_maximum_fusion.1.first_ref), channel_id=1, source_target_pairs={{0,8},{1,9},{2,10},{3,11},{4,12},{5,13},{6,14},{7,15},{8,0},{9,1},... | collective-permute-start | bytes 1572872 | tf_op jit(solution)/shard_map/ppermute | solution.py:37
  63.5 3.3 %copy-start = (f32[512,512]{1,0:T(8,128)S(1)}, f32[512,512]{1,0:T(8,128)}, u32[]{:S(2)}) copy-start(f32[512,512]{1,0:T(8,128)} %z_ref.1) | copy-start | bytes 3145732
  63.5 3.3 %copy-start.1 = (f32[512,256]{1,0:T(8,128)S(1)}, f32[512,256]{1,0:T(8,128)}, u32[]{:S(2)}) copy-start(f32[512,256]{1,0:T(8,128)} %y_ref.1) | copy-start | bytes 1572868
  66.7 2.0 %collective-permute-start.14 = (f32[256,512]{1,0:T(8,128)S(1)}, f32[256,512]{1,0:T(8,128)S(1)}, u32[]{:S(2)}, u32[]{:S(2)}) collective-permute-start(f32[256,512]{1,0:T(8,128)S(1)} %shard_map.62.mine_ref), channel_id=1, source_target_pairs={{0,1},{1,0},{2,3},{3,2},{4,5},{5,4},{6,7},{7,6},{8,9},{9,8},{10,11... | collective-permute-start | bytes 1572872 | tf_op jit(solution)/shard_map/ppermute | solution.py:41

commit v7 on v6

--- a/solution.py
+++ b/solution.py
@@ -62,18 +62,25 @@
     return lax.bitwise_xor(own, jnp.where(core == 0, moves[0], moves[1]))
 
 
-def local_kernel(bits, *refs):
-    inputs, outputs = refs[:4], refs[4:8]
-    loaded, (joined, sums), (in_sems,) = refs[8:12], refs[12:14], refs[14:]
+def hand_out(sums, chain, bits, send_ref, keep_ref):
+    blocks = 1 << bits
+    rows = sums.shape[0] // blocks
+    for r in range(blocks):
+        start = pl.multiple_of(block_of(r, chain, bits, "scatter") * rows, rows)
+        target = send_ref if r >= blocks // 2 else keep_ref
+        target[r % (blocks // 2)] = sums[pl.ds(start, rows), :]
+
+
+def low_kernel(bits, *refs):
+    inputs, (send_ref, keep_ref, joined) = refs[:3], refs[3:6]
+    loaded, (sums, sems) = refs[6:9], refs[9:]
     depth, rank = inputs[0].shape
-    blocks = 1 << bits
-    rows = rank // blocks
-    parts = 2
+    parts = sems.shape[0]
     part = depth // parts
     copies = [
         [
             pltpu.make_async_copy(
-                source.at[pl.ds(p * part, part)], target.at[pl.ds(p * part, part)], in_sems.at[p, i]
+                source.at[pl.ds(p * part, part)], target.at[pl.ds(p * part, part)], sems.at[p, i]
             )
             for i, (source, target) in enumerate(zip(inputs, loaded))
         ]
@@ -82,26 +89,25 @@
     for group in copies:
         for copy in group:
             copy.start()
-    y, z, low_basis, high_basis = loaded
+    y, z, basis = loaded
     dims = (((0,), (0,)), ((), ()))
     for p in range(parts):
         span = pl.ds(p * part, part)
-        for copy in copies[p][:3]:
+        for copy in copies[p]:
             copy.wait()
         for source, columns in ((y, pl.ds(0, rank)), (z, pl.ds(rank, 2 * rank))):
             high, low = split(source[span, :])
             joined[0, span, columns] = high
             joined[1, span, columns] = low
-        term = dot3(split(low_basis[span, :]), (joined[0, span, :], joined[1, span, :]), dims)
-        sums[0] = term if p == 0 else sums[0] + term
-    for p in range(parts):
-        copies[p][3].wait()
-    sums[1] = dot3(split(high_basis[...]), (joined[0], joined[1]), dims)
-    for i, chain in enumerate(("low", "high")):
-        for r in range(blocks):
-            start = pl.multiple_of(block_of(r, chain, bits, "scatter") * rows, rows)
-            target = outputs[2 * i + (0 if r >= blocks // 2 else 1)]
-            target[r % (blocks // 2)] = sums[i, pl.ds(start, rows), :]
+        term = dot3(split(basis[span, :]), (joined[0, span, :], joined[1, span, :]), dims)
+        sums[...] = term if p == 0 else sums[...] + term
+    hand_out(sums, "low", bits, send_ref, keep_ref)
+
+
+def high_kernel(bits, basis_ref, joined, send_ref, keep_ref, sums):
+    dims = (((0,), (0,)), ((), ()))
+    sums[...] = dot3(split(basis_ref[...]), (joined[0], joined[1]), dims)
+    hand_out(sums, "high", bits, send_ref, keep_ref)
 
 
 def place(parts, chain, bits, target):
@@ -183,24 +189,29 @@
     unit = 6 * rank * rank
 
     half = array(blocks // 2, rows, 3 * rank)
-    low_send, low_keep, high_send, high_keep = run(
-        functools.partial(local_kernel, bits),
-        [half] * 4,
+    low_send, low_keep, joined = run(
+        functools.partial(low_kernel, bits),
+        [half, half, array(2, depth, 3 * rank, dtype=jnp.bfloat16)],
         [
             pltpu.with_memory_space_constraint(x, pltpu.HBM)
-            for x in (low_solved, upper_solved, low_basis, upper_basis)
+            for x in (low_solved, upper_solved, low_basis)
         ],
         [
             pltpu.VMEM((depth, rank), jnp.float32),
             pltpu.VMEM((depth, 2 * rank), jnp.float32),
             pltpu.VMEM((depth, rank), jnp.float32),
-            pltpu.VMEM((depth, rank), jnp.float32),
-            pltpu.VMEM((2, depth, 3 * rank), jnp.bfloat16),
-            pltpu.VMEM((2, rank, 3 * rank), jnp.float32),
-            pltpu.SemaphoreType.DMA((2, 4)),
+            pltpu.VMEM((rank, 3 * rank), jnp.float32),
+            pltpu.SemaphoreType.DMA((2, 3)),
         ],
-        flops=6 * unit * depth,
+        flops=3 * unit * depth,
         space=pltpu.HBM,
+    )
+    high_send, high_keep = run(
+        functools.partial(high_kernel, bits),
+        [half, half],
+        [upper_basis, joined],
+        [pltpu.VMEM((rank, 3 * rank), jnp.float32)],
+        flops=3 * unit * depth,
     )
 
     def rounds(chain, send, keep):
@@ -225,12 +236,16 @@
 
     low, high = rounds("low", low_send, low_keep), rounds("high", high_send, high_keep)
     (low_out, low_move), (high_out, high_move) = next(low), next(high)
-    while low_move is not None:
+    for t in range(2 * bits + 1):
         low_got, high_got = low_move(low_out), high_move(high_out)
-        low_out, low_move = low.send(after(low_got, high_out))
-        if low_move is not None:
-            high_got = after(high_got, low_out)
-        high_out, high_move = high.send(high_got)
+        if bits < t < 2 * bits:
+            high_out, high_move = high.send(high_got)
+            low_out, low_move = low.send(after(low_got, high_out))
+        else:
+            low_out, low_move = low.send(after(low_got, high_out))
+            if low_move is not None:
+                high_got = after(high_got, low_out)
+            high_out, high_move = high.send(high_got)
     low_parts, high_parts = low_out, high_out
 
     (update,) = run(

time: 71 us -> 72.1 us (1.015)
  waiting for transfers between devices: 35.1 us -> 38.9 us
  starting transfers between devices: 24 us -> 22.3 us
  Pallas kernels: 10.6 us -> 9.67 us
    ppermute x12, waiting for transfers between devices: 30.4 us -> 33.3 us  [step(): return lax.ppermute(x, AXES, pairs)]
    ppermute x12, starting transfers between devices: 18.7 us -> 16.8 us  [step(): return lax.ppermute(x, AXES, pairs)]
    ppermute x3, waiting for transfers between devices: 4.68 us -> 5.63 us  [flip(): lax.ppermute(x, axis, [(i, i ^ 1 << bit) for i in range(lax.axis_size(axi...]
    pallas_call x5 -> x6, Pallas kernels: 10.6 us -> 9.67 us  [run(): pl.pallas_call(kernel, out_shape=shapes, in_specs=[pl.BlockSpec(memory_sp...]
  transfers between devices with their start and end apart: 15 -> 15, of which waited for: 14 -> 14; matrix products, arithmetic and copies ran while one was open for 0% -> 0% of each run, Pallas kernels for 5% -> 6%
where the time goes in v7:
time: 72.1 us; the launch traced here: 72 us
  waiting for transfers between devices  38.9 us (54%)
  starting transfers between devices  22.3 us (31%)
  Pallas kernels  9.67 us (13%)
  between operations  0.79 us (1%)
    ppermute x12, waiting for transfers between devices, step(): return lax.ppermute(x, AXES, pairs)  33.3 us
    ppermute x12, starting transfers between devices, step(): return lax.ppermute(x, AXES, pairs)  16.8 us
    pallas_call x6, Pallas kernels, run(): pl.pallas_call(kernel, out_shape=shapes, in_specs=[pl.BlockSpec(memory_sp...  9.67 us
    ppermute x3, waiting for transfers between devices, flip(): lax.ppermute(x, axis, [(i, i ^ 1 << bit) for i in range(lax.axis_size(axi...  5.63 us
    ppermute x3, starting transfers between devices, flip(): lax.ppermute(x, axis, [(i, i ^ 1 << bit) for i in range(lax.axis_size(axi...  5.47 us
  transfers between devices with their start and end apart: 15, of which 14 were waited for; matrix products, arithmetic and copies ran while one was open for 0% of the time, Pallas kernels for 6%

profile of v7, /device:TPU:0, one launch (start us, length us, event | category | flops | bytes accessed | tf_op | source)
XLA Modules:
  0.0 72.0 jit_solution(11077046063229680129)
XLA Ops:
  0.6 0.0 copy-start.2
  0.6 2.4 %shard_map.59 = (f32[4,32,768]{2,1,0:T(8,128)S(1)}, f32[4,32,768]{2,1,0:T(8,128)S(1)}, bf16[2,512,768]{2,1,0:T(8,128)(2,1)S(1)}) custom-call(f32[512,256]{1,0:T(8,128)} %y_ref.1, f32[512,512]{1,0:T(8,128)} %z_ref.1, f32[512,256]{1,0:T(8,128)} %refs_2_.1), custom_call_target="tpu_custom_call" | custom-call | flops 603979776 | bytes 6029312 | tf_op jit(solution)/shard_map/pallas_call | solution.py:164
  3.1 3.0 %collective-permute-start = (f32[4,32,768]{2,1,0:T(8,128)S(1)}, f32[4,32,768]{2,1,0:T(8,128)S(1)}, u32[]{:S(2)}, u32[]{:S(2)}) collective-permute-start(f32[4,32,768]{2,1,0:T(8,128)S(1)} %get-tuple-element.22), channel_id=1, source_target_pairs={{0,2},{1,5},{2,0},{3,7},{4,6},{5,1},{6,4},{7,3},{8,10},{9,13},{10,... | collective-permute-start | bytes 1179656 | tf_op jit(solution)/shard_map/ppermute | solution.py:37
  6.1 0.0 copy-done.2
  6.1 0.9 %shard_map.60 = (f32[4,32,768]{2,1,0:T(8,128)S(1)}, f32[4,32,768]{2,1,0:T(8,128)S(1)}) custom-call(f32[512,256]{1,0:T(8,128)S(1)} %copy-done.2, bf16[2,512,768]{2,1,0:T(8,128)(2,1)S(1)} %get-tuple-element.23.joined), custom_call_target="tpu_custom_call" | custom-call | flops 603979776 | bytes 4456448 | tf_op jit(solution)/shard_map/pallas_call | solution.py:164
  7.0 1.6 %collective-permute-start.2 = (f32[4,32,768]{2,1,0:T(8,128)S(1)}, f32[4,32,768]{2,1,0:T(8,128)S(1)}, u32[]{:S(2)}, u32[]{:S(2)}) collective-permute-start(f32[4,32,768]{2,1,0:T(8,128)S(1)} %get-tuple-element.24), channel_id=1, source_target_pairs={{0,8},{1,9},{2,10},{3,11},{4,12},{5,13},{6,14},{7,15},{8,0},{9,1},... | collective-permute-start | bytes 1179656 | tf_op jit(solution)/shard_map/ppermute | solution.py:37
  8.6 3.2 %collective-permute-done = f32[4,32,768]{2,1,0:T(8,128)S(1)} collective-permute-done((f32[4,32,768]{2,1,0:T(8,128)S(1)}, f32[4,32,768]{2,1,0:T(8,128)S(1)}, u32[]{:S(2)}, u32[]{:S(2)}) %collective-permute-start) | collective-permute-done | bytes 393248 | tf_op jit(solution)/shard_map/ppermute | solution.py:37
  11.9 2.1 %collective-permute-start.1 = (f32[2,32,768]{2,1,0:T(8,128)S(1)}, f32[2,32,768]{2,1,0:T(8,128)S(1)}, u32[]{:S(2)}, u32[]{:S(2)}) collective-permute-start(f32[2,32,768]{2,1,0:T(8,128)S(1)} %get-tuple-element.42), channel_id=1, source_target_pairs={{0,4},{1,3},{2,6},{3,1},{4,0},{5,7},{6,2},{7,5},{8,12},{9,11},{10,... | collective-permute-start | bytes 589832 | tf_op jit(solution)/shard_map/ppermute | solution.py:37
  14.0 3.6 %collective-permute-done.2 = f32[4,32,768]{2,1,0:T(8,128)S(1)} collective-permute-done((f32[4,32,768]{2,1,0:T(8,128)S(1)}, f32[4,32,768]{2,1,0:T(8,128)S(1)}, u32[]{:S(2)}, u32[]{:S(2)}) %collective-permute-start.2) | collective-permute-done | bytes 393248 | tf_op jit(solution)/shard_map/ppermute | solution.py:37
  17.7 1.5 %collective-permute-start.4 = (f32[2,32,768]{2,1,0:T(8,128)S(1)}, f32[2,32,768]{2,1,0:T(8,128)S(1)}, u32[]{:S(2)}, u32[]{:S(2)}) collective-permute-start(f32[2,32,768]{2,1,0:T(8,128)S(1)} %get-tuple-element.41), channel_id=1, source_target_pairs={{0,2},{1,5},{2,0},{3,7},{4,6},{5,1},{6,4},{7,3},{8,10},{9,13},{10,... | collective-permute-start | bytes 589832 | tf_op jit(solution)/shard_map/ppermute | solution.py:37
  19.2 0.0 collective-permute-done.1
  19.3 1.7 %collective-permute-start.3 = (f32[1,32,768]{2,1,0:T(8,128)S(1)}, f32[1,32,768]{2,1,0:T(8,128)S(1)}, u32[]{:S(2)}, u32[]{:S(2)}) collective-permute-start(f32[1,32,768]{2,1,0:T(8,128)S(1)} %slice_add_fusion.6), channel_id=1, source_target_pairs={{0,8},{1,9},{2,10},{3,11},{4,12},{5,13},{6,14},{7,15},{8,0},{9,1},... | collective-permute-start | bytes 294920 | tf_op jit(solution)/shard_map/ppermute | solution.py:37
  20.9 2.5 %collective-permute-done.4 = f32[2,32,768]{2,1,0:T(8,128)S(1)} collective-permute-done((f32[2,32,768]{2,1,0:T(8,128)S(1)}, f32[2,32,768]{2,1,0:T(8,128)S(1)}, u32[]{:S(2)}, u32[]{:S(2)}) %collective-permute-start.4) | collective-permute-done | bytes 196640 | tf_op jit(solution)/shard_map/ppermute | solution.py:37
  23.5 0.4 collective-permute-start.6
  23.9 0.1 collective-permute-done.3
  24.0 2.7 %collective-permute-start.5 = (f32[32,768]{1,0:T(8,128)S(1)}, f32[32,768]{1,0:T(8,128)S(1)}, u32[]{:S(2)}, u32[]{:S(2)}) collective-permute-start(f32[32,768]{1,0:T(8,128)S(1)} %bitcast.8), channel_id=1, source_target_pairs={{0,16},{2,18},{4,20},{6,22},{8,24},{10,26},{12,28},{14,30},{16,0},... | collective-permute-start | bytes 294920 | tf_op jit(solution)/shard_map/ppermute | solution.py:41
  26.7 1.4 %collective-permute-done.6 = f32[1,32,768]{2,1,0:T(8,128)S(1)} collective-permute-done((f32[1,32,768]{2,1,0:T(8,128)S(1)}, f32[1,32,768]{2,1,0:T(8,128)S(1)}, u32[]{:S(2)}, u32[]{:S(2)}) %collective-permute-start.6) | collective-permute-done | bytes 98336 | tf_op jit(solution)/shard_map/ppermute | solution.py:37
  28.2 2.7 %collective-permute-start.8 = (f32[32,768]{1,0:T(8,128)S(1)}, f32[32,768]{1,0:T(8,128)S(1)}, u32[]{:S(2)}, u32[]{:S(2)}) collective-permute-start(f32[32,768]{1,0:T(8,128)S(1)} %fusion.1), channel_id=1, source_target_pairs={{0,16},{2,18},{4,20},{6,22},{8,24},{10,26},{12,28},{14,30},{16,0},... | collective-permute-start | bytes 294920 | tf_op jit(solution)/shard_map/ppermute | solution.py:41
  30.8 2.8 %collective-permute-done.5 = f32[32,768]{1,0:T(8,128)S(1)} collective-permute-done((f32[32,768]{1,0:T(8,128)S(1)}, f32[32,768]{1,0:T(8,128)S(1)}, u32[]{:S(2)}, u32[]{:S(2)}) %collective-permute-start.5) | collective-permute-done | bytes 98336 | tf_op jit(solution)/shard_map/ppermute | solution.py:41
  33.6 2.4 %collective-permute-done.8 = f32[32,768]{1,0:T(8,128)S(1)} collective-permute-done((f32[32,768]{1,0:T(8,128)S(1)}, f32[32,768]{1,0:T(8,128)S(1)}, u32[]{:S(2)}, u32[]{:S(2)}) %collective-permute-start.8) | collective-permute-done | bytes 98336 | tf_op jit(solution)/shard_map/ppermute | solution.py:41
  36.0 0.5 collective-permute-start.9
  36.5 1.5 %collective-permute-start.7 = (f32[1,2,32,768]{3,2,1,0:T(8,128)S(1)}, f32[1,2,32,768]{3,2,1,0:T(8,128)S(1)}, u32[]{:S(2)}, u32[]{:S(2)}) collective-permute-start(f32[1,2,32,768]{3,2,1,0:T(8,128)S(1)} %maximum_bitcast_fusion), channel_id=1, source_target_pairs={{0,4},{1,3},{2,6},{3,1},{4,0},{5,7},{6,2},{7,5},{8,12},{9,11},{10,... | collective-permute-start | bytes 589832 | tf_op jit(solution)/shard_map/ppermute | solution.py:37
  38.0 3.6 %collective-permute-done.9 = f32[1,32,1024]{2,1,0:T(8,128)S(1)} collective-permute-done((f32[1,32,1024]{2,1,0:T(8,128)S(1)}, f32[1,32,1024]{2,1,0:T(8,128)S(1)}, u32[]{:S(2)}, u32[]{:S(2)}) %collective-permute-start.9) | collective-permute-done | bytes 131104 | tf_op jit(solution)/shard_map/ppermute | solution.py:37
  41.7 0.5 collective-permute-done.7
  42.2 0.7 %collective-permute-start.10 = (f32[2,2,32,768]{3,2,1,0:T(8,128)S(1)}, f32[2,2,32,768]{3,2,1,0:T(8,128)S(1)}, u32[]{:S(2)}, u32[]{:S(2)}) collective-permute-start(f32[2,2,32,768]{3,2,1,0:T(8,128)S(1)} %pad_maximum_fusion.2), channel_id=1, source_target_pairs={{0,8},{1,9},{2,10},{3,11},{4,12},{5,13},{6,14},{7,15},{8,0},{9,1},... | collective-permute-start | bytes 1179656 | tf_op jit(solution)/shard_map/ppermute | solution.py:37
  42.9 1.2 %collective-permute-start.11 = (f32[2,32,1024]{2,1,0:T(8,128)S(1)}, f32[2,32,1024]{2,1,0:T(8,128)S(1)}, u32[]{:S(2)}, u32[]{:S(2)}) collective-permute-start(f32[2,32,1024]{2,1,0:T(8,128)S(1)} %pad_maximum_fusion.3), channel_id=1, source_target_pairs={{0,4},{1,3},{2,6},{3,1},{4,0},{5,7},{6,2},{7,5},{8,12},{9,11},{10,... | collective-permute-start | bytes 786440 | tf_op jit(solution)/shard_map/ppermute | solution.py:37
  44.1 5.2 %collective-permute-done.11 = f32[2,32,1024]{2,1,0:T(8,128)S(1)} collective-permute-done((f32[2,32,1024]{2,1,0:T(8,128)S(1)}, f32[2,32,1024]{2,1,0:T(8,128)S(1)}, u32[]{:S(2)}, u32[]{:S(2)}) %collective-permute-start.11) | collective-permute-done | bytes 262176 | tf_op jit(solution)/shard_map/ppermute | solution.py:37
  49.3 2.6 %collective-permute-done.10 = f32[2,2,32,768]{3,2,1,0:T(8,128)S(1)} collective-permute-done((f32[2,2,32,768]{3,2,1,0:T(8,128)S(1)}, f32[2,2,32,768]{3,2,1,0:T(8,128)S(1)}, u32[]{:S(2)}, u32[]{:S(2)}) %collective-permute-start.10) | collective-permute-done | bytes 393248 | tf_op jit(solution)/shard_map/ppermute | solution.py:37
  52.0 0.1 pad_maximum_fusion.first_ref
  52.0 2.2 %collective-permute-start.12 = (f32[4,2,32,768]{3,2,1,0:T(8,128)S(1)}, f32[4,2,32,768]{3,2,1,0:T(8,128)S(1)}, u32[]{:S(2)}, u32[]{:S(2)}) collective-permute-start(f32[4,2,32,768]{3,2,1,0:T(8,128)S(1)} %pad_maximum_fusion.first_ref), channel_id=1, source_target_pairs={{0,2},{1,5},{2,0},{3,7},{4,6},{5,1},{6,4},{7,3},{8,10},{9,13},{10,... | collective-permute-start | bytes 2359304 | tf_op jit(solution)/shard_map/ppermute | solution.py:37
  54.3 0.3 collective-permute-start.13
  54.6 9.7 %collective-permute-done.12.second_ref = f32[4,2,32,768]{3,2,1,0:T(8,128)S(1)} collective-permute-done((f32[4,2,32,768]{3,2,1,0:T(8,128)S(1)}, f32[4,2,32,768]{3,2,1,0:T(8,128)S(1)}, u32[]{:S(2)}, u32[]{:S(2)}) %collective-permute-start.12) | collective-permute-done | bytes 786464 | tf_op jit(solution)/shard_map/ppermute | solution.py:37
  64.2 2.1 %shard_map.61.update_ref = f32[2,256,512]{2,1,0:T(8,128)S(1)} custom-call(f32[4,2,32,768]{3,2,1,0:T(8,128)S(1)} %pad_maximum_fusion.first_ref, f32[4,2,32,768]{3,2,1,0:T(8,128)S(1)} %collective-permute-done.12.second_ref), custom_call_target="tpu_custom_call" | custom-call | flops 1207959552 | bytes 2621440 | tf_op jit(solution)/shard_map/pallas_call | solution.py:164
  66.3 0.0 copy-start
  66.3 0.0 copy-start.1
  66.3 0.7 %collective-permute-done.13.second_ref = f32[4,32,1024]{2,1,0:T(8,128)S(1)} collective-permute-done((f32[4,32,1024]{2,1,0:T(8,128)S(1)}, f32[4,32,1024]{2,1,0:T(8,128)S(1)}, u32[]{:S(2)}, u32[]{:S(2)}) %collective-permute-start.13) | collective-permute-done | bytes 524320 | tf_op jit(solution)/shard_map/ppermute | solution.py:37
  67.1 0.7 shard_map.63.mine_ref
  67.8 0.1 collective-permute-start.14
  67.8 0.0 copy-done
  67.8 0.0 copy-done.1
  67.9 1.4 %shard_map.62 = (f32[512,256]{1,0:T(8,128)}, bf16[2,512,256]{2,1,0:T(8,128)(2,1)S(1)}, f32[512,256]{1,0:T(8,128)S(1)}) custom-call(f32[512,256]{1,0:T(8,128)S(1)} %copy-done.1, f32[512,512]{1,0:T(8,128)S(1)} %copy-done, f32[2,256,512]{2,1,0:T(8,128)S(1)} %shard_map.61.update_ref), custom_call_target="tpu_custom_call" | custom-call | flops 402653184 | bytes 4718592 | tf_op jit(solution)/shard_map/pallas_call | solution.py:164
  69.2 0.5 collective-permute-done.14.other_ref
  69.7 2.2 %shard_map.64 = f32[512,256]{1,0:T(8,128)} custom-call(f32[256,512]{1,0:T(8,128)S(1)} %shard_map.63.mine_ref, f32[256,512]{1,0:T(8,128)S(1)} %collective-permute-done.14.other_ref, bf16[2,512,256]{2,1,0:T(8,128)(2,1)S(1)} %get-tuple-element.38.halves_ref, f32[512,256]{1,0:T(8,128)S(1)} %get-tuple-element.39.next_ref), custom_call_target="tpu_custom_call" | custom-call | flops 503316480 | bytes 3145728 | tf_op jit(solution)/shard_map/pallas_call | solution.py:164
  (14 shorter events, 0.3 us)
Async XLA Ops:
  0.6 5.5 %copy-start.2 = (f32[512,256]{1,0:T(8,128)S(1)}, f32[512,256]{1,0:T(8,128)}, u32[]{:S(2)}) copy-start(f32[512,256]{1,0:T(8,128)} %basis_ref.1) | copy-start | bytes 1572868
  3.1 8.8 %collective-permute-start = (f32[4,32,768]{2,1,0:T(8,128)S(1)}, f32[4,32,768]{2,1,0:T(8,128)S(1)}, u32[]{:S(2)}, u32[]{:S(2)}) collective-permute-start(f32[4,32,768]{2,1,0:T(8,128)S(1)} %get-tuple-element.22), channel_id=1, source_target_pairs={{0,2},{1,5},{2,0},{3,7},{4,6},{5,1},{6,4},{7,3},{8,10},{9,13},{10,... | collective-permute-start | bytes 1179656 | tf_op jit(solution)/shard_map/ppermute | solution.py:37
  7.0 10.7 %collective-permute-start.2 = (f32[4,32,768]{2,1,0:T(8,128)S(1)}, f32[4,32,768]{2,1,0:T(8,128)S(1)}, u32[]{:S(2)}, u32[]{:S(2)}) collective-permute-start(f32[4,32,768]{2,1,0:T(8,128)S(1)} %get-tuple-element.24), channel_id=1, source_target_pairs={{0,8},{1,9},{2,10},{3,11},{4,12},{5,13},{6,14},{7,15},{8,0},{9,1},... | collective-permute-start | bytes 1179656 | tf_op jit(solution)/shard_map/ppermute | solution.py:37
  11.9 7.3 %collective-permute-start.1 = (f32[2,32,768]{2,1,0:T(8,128)S(1)}, f32[2,32,768]{2,1,0:T(8,128)S(1)}, u32[]{:S(2)}, u32[]{:S(2)}) collective-permute-start(f32[2,32,768]{2,1,0:T(8,128)S(1)} %get-tuple-element.42), channel_id=1, source_target_pairs={{0,4},{1,3},{2,6},{3,1},{4,0},{5,7},{6,2},{7,5},{8,12},{9,11},{10,... | collective-permute-start | bytes 589832 | tf_op jit(solution)/shard_map/ppermute | solution.py:37
  17.7 5.7 %collective-permute-start.4 = (f32[2,32,768]{2,1,0:T(8,128)S(1)}, f32[2,32,768]{2,1,0:T(8,128)S(1)}, u32[]{:S(2)}, u32[]{:S(2)}) collective-permute-start(f32[2,32,768]{2,1,0:T(8,128)S(1)} %get-tuple-element.41), channel_id=1, source_target_pairs={{0,2},{1,5},{2,0},{3,7},{4,6},{5,1},{6,4},{7,3},{8,10},{9,13},{10,... | collective-permute-start | bytes 589832 | tf_op jit(solution)/shard_map/ppermute | solution.py:37
  19.3 4.7 %collective-permute-start.3 = (f32[1,32,768]{2,1,0:T(8,128)S(1)}, f32[1,32,768]{2,1,0:T(8,128)S(1)}, u32[]{:S(2)}, u32[]{:S(2)}) collective-permute-start(f32[1,32,768]{2,1,0:T(8,128)S(1)} %slice_add_fusion.6), channel_id=1, source_target_pairs={{0,8},{1,9},{2,10},{3,11},{4,12},{5,13},{6,14},{7,15},{8,0},{9,1},... | collective-permute-start | bytes 294920 | tf_op jit(solution)/shard_map/ppermute | solution.py:37
  23.5 4.7 %collective-permute-start.6 = (f32[1,32,768]{2,1,0:T(8,128)S(1)}, f32[1,32,768]{2,1,0:T(8,128)S(1)}, u32[]{:S(2)}, u32[]{:S(2)}) collective-permute-start(f32[1,32,768]{2,1,0:T(8,128)S(1)} %slice_add_fusion.5), channel_id=1, source_target_pairs={{0,4},{1,3},{2,6},{3,1},{4,0},{5,7},{6,2},{7,5},{8,12},{9,11},{10,... | collective-permute-start | bytes 294920 | tf_op jit(solution)/shard_map/ppermute | solution.py:37
  24.0 9.6 %collective-permute-start.5 = (f32[32,768]{1,0:T(8,128)S(1)}, f32[32,768]{1,0:T(8,128)S(1)}, u32[]{:S(2)}, u32[]{:S(2)}) collective-permute-start(f32[32,768]{1,0:T(8,128)S(1)} %bitcast.8), channel_id=1, source_target_pairs={{0,16},{2,18},{4,20},{6,22},{8,24},{10,26},{12,28},{14,30},{16,0},... | collective-permute-start | bytes 294920 | tf_op jit(solution)/shard_map/ppermute | solution.py:41
  28.2 7.8 %collective-permute-start.8 = (f32[32,768]{1,0:T(8,128)S(1)}, f32[32,768]{1,0:T(8,128)S(1)}, u32[]{:S(2)}, u32[]{:S(2)}) collective-permute-start(f32[32,768]{1,0:T(8,128)S(1)} %fusion.1), channel_id=1, source_target_pairs={{0,16},{2,18},{4,20},{6,22},{8,24},{10,26},{12,28},{14,30},{16,0},... | collective-permute-start | bytes 294920 | tf_op jit(solution)/shard_map/ppermute | solution.py:41
  36.0 5.6 %collective-permute-start.9 = (f32[1,32,1024]{2,1,0:T(8,128)S(1)}, f32[1,32,1024]{2,1,0:T(8,128)S(1)}, u32[]{:S(2)}, u32[]{:S(2)}) collective-permute-start(f32[1,32,1024]{2,1,0:T(8,128)S(1)} %maximum_bitcast_fusion.1), channel_id=1, source_target_pairs={{0,2},{1,5},{2,0},{3,7},{4,6},{5,1},{6,4},{7,3},{8,10},{9,13},{10,... | collective-permute-start | bytes 393224 | tf_op jit(solution)/shard_map/ppermute | solution.py:37
  36.5 5.7 %collective-permute-start.7 = (f32[1,2,32,768]{3,2,1,0:T(8,128)S(1)}, f32[1,2,32,768]{3,2,1,0:T(8,128)S(1)}, u32[]{:S(2)}, u32[]{:S(2)}) collective-permute-start(f32[1,2,32,768]{3,2,1,0:T(8,128)S(1)} %maximum_bitcast_fusion), channel_id=1, source_target_pairs={{0,4},{1,3},{2,6},{3,1},{4,0},{5,7},{6,2},{7,5},{8,12},{9,11},{10,... | collective-permute-start | bytes 589832 | tf_op jit(solution)/shard_map/ppermute | solution.py:37
  42.2 9.8 %collective-permute-start.10 = (f32[2,2,32,768]{3,2,1,0:T(8,128)S(1)}, f32[2,2,32,768]{3,2,1,0:T(8,128)S(1)}, u32[]{:S(2)}, u32[]{:S(2)}) collective-permute-start(f32[2,2,32,768]{3,2,1,0:T(8,128)S(1)} %pad_maximum_fusion.2), channel_id=1, source_target_pairs={{0,8},{1,9},{2,10},{3,11},{4,12},{5,13},{6,14},{7,15},{8,0},{9,1},... | collective-permute-start | bytes 1179656 | tf_op jit(solution)/shard_map/ppermute | solution.py:37
  42.9 6.4 %collective-permute-start.11 = (f32[2,32,1024]{2,1,0:T(8,128)S(1)}, f32[2,32,1024]{2,1,0:T(8,128)S(1)}, u32[]{:S(2)}, u32[]{:S(2)}) collective-permute-start(f32[2,32,1024]{2,1,0:T(8,128)S(1)} %pad_maximum_fusion.3), channel_id=1, source_target_pairs={{0,4},{1,3},{2,6},{3,1},{4,0},{5,7},{6,2},{7,5},{8,12},{9,11},{10,... | collective-permute-start | bytes 786440 | tf_op jit(solution)/shard_map/ppermute | solution.py:37
  52.0 12.2 %collective-permute-start.12 = (f32[4,2,32,768]{3,2,1,0:T(8,128)S(1)}, f32[4,2,32,768]{3,2,1,0:T(8,128)S(1)}, u32[]{:S(2)}, u32[]{:S(2)}) collective-permute-start(f32[4,2,32,768]{3,2,1,0:T(8,128)S(1)} %pad_maximum_fusion.first_ref), channel_id=1, source_target_pairs={{0,2},{1,5},{2,0},{3,7},{4,6},{5,1},{6,4},{7,3},{8,10},{9,13},{10,... | collective-permute-start | bytes 2359304 | tf_op jit(solution)/shard_map/ppermute | solution.py:37
  54.3 12.8 %collective-permute-start.13 = (f32[4,32,1024]{2,1,0:T(8,128)S(1)}, f32[4,32,1024]{2,1,0:T(8,128)S(1)}, u32[]{:S(2)}, u32[]{:S(2)}) collective-permute-start(f32[4,32,1024]{2,1,0:T(8,128)S(1)} %pad_maximum_fusion.1.first_ref), channel_id=1, source_target_pairs={{0,8},{1,9},{2,10},{3,11},{4,12},{5,13},{6,14},{7,15},{8,0},{9,1},... | collective-permute-start | bytes 1572872 | tf_op jit(solution)/shard_map/ppermute | solution.py:37
  66.3 1.5 %copy-start = (f32[512,512]{1,0:T(8,128)S(1)}, f32[512,512]{1,0:T(8,128)}, u32[]{:S(2)}) copy-start(f32[512,512]{1,0:T(8,128)} %z_ref.1) | copy-start | bytes 3145732
  66.3 1.5 %copy-start.1 = (f32[512,256]{1,0:T(8,128)S(1)}, f32[512,256]{1,0:T(8,128)}, u32[]{:S(2)}) copy-start(f32[512,256]{1,0:T(8,128)} %y_ref.1) | copy-start | bytes 1572868
  67.8 2.0 %collective-permute-start.14 = (f32[256,512]{1,0:T(8,128)S(1)}, f32[256,512]{1,0:T(8,128)S(1)}, u32[]{:S(2)}, u32[]{:S(2)}) collective-permute-start(f32[256,512]{1,0:T(8,128)S(1)} %shard_map.63.mine_ref), channel_id=1, source_target_pairs={{0,1},{1,0},{2,3},{3,2},{4,5},{5,4},{6,7},{7,6},{8,9},{9,8},{10,11... | collective-permute-start | bytes 1572872 | tf_op jit(solution)/shard_map/ppermute | solution.py:41

commit v8 on v7

--- a/solution.py
+++ b/solution.py
@@ -14,7 +14,7 @@
     pair, rest = [core, 1 - core], list(range(2, bits))
     if stage == "scatter":
         return pair + rest if chain == "low" else rest + pair
-    return [1 - core] + rest + [core] if chain == "low" else pair + rest
+    return {"own": pair + rest, "other": rest + pair[::-1], "high": rest + pair}[chain]
 
 
 def relative_bits(order, r, first_is_high):
@@ -112,24 +112,22 @@
 
 def place(parts, chain, bits, target):
     blocks = 1 << bits
-    rows = target.shape[-2] // blocks
+    rows = target.shape[0] // blocks
     for r in range(blocks):
         start = pl.multiple_of(block_of(r, chain, bits, "gather") * rows, rows)
-        piece = parts[r // (blocks // 2)][r % (blocks // 2)]
-        if len(target.shape) == 3:
-            target[:, pl.ds(start, rows), :] = piece
-        else:
-            target[pl.ds(start, rows), :] = piece
-
-
-def solve_kernel(bits, first_ref, second_ref, update_ref, terms):
+        target[pl.ds(start, rows), :] = parts[r // (blocks // 2)][r % (blocks // 2)]
+
+
+def solve_kernel(bits, own_low, own_high, other_low, other_high, update_ref, own, other):
     rank = update_ref.shape[1]
-    place((first_ref, second_ref), "low", bits, terms)
-    couples = [split(terms[i, :, :rank]) for i in range(2)]
+    place((own_low, own_high), "own", bits, own)
+    place((other_low, other_high), "other", bits, other)
+    terms = (own, other)
+    couples = [split(x[:, :rank]) for x in terms]
     for i in range(2):
-        mine, other = couples[i], couples[1 - i]
-        start = terms[1 - i, :, rank:] - dot3(other, split(terms[i, :, rank:]))
-        update_ref[i] = start + dot3(other, split(dot3(mine, split(start))))
+        mine, far = couples[i], couples[1 - i]
+        start = terms[1 - i][:, rank:] - dot3(far, split(terms[i][:, rank:]))
+        update_ref[i] = start + dot3(far, split(dot3(mine, split(start))))
 
 
 def total_kernel(bits, first_ref, second_ref, update_ref, total_ref, terms):
@@ -214,45 +212,45 @@
         flops=3 * unit * depth,
     )
 
-    def rounds(chain, send, keep):
-        for t in range(bits):
-            got = yield send, functools.partial(step, chain=chain, t=t, bits=bits, stage="scatter")
-            half = keep.shape[0] // 2
-            if t < bits - 1:
-                send = keep[half:] + got[half:]
-                keep = keep[:half] + got[:half]
-        mine = keep[0] + got[0]
-        other = yield mine, functools.partial(flip, axis="leaf", bit=bits)
-        if chain == "low":
-            grown = jnp.stack([mine, other])[None]
-        else:
-            both = [mine[:, :rank], other[:, :rank], mine[:, rank:] + other[:, rank:]]
-            grown = jnp.concatenate(both, axis=1)[None]
-        for t in range(bits):
-            got = yield grown, functools.partial(step, chain=chain, t=t, bits=bits, stage="gather")
-            if t < bits - 1:
-                grown = jnp.concatenate([grown, got], axis=0)
-        yield (grown, got), None
-
-    low, high = rounds("low", low_send, low_keep), rounds("high", high_send, high_keep)
-    (low_out, low_move), (high_out, high_move) = next(low), next(high)
-    for t in range(2 * bits + 1):
-        low_got, high_got = low_move(low_out), high_move(high_out)
-        if bits < t < 2 * bits:
-            high_out, high_move = high.send(high_got)
-            low_out, low_move = low.send(after(low_got, high_out))
-        else:
-            low_out, low_move = low.send(after(low_got, high_out))
-            if low_move is not None:
-                high_got = after(high_got, low_out)
-            high_out, high_move = high.send(high_got)
-    low_parts, high_parts = low_out, high_out
+    def merge(keep, got):
+        half = keep.shape[0] // 2
+        if half == 0:
+            return keep[0] + got[0], None
+        return keep[half:] + got[half:], keep[:half] + got[:half]
+
+    def grow(x, got):
+        return jnp.concatenate([x, got], axis=0)
+
+    for t in range(bits):
+        low_got = step(low_send, "low", t, bits, "scatter")
+        high_got = step(high_send, "high", t, bits, "scatter")
+        low_send, low_keep = merge(low_keep, after(low_got, high_send))
+        high_send, high_keep = merge(high_keep, after(high_got, low_send))
+    low_mine, high_mine = low_send, high_send
+    low_other, high_other = flip(low_mine, "leaf", bits), flip(high_mine, "leaf", bits)
+
+    other, own = after(low_other, high_mine)[None], low_mine[None]
+    own = grow(own, after(step(own, "own", 0, bits, "gather"), other))
+    high_other = after(high_other, own)
+    both = [high_mine[:, :rank], high_other[:, :rank], high_mine[:, rank:] + high_other[:, rank:]]
+    high = jnp.concatenate(both, axis=1)[None]
+    for t in range(bits - 1):
+        other_got = step(other, "other", t, bits, "gather")
+        own_got = step(own, "own", t + 1, bits, "gather")
+        high_got = step(high, "high", t, bits, "gather")
+        other = grow(other, after(other_got, high))
+        own_got = after(own_got, other)
+        if t < bits - 2:
+            own = grow(own, own_got)
+        high = grow(high, after(high_got, own_got))
+    low_parts = [own, own_got, other, step(other, "other", bits - 1, bits, "gather")]
+    high_parts = [high, step(high, "high", bits - 1, bits, "gather")]
 
     (update,) = run(
         functools.partial(solve_kernel, bits),
         [array(2, rank, 2 * rank)],
         low_parts,
-        [pltpu.VMEM((2, rank, 3 * rank), jnp.float32)],
+        [pltpu.VMEM((rank, 3 * rank), jnp.float32)] * 2,
         flops=12 * unit * rank,
     )
     (total,) = run(

time: 72.1 us -> 68.1 us (0.945)
  waiting for transfers between devices: 38.9 us -> 31.4 us
  starting transfers between devices: 22.3 us -> 25.2 us
    ppermute x12 -> x15, waiting for transfers between devices: 33.3 us -> 27.5 us  [step(): return lax.ppermute(x, AXES, pairs)]
    ppermute x12 -> x15, starting transfers between devices: 16.8 us -> 20.2 us  [step(): return lax.ppermute(x, AXES, pairs)]
    ppermute x3, waiting for transfers between devices: 5.63 us -> 3.84 us  [flip(): lax.ppermute(x, axis, [(i, i ^ 1 << bit) for i in range(lax.axis_size(axi...]
  transfers between devices with their start and end apart: 15 -> 18, of which waited for: 14 -> 12; matrix products, arithmetic and copies ran while one was open for 0% -> 0% of each run, Pallas kernels for 6% -> 6%
where the time goes in v8:
time: 68.1 us; the launch traced here: 68 us
  waiting for transfers between devices  31.4 us (46%)
  starting transfers between devices  25.2 us (37%)
  Pallas kernels  9.67 us (14%)
  between operations  0.8 us (1%)
    ppermute x15, waiting for transfers between devices, step(): return lax.ppermute(x, AXES, pairs)  27.5 us
    ppermute x15, starting transfers between devices, step(): return lax.ppermute(x, AXES, pairs)  20.2 us
    pallas_call x6, Pallas kernels, run(): pl.pallas_call(kernel, out_shape=shapes, in_specs=[pl.BlockSpec(memory_sp...  9.67 us
    ppermute x3, starting transfers between devices, flip(): lax.ppermute(x, axis, [(i, i ^ 1 << bit) for i in range(lax.axis_size(axi...  4.98 us
    ppermute x3, waiting for transfers between devices, flip(): lax.ppermute(x, axis, [(i, i ^ 1 << bit) for i in range(lax.axis_size(axi...  3.84 us
  transfers between devices with their start and end apart: 18, of which 12 were waited for; matrix products, arithmetic and copies ran while one was open for 0% of the time, Pallas kernels for 6%

profile of v8, /device:TPU:0, one launch (start us, length us, event | category | flops | bytes accessed | tf_op | source)
XLA Modules:
  0.0 68.0 jit_solution(6627991437491322706)
XLA Ops:
  0.6 0.0 copy-start.2
  0.6 2.4 %shard_map.59 = (f32[4,32,768]{2,1,0:T(8,128)S(1)}, f32[4,32,768]{2,1,0:T(8,128)S(1)}, bf16[2,512,768]{2,1,0:T(8,128)(2,1)S(1)}) custom-call(f32[512,256]{1,0:T(8,128)} %y_ref.1, f32[512,512]{1,0:T(8,128)} %z_ref.1, f32[512,256]{1,0:T(8,128)} %refs_2_.1), custom_call_target="tpu_custom_call" | custom-call | flops 603979776 | bytes 6029312 | tf_op jit(solution)/shard_map/pallas_call | solution.py:162
  3.1 3.0 %collective-permute-start = (f32[4,32,768]{2,1,0:T(8,128)S(1)}, f32[4,32,768]{2,1,0:T(8,128)S(1)}, u32[]{:S(2)}, u32[]{:S(2)}) collective-permute-start(f32[4,32,768]{2,1,0:T(8,128)S(1)} %get-tuple-element.26), channel_id=1, source_target_pairs={{0,2},{1,5},{2,0},{3,7},{4,6},{5,1},{6,4},{7,3},{8,10},{9,13},{10,... | collective-permute-start | bytes 1179656 | tf_op jit(solution)/shard_map/ppermute | solution.py:37
  6.1 0.0 copy-done.2
  6.1 0.9 %shard_map.60 = (f32[4,32,768]{2,1,0:T(8,128)S(1)}, f32[4,32,768]{2,1,0:T(8,128)S(1)}) custom-call(f32[512,256]{1,0:T(8,128)S(1)} %copy-done.2, bf16[2,512,768]{2,1,0:T(8,128)(2,1)S(1)} %get-tuple-element.27.joined), custom_call_target="tpu_custom_call" | custom-call | flops 603979776 | bytes 4456448 | tf_op jit(solution)/shard_map/pallas_call | solution.py:162
  7.0 1.6 %collective-permute-start.2 = (f32[4,32,768]{2,1,0:T(8,128)S(1)}, f32[4,32,768]{2,1,0:T(8,128)S(1)}, u32[]{:S(2)}, u32[]{:S(2)}) collective-permute-start(f32[4,32,768]{2,1,0:T(8,128)S(1)} %get-tuple-element.28), channel_id=1, source_target_pairs={{0,8},{1,9},{2,10},{3,11},{4,12},{5,13},{6,14},{7,15},{8,0},{9,1},... | collective-permute-start | bytes 1179656 | tf_op jit(solution)/shard_map/ppermute | solution.py:37
  8.6 3.2 %collective-permute-done = f32[4,32,768]{2,1,0:T(8,128)S(1)} collective-permute-done((f32[4,32,768]{2,1,0:T(8,128)S(1)}, f32[4,32,768]{2,1,0:T(8,128)S(1)}, u32[]{:S(2)}, u32[]{:S(2)}) %collective-permute-start) | collective-permute-done | bytes 393248 | tf_op jit(solution)/shard_map/ppermute | solution.py:37
  11.9 2.1 %collective-permute-start.1 = (f32[2,32,768]{2,1,0:T(8,128)S(1)}, f32[2,32,768]{2,1,0:T(8,128)S(1)}, u32[]{:S(2)}, u32[]{:S(2)}) collective-permute-start(f32[2,32,768]{2,1,0:T(8,128)S(1)} %get-tuple-element.50), channel_id=1, source_target_pairs={{0,4},{1,3},{2,6},{3,1},{4,0},{5,7},{6,2},{7,5},{8,12},{9,11},{10,... | collective-permute-start | bytes 589832 | tf_op jit(solution)/shard_map/ppermute | solution.py:37
  14.0 3.6 %collective-permute-done.2 = f32[4,32,768]{2,1,0:T(8,128)S(1)} collective-permute-done((f32[4,32,768]{2,1,0:T(8,128)S(1)}, f32[4,32,768]{2,1,0:T(8,128)S(1)}, u32[]{:S(2)}, u32[]{:S(2)}) %collective-permute-start.2) | collective-permute-done | bytes 393248 | tf_op jit(solution)/shard_map/ppermute | solution.py:37
  17.7 1.5 %collective-permute-start.4 = (f32[2,32,768]{2,1,0:T(8,128)S(1)}, f32[2,32,768]{2,1,0:T(8,128)S(1)}, u32[]{:S(2)}, u32[]{:S(2)}) collective-permute-start(f32[2,32,768]{2,1,0:T(8,128)S(1)} %get-tuple-element.49), channel_id=1, source_target_pairs={{0,2},{1,5},{2,0},{3,7},{4,6},{5,1},{6,4},{7,3},{8,10},{9,13},{10,... | collective-permute-start | bytes 589832 | tf_op jit(solution)/shard_map/ppermute | solution.py:37
  19.2 0.0 collective-permute-done.1
  19.3 1.7 %collective-permute-start.3 = (f32[1,32,768]{2,1,0:T(8,128)S(1)}, f32[1,32,768]{2,1,0:T(8,128)S(1)}, u32[]{:S(2)}, u32[]{:S(2)}) collective-permute-start(f32[1,32,768]{2,1,0:T(8,128)S(1)} %slice_add_fusion.6), channel_id=1, source_target_pairs={{0,8},{1,9},{2,10},{3,11},{4,12},{5,13},{6,14},{7,15},{8,0},{9,1},... | collective-permute-start | bytes 294920 | tf_op jit(solution)/shard_map/ppermute | solution.py:37
  20.9 2.5 %collective-permute-done.4 = f32[2,32,768]{2,1,0:T(8,128)S(1)} collective-permute-done((f32[2,32,768]{2,1,0:T(8,128)S(1)}, f32[2,32,768]{2,1,0:T(8,128)S(1)}, u32[]{:S(2)}, u32[]{:S(2)}) %collective-permute-start.4) | collective-permute-done | bytes 196640 | tf_op jit(solution)/shard_map/ppermute | solution.py:37
  23.5 0.4 collective-permute-start.7
  23.9 0.1 collective-permute-done.3
  24.0 1.6 %collective-permute-start.5 = (f32[1,32,768]{2,1,0:T(8,128)S(1)}, f32[1,32,768]{2,1,0:T(8,128)S(1)}, u32[]{:S(2)}, u32[]{:S(2)}) collective-permute-start(f32[1,32,768]{2,1,0:T(8,128)S(1)} %fusion.2), channel_id=1, source_target_pairs={{0,2},{1,5},{2,0},{3,7},{4,6},{5,1},{6,4},{7,3},{8,10},{9,13},{10,... | collective-permute-start | bytes 294920 | tf_op jit(solution)/shard_map/ppermute | solution.py:37
  25.6 2.6 %collective-permute-start.6 = (f32[32,768]{1,0:T(8,128)S(1)}, f32[32,768]{1,0:T(8,128)S(1)}, u32[]{:S(2)}, u32[]{:S(2)}) collective-permute-start(f32[32,768]{1,0:T(8,128)S(1)} %bitcast.6), channel_id=1, source_target_pairs={{0,16},{2,18},{4,20},{6,22},{8,24},{10,26},{12,28},{14,30},{16,0},... | collective-permute-start | bytes 294920 | tf_op jit(solution)/shard_map/ppermute | solution.py:41
  28.2 0.6 collective-permute-done.7
  28.8 2.3 %collective-permute-start.10 = (f32[32,768]{1,0:T(8,128)S(1)}, f32[32,768]{1,0:T(8,128)S(1)}, u32[]{:S(2)}, u32[]{:S(2)}) collective-permute-start(f32[32,768]{1,0:T(8,128)S(1)} %fusion.1), channel_id=1, source_target_pairs={{0,16},{2,18},{4,20},{6,22},{8,24},{10,26},{12,28},{14,30},{16,0},... | collective-permute-start | bytes 294920 | tf_op jit(solution)/shard_map/ppermute | solution.py:41
  31.1 2.9 %collective-permute-done.6 = f32[32,768]{1,0:T(8,128)S(1)} collective-permute-done((f32[32,768]{1,0:T(8,128)S(1)}, f32[32,768]{1,0:T(8,128)S(1)}, u32[]{:S(2)}, u32[]{:S(2)}) %collective-permute-start.6) | collective-permute-done | bytes 98336 | tf_op jit(solution)/shard_map/ppermute | solution.py:41
  34.1 1.1 %collective-permute-start.9 = (f32[1,32,768]{2,1,0:T(8,128)S(1)}, f32[1,32,768]{2,1,0:T(8,128)S(1)}, u32[]{:S(2)}, u32[]{:S(2)}) collective-permute-start(f32[1,32,768]{2,1,0:T(8,128)S(1)} %bitcast.7), channel_id=1, source_target_pairs={{0,8},{1,9},{2,10},{3,11},{4,12},{5,13},{6,14},{7,15},{8,0},{9,1},... | collective-permute-start | bytes 294920 | tf_op jit(solution)/shard_map/ppermute | solution.py:37
  35.2 0.0 collective-permute-done.5
  35.2 0.9 %collective-permute-done.10 = f32[32,768]{1,0:T(8,128)S(1)} collective-permute-done((f32[32,768]{1,0:T(8,128)S(1)}, f32[32,768]{1,0:T(8,128)S(1)}, u32[]{:S(2)}, u32[]{:S(2)}) %collective-permute-start.10) | collective-permute-done | bytes 98336 | tf_op jit(solution)/shard_map/ppermute | solution.py:41
  36.1 1.7 %collective-permute-start.8 = (f32[2,32,768]{2,1,0:T(8,128)S(1)}, f32[2,32,768]{2,1,0:T(8,128)S(1)}, u32[]{:S(2)}, u32[]{:S(2)}) collective-permute-start(f32[2,32,768]{2,1,0:T(8,128)S(1)} %pad_maximum_fusion.4), channel_id=1, source_target_pairs={{0,4},{1,3},{2,6},{3,1},{4,0},{5,7},{6,2},{7,5},{8,12},{9,11},{10,... | collective-permute-start | bytes 589832 | tf_op jit(solution)/shard_map/ppermute | solution.py:37
  37.8 1.1 %collective-permute-start.13 = (f32[1,32,1024]{2,1,0:T(8,128)S(1)}, f32[1,32,1024]{2,1,0:T(8,128)S(1)}, u32[]{:S(2)}, u32[]{:S(2)}) collective-permute-start(f32[1,32,1024]{2,1,0:T(8,128)S(1)} %maximum_bitcast_fusion), channel_id=1, source_target_pairs={{0,8},{1,9},{2,10},{3,11},{4,12},{5,13},{6,14},{7,15},{8,0},{9,1},... | collective-permute-start | bytes 393224 | tf_op jit(solution)/shard_map/ppermute | solution.py:37
  38.9 0.6 collective-permute-done.9
  39.5 2.3 %collective-permute-done.8 = f32[2,32,768]{2,1,0:T(8,128)S(1)} collective-permute-done((f32[2,32,768]{2,1,0:T(8,128)S(1)}, f32[2,32,768]{2,1,0:T(8,128)S(1)}, u32[]{:S(2)}, u32[]{:S(2)}) %collective-permute-start.8) | collective-permute-done | bytes 196640 | tf_op jit(solution)/shard_map/ppermute | solution.py:37
  41.9 0.7 collective-permute-start.11
  42.6 2.0 %collective-permute-start.12 = (f32[2,32,768]{2,1,0:T(8,128)S(1)}, f32[2,32,768]{2,1,0:T(8,128)S(1)}, u32[]{:S(2)}, u32[]{:S(2)}) collective-permute-start(f32[2,32,768]{2,1,0:T(8,128)S(1)} %pad_maximum_fusion.5), channel_id=1, source_target_pairs={{0,4},{1,3},{2,6},{3,1},{4,0},{5,7},{6,2},{7,5},{8,12},{9,11},{10,... | collective-permute-start | bytes 589832 | tf_op jit(solution)/shard_map/ppermute | solution.py:37
  44.6 0.0 collective-permute-done.13
  44.6 0.1 collective-permute-start.15
  44.7 4.1 %collective-permute-done.12 = f32[2,32,768]{2,1,0:T(8,128)S(1)} collective-permute-done((f32[2,32,768]{2,1,0:T(8,128)S(1)}, f32[2,32,768]{2,1,0:T(8,128)S(1)}, u32[]{:S(2)}, u32[]{:S(2)}) %collective-permute-start.12) | collective-permute-done | bytes 196640 | tf_op jit(solution)/shard_map/ppermute | solution.py:37
  48.8 2.3 %collective-permute-done.11.own_high = f32[4,32,768]{2,1,0:T(8,128)S(1)} collective-permute-done((f32[4,32,768]{2,1,0:T(8,128)S(1)}, f32[4,32,768]{2,1,0:T(8,128)S(1)}, u32[]{:S(2)}, u32[]{:S(2)}) %collective-permute-start.11) | collective-permute-done | bytes 393248 | tf_op jit(solution)/shard_map/ppermute | solution.py:37
  51.1 0.0 collective-permute-done.15
  51.2 1.6 %collective-permute-start.16 = (f32[4,32,1024]{2,1,0:T(8,128)S(1)}, f32[4,32,1024]{2,1,0:T(8,128)S(1)}, u32[]{:S(2)}, u32[]{:S(2)}) collective-permute-start(f32[4,32,1024]{2,1,0:T(8,128)S(1)} %pad_maximum_fusion.first_ref), channel_id=1, source_target_pairs={{0,4},{1,3},{2,6},{3,1},{4,0},{5,7},{6,2},{7,5},{8,12},{9,11},{10,... | collective-permute-start | bytes 1572872 | tf_op jit(solution)/shard_map/ppermute | solution.py:37
  52.7 0.0 collective-permute-start.14
  52.7 8.2 %collective-permute-done.14.other_high = f32[4,32,768]{2,1,0:T(8,128)S(1)} collective-permute-done((f32[4,32,768]{2,1,0:T(8,128)S(1)}, f32[4,32,768]{2,1,0:T(8,128)S(1)}, u32[]{:S(2)}, u32[]{:S(2)}) %collective-permute-start.14) | collective-permute-done | bytes 393248 | tf_op jit(solution)/shard_map/ppermute | solution.py:37
  60.9 2.1 %shard_map.61.update_ref = f32[2,256,512]{2,1,0:T(8,128)S(1)} custom-call(f32[4,32,768]{2,1,0:T(8,128)S(1)} %pad_maximum_fusion.1.own_low, f32[4,32,768]{2,1,0:T(8,128)S(1)} %collective-permute-done.11.own_high, f32[4,32,768]{2,1,0:T(8,128)S(1)} %pad_maximum_fusion.2.other_low, f32[4,32,768]{2,1,0:T(8,128)S(1)} %collective-permute-done.14.other_high), custom_call_target="tpu_custom_call" | custom-call | flops 1207959552 | bytes 2621440 | tf_op jit(solution)/shard_map/pallas_call | solution.py:162
  63.0 0.0 copy-start
  63.0 0.0 copy-start.1
  63.0 0.0 collective-permute-done.16.second_ref
  63.0 0.7 shard_map.63.mine_ref
  63.7 0.1 collective-permute-start.17
  63.8 0.4 copy-done
  64.2 0.1 copy-done.1
  64.3 1.4 %shard_map.62 = (f32[512,256]{1,0:T(8,128)}, bf16[2,512,256]{2,1,0:T(8,128)(2,1)S(1)}, f32[512,256]{1,0:T(8,128)S(1)}) custom-call(f32[512,256]{1,0:T(8,128)S(1)} %copy-done.1, f32[512,512]{1,0:T(8,128)S(1)} %copy-done, f32[2,256,512]{2,1,0:T(8,128)S(1)} %shard_map.61.update_ref), custom_call_target="tpu_custom_call" | custom-call | flops 402653184 | bytes 4718592 | tf_op jit(solution)/shard_map/pallas_call | solution.py:162
  65.7 0.0 collective-permute-done.17.other_ref
  65.7 2.2 %shard_map.64 = f32[512,256]{1,0:T(8,128)} custom-call(f32[256,512]{1,0:T(8,128)S(1)} %shard_map.63.mine_ref, f32[256,512]{1,0:T(8,128)S(1)} %collective-permute-done.17.other_ref, bf16[2,512,256]{2,1,0:T(8,128)(2,1)S(1)} %get-tuple-element.46.halves_ref, f32[512,256]{1,0:T(8,128)S(1)} %get-tuple-element.47.next_ref), custom_call_target="tpu_custom_call" | custom-call | flops 503316480 | bytes 3145728 | tf_op jit(solution)/shard_map/pallas_call | solution.py:162
  (16 shorter events, 0.3 us)
Async XLA Ops:
  0.6 5.5 %copy-start.2 = (f32[512,256]{1,0:T(8,128)S(1)}, f32[512,256]{1,0:T(8,128)}, u32[]{:S(2)}) copy-start(f32[512,256]{1,0:T(8,128)} %basis_ref.1) | copy-start | bytes 1572868
  3.1 8.8 %collective-permute-start = (f32[4,32,768]{2,1,0:T(8,128)S(1)}, f32[4,32,768]{2,1,0:T(8,128)S(1)}, u32[]{:S(2)}, u32[]{:S(2)}) collective-permute-start(f32[4,32,768]{2,1,0:T(8,128)S(1)} %get-tuple-element.26), channel_id=1, source_target_pairs={{0,2},{1,5},{2,0},{3,7},{4,6},{5,1},{6,4},{7,3},{8,10},{9,13},{10,... | collective-permute-start | bytes 1179656 | tf_op jit(solution)/shard_map/ppermute | solution.py:37
  7.0 10.7 %collective-permute-start.2 = (f32[4,32,768]{2,1,0:T(8,128)S(1)}, f32[4,32,768]{2,1,0:T(8,128)S(1)}, u32[]{:S(2)}, u32[]{:S(2)}) collective-permute-start(f32[4,32,768]{2,1,0:T(8,128)S(1)} %get-tuple-element.28), channel_id=1, source_target_pairs={{0,8},{1,9},{2,10},{3,11},{4,12},{5,13},{6,14},{7,15},{8,0},{9,1},... | collective-permute-start | bytes 1179656 | tf_op jit(solution)/shard_map/ppermute | solution.py:37
  11.9 7.3 %collective-permute-start.1 = (f32[2,32,768]{2,1,0:T(8,128)S(1)}, f32[2,32,768]{2,1,0:T(8,128)S(1)}, u32[]{:S(2)}, u32[]{:S(2)}) collective-permute-start(f32[2,32,768]{2,1,0:T(8,128)S(1)} %get-tuple-element.50), channel_id=1, source_target_pairs={{0,4},{1,3},{2,6},{3,1},{4,0},{5,7},{6,2},{7,5},{8,12},{9,11},{10,... | collective-permute-start | bytes 589832 | tf_op jit(solution)/shard_map/ppermute | solution.py:37
  17.7 5.7 %collective-permute-start.4 = (f32[2,32,768]{2,1,0:T(8,128)S(1)}, f32[2,32,768]{2,1,0:T(8,128)S(1)}, u32[]{:S(2)}, u32[]{:S(2)}) collective-permute-start(f32[2,32,768]{2,1,0:T(8,128)S(1)} %get-tuple-element.49), channel_id=1, source_target_pairs={{0,2},{1,5},{2,0},{3,7},{4,6},{5,1},{6,4},{7,3},{8,10},{9,13},{10,... | collective-permute-start | bytes 589832 | tf_op jit(solution)/shard_map/ppermute | solution.py:37
  19.3 4.7 %collective-permute-start.3 = (f32[1,32,768]{2,1,0:T(8,128)S(1)}, f32[1,32,768]{2,1,0:T(8,128)S(1)}, u32[]{:S(2)}, u32[]{:S(2)}) collective-permute-start(f32[1,32,768]{2,1,0:T(8,128)S(1)} %slice_add_fusion.6), channel_id=1, source_target_pairs={{0,8},{1,9},{2,10},{3,11},{4,12},{5,13},{6,14},{7,15},{8,0},{9,1},... | collective-permute-start | bytes 294920 | tf_op jit(solution)/shard_map/ppermute | solution.py:37
  23.5 5.3 %collective-permute-start.7 = (f32[1,32,768]{2,1,0:T(8,128)S(1)}, f32[1,32,768]{2,1,0:T(8,128)S(1)}, u32[]{:S(2)}, u32[]{:S(2)}) collective-permute-start(f32[1,32,768]{2,1,0:T(8,128)S(1)} %slice_add_fusion.5), channel_id=1, source_target_pairs={{0,4},{1,3},{2,6},{3,1},{4,0},{5,7},{6,2},{7,5},{8,12},{9,11},{10,... | collective-permute-start | bytes 294920 | tf_op jit(solution)/shard_map/ppermute | solution.py:37
  24.0 11.2 %collective-permute-start.5 = (f32[1,32,768]{2,1,0:T(8,128)S(1)}, f32[1,32,768]{2,1,0:T(8,128)S(1)}, u32[]{:S(2)}, u32[]{:S(2)}) collective-permute-start(f32[1,32,768]{2,1,0:T(8,128)S(1)} %fusion.2), channel_id=1, source_target_pairs={{0,2},{1,5},{2,0},{3,7},{4,6},{5,1},{6,4},{7,3},{8,10},{9,13},{10,... | collective-permute-start | bytes 294920 | tf_op jit(solution)/shard_map/ppermute | solution.py:37
  25.6 8.5 %collective-permute-start.6 = (f32[32,768]{1,0:T(8,128)S(1)}, f32[32,768]{1,0:T(8,128)S(1)}, u32[]{:S(2)}, u32[]{:S(2)}) collective-permute-start(f32[32,768]{1,0:T(8,128)S(1)} %bitcast.6), channel_id=1, source_target_pairs={{0,16},{2,18},{4,20},{6,22},{8,24},{10,26},{12,28},{14,30},{16,0},... | collective-permute-start | bytes 294920 | tf_op jit(solution)/shard_map/ppermute | solution.py:41
  28.8 7.3 %collective-permute-start.10 = (f32[32,768]{1,0:T(8,128)S(1)}, f32[32,768]{1,0:T(8,128)S(1)}, u32[]{:S(2)}, u32[]{:S(2)}) collective-permute-start(f32[32,768]{1,0:T(8,128)S(1)} %fusion.1), channel_id=1, source_target_pairs={{0,16},{2,18},{4,20},{6,22},{8,24},{10,26},{12,28},{14,30},{16,0},... | collective-permute-start | bytes 294920 | tf_op jit(solution)/shard_map/ppermute | solution.py:41
  34.1 5.5 %collective-permute-start.9 = (f32[1,32,768]{2,1,0:T(8,128)S(1)}, f32[1,32,768]{2,1,0:T(8,128)S(1)}, u32[]{:S(2)}, u32[]{:S(2)}) collective-permute-start(f32[1,32,768]{2,1,0:T(8,128)S(1)} %bitcast.7), channel_id=1, source_target_pairs={{0,8},{1,9},{2,10},{3,11},{4,12},{5,13},{6,14},{7,15},{8,0},{9,1},... | collective-permute-start | bytes 294920 | tf_op jit(solution)/shard_map/ppermute | solution.py:37
  36.1 5.7 %collective-permute-start.8 = (f32[2,32,768]{2,1,0:T(8,128)S(1)}, f32[2,32,768]{2,1,0:T(8,128)S(1)}, u32[]{:S(2)}, u32[]{:S(2)}) collective-permute-start(f32[2,32,768]{2,1,0:T(8,128)S(1)} %pad_maximum_fusion.4), channel_id=1, source_target_pairs={{0,4},{1,3},{2,6},{3,1},{4,0},{5,7},{6,2},{7,5},{8,12},{9,11},{10,... | collective-permute-start | bytes 589832 | tf_op jit(solution)/shard_map/ppermute | solution.py:37
  37.8 6.8 %collective-permute-start.13 = (f32[1,32,1024]{2,1,0:T(8,128)S(1)}, f32[1,32,1024]{2,1,0:T(8,128)S(1)}, u32[]{:S(2)}, u32[]{:S(2)}) collective-permute-start(f32[1,32,1024]{2,1,0:T(8,128)S(1)} %maximum_bitcast_fusion), channel_id=1, source_target_pairs={{0,8},{1,9},{2,10},{3,11},{4,12},{5,13},{6,14},{7,15},{8,0},{9,1},... | collective-permute-start | bytes 393224 | tf_op jit(solution)/shard_map/ppermute | solution.py:37
  41.9 9.2 %collective-permute-start.11 = (f32[4,32,768]{2,1,0:T(8,128)S(1)}, f32[4,32,768]{2,1,0:T(8,128)S(1)}, u32[]{:S(2)}, u32[]{:S(2)}) collective-permute-start(f32[4,32,768]{2,1,0:T(8,128)S(1)} %pad_maximum_fusion.1.own_low), channel_id=1, source_target_pairs={{0,8},{1,9},{2,10},{3,11},{4,12},{5,13},{6,14},{7,15},{8,0},{9,1},... | collective-permute-start | bytes 1179656 | tf_op jit(solution)/shard_map/ppermute | solution.py:37
  42.6 6.2 %collective-permute-start.12 = (f32[2,32,768]{2,1,0:T(8,128)S(1)}, f32[2,32,768]{2,1,0:T(8,128)S(1)}, u32[]{:S(2)}, u32[]{:S(2)}) collective-permute-start(f32[2,32,768]{2,1,0:T(8,128)S(1)} %pad_maximum_fusion.5), channel_id=1, source_target_pairs={{0,4},{1,3},{2,6},{3,1},{4,0},{5,7},{6,2},{7,5},{8,12},{9,11},{10,... | collective-permute-start | bytes 589832 | tf_op jit(solution)/shard_map/ppermute | solution.py:37
  44.6 6.5 %collective-permute-start.15 = (f32[2,32,1024]{2,1,0:T(8,128)S(1)}, f32[2,32,1024]{2,1,0:T(8,128)S(1)}, u32[]{:S(2)}, u32[]{:S(2)}) collective-permute-start(f32[2,32,1024]{2,1,0:T(8,128)S(1)} %pad_maximum_fusion.3), channel_id=1, source_target_pairs={{0,2},{1,5},{2,0},{3,7},{4,6},{5,1},{6,4},{7,3},{8,10},{9,13},{10,... | collective-permute-start | bytes 786440 | tf_op jit(solution)/shard_map/ppermute | solution.py:37
  51.2 11.8 %collective-permute-start.16 = (f32[4,32,1024]{2,1,0:T(8,128)S(1)}, f32[4,32,1024]{2,1,0:T(8,128)S(1)}, u32[]{:S(2)}, u32[]{:S(2)}) collective-permute-start(f32[4,32,1024]{2,1,0:T(8,128)S(1)} %pad_maximum_fusion.first_ref), channel_id=1, source_target_pairs={{0,4},{1,3},{2,6},{3,1},{4,0},{5,7},{6,2},{7,5},{8,12},{9,11},{10,... | collective-permute-start | bytes 1572872 | tf_op jit(solution)/shard_map/ppermute | solution.py:37
  52.7 8.2 %collective-permute-start.14 = (f32[4,32,768]{2,1,0:T(8,128)S(1)}, f32[4,32,768]{2,1,0:T(8,128)S(1)}, u32[]{:S(2)}, u32[]{:S(2)}) collective-permute-start(f32[4,32,768]{2,1,0:T(8,128)S(1)} %pad_maximum_fusion.2.other_low), channel_id=1, source_target_pairs={{0,2},{1,5},{2,0},{3,7},{4,6},{5,1},{6,4},{7,3},{8,10},{9,13},{10,... | collective-permute-start | bytes 1179656 | tf_op jit(solution)/shard_map/ppermute | solution.py:37
  63.0 1.2 %copy-start = (f32[512,512]{1,0:T(8,128)S(1)}, f32[512,512]{1,0:T(8,128)}, u32[]{:S(2)}) copy-start(f32[512,512]{1,0:T(8,128)} %z_ref.1) | copy-start | bytes 3145732
  63.0 1.3 %copy-start.1 = (f32[512,256]{1,0:T(8,128)S(1)}, f32[512,256]{1,0:T(8,128)}, u32[]{:S(2)}) copy-start(f32[512,256]{1,0:T(8,128)} %y_ref.1) | copy-start | bytes 1572868
  63.7 2.0 %collective-permute-start.17 = (f32[256,512]{1,0:T(8,128)S(1)}, f32[256,512]{1,0:T(8,128)S(1)}, u32[]{:S(2)}, u32[]{:S(2)}) collective-permute-start(f32[256,512]{1,0:T(8,128)S(1)} %shard_map.63.mine_ref), channel_id=1, source_target_pairs={{0,1},{1,0},{2,3},{3,2},{4,5},{5,4},{6,7},{7,6},{8,9},{9,8},{10,11... | collective-permute-start | bytes 1572872 | tf_op jit(solution)/shard_map/ppermute | solution.py:41

commit v9 on v8

--- a/solution.py
+++ b/solution.py
@@ -34,7 +34,8 @@
         for group in range(groups):
             bit = axis_order(chain, group % 2, bits, stage)[t]
             pairs.append((leaf * groups + group, (leaf ^ (1 << bit)) * groups + group))
-    return lax.ppermute(x, AXES, pairs)
+    with jax.named_scope(f"{chain}_{stage}_{t}"):
+        return lax.ppermute(x, AXES, pairs)
 
 
 def flip(x, axis, bit):
@@ -227,9 +228,12 @@
         low_send, low_keep = merge(low_keep, after(low_got, high_send))
         high_send, high_keep = merge(high_keep, after(high_got, low_send))
     low_mine, high_mine = low_send, high_send
-    low_other, high_other = flip(low_mine, "leaf", bits), flip(high_mine, "leaf", bits)
-
-    other, own = after(low_other, high_mine)[None], low_mine[None]
+    with jax.named_scope("low_swap"):
+        low_other = flip(low_mine, "leaf", bits)
+    with jax.named_scope("high_swap"):
+        high_other = flip(high_mine, "leaf", bits)
+
+    other, own = low_other[None], after(low_mine, high_mine)[None]
     own = grow(own, after(step(own, "own", 0, bits, "gather"), other))
     high_other = after(high_other, own)
     both = [high_mine[:, :rank], high_other[:, :rank], high_mine[:, rank:] + high_other[:, rank:]]
@@ -251,7 +255,7 @@
         [array(2, rank, 2 * rank)],
         low_parts,
         [pltpu.VMEM((rank, 3 * rank), jnp.float32)] * 2,
-        flops=12 * unit * rank,
+        flops=36 * unit * rank,
     )
     (total,) = run(
         functools.partial(total_kernel, bits),

time: 68.1 us -> 65.7 us (0.965)
  waiting for transfers between devices: 31.4 us -> 28.1 us
  starting transfers between devices: 25.2 us -> 26 us
    ppermute x15, waiting for transfers between devices: 27.5 us -> 25.5 us  [step(): return lax.ppermute(x, AXES, pairs)]
    ppermute x3, waiting for transfers between devices: 3.84 us -> 2.62 us  [flip(): lax.ppermute(x, axis, [(i, i ^ 1 << bit) for i in range(lax.axis_size(axi...]
  transfers between devices with their start and end apart: 18 -> 18, of which waited for: 12 -> 12; matrix products, arithmetic and copies ran while one was open for 0% -> 0% of each run, Pallas kernels for 6% -> 7%
where the time goes in v9:
time: 65.7 us; the launch traced here: 65.5 us
  waiting for transfers between devices  28.1 us (43%)
  starting transfers between devices  26 us (40%)
  Pallas kernels  9.66 us (15%)
  between operations  0.79 us (1%)
    ppermute x15, waiting for transfers between devices, step(): return lax.ppermute(x, AXES, pairs)  25.5 us
    ppermute x15, starting transfers between devices, step(): return lax.ppermute(x, AXES, pairs)  20.6 us
    pallas_call x6, Pallas kernels, run(): pl.pallas_call(kernel, out_shape=shapes, in_specs=[pl.BlockSpec(memory_sp...  9.66 us
    ppermute x3, starting transfers between devices, flip(): lax.ppermute(x, axis, [(i, i ^ 1 << bit) for i in range(lax.axis_size(axi...  5.43 us
    ppermute x3, waiting for transfers between devices, flip(): lax.ppermute(x, axis, [(i, i ^ 1 << bit) for i in range(lax.axis_size(axi...  2.62 us
  transfers between devices with their start and end apart: 18, of which 12 were waited for; matrix products, arithmetic and copies ran while one was open for 0% of the time, Pallas kernels for 7%

profile of v9, /device:TPU:0, one launch (start us, length us, event | category | flops | bytes accessed | tf_op | source)
XLA Modules:
  0.0 65.5 jit_solution(11775478842618495871)
XLA Ops:
  0.6 0.0 copy-start.2
  0.6 2.4 %shard_map.59 = (f32[4,32,768]{2,1,0:T(8,128)S(1)}, f32[4,32,768]{2,1,0:T(8,128)S(1)}, bf16[2,512,768]{2,1,0:T(8,128)(2,1)S(1)}) custom-call(f32[512,256]{1,0:T(8,128)} %y_ref.1, f32[512,512]{1,0:T(8,128)} %z_ref.1, f32[512,256]{1,0:T(8,128)} %refs_2_.1), custom_call_target="tpu_custom_call" | custom-call | flops 603979776 | bytes 6029312 | tf_op jit(solution)/shard_map/pallas_call | solution.py:163
  3.1 3.0 %collective-permute-start = (f32[4,32,768]{2,1,0:T(8,128)S(1)}, f32[4,32,768]{2,1,0:T(8,128)S(1)}, u32[]{:S(2)}, u32[]{:S(2)}) collective-permute-start(f32[4,32,768]{2,1,0:T(8,128)S(1)} %get-tuple-element.26), channel_id=1, source_target_pairs={{0,2},{1,5},{2,0},{3,7},{4,6},{5,1},{6,4},{7,3},{8,10},{9,13},{10,... | collective-permute-start | bytes 1179656 | tf_op jit(solution)/shard_map/low_scatter_0/ppermute | solution.py:38
  6.1 0.0 copy-done.2
  6.1 0.9 %shard_map.60 = (f32[4,32,768]{2,1,0:T(8,128)S(1)}, f32[4,32,768]{2,1,0:T(8,128)S(1)}) custom-call(f32[512,256]{1,0:T(8,128)S(1)} %copy-done.2, bf16[2,512,768]{2,1,0:T(8,128)(2,1)S(1)} %get-tuple-element.27.joined), custom_call_target="tpu_custom_call" | custom-call | flops 603979776 | bytes 4456448 | tf_op jit(solution)/shard_map/pallas_call | solution.py:163
  7.0 1.6 %collective-permute-start.2 = (f32[4,32,768]{2,1,0:T(8,128)S(1)}, f32[4,32,768]{2,1,0:T(8,128)S(1)}, u32[]{:S(2)}, u32[]{:S(2)}) collective-permute-start(f32[4,32,768]{2,1,0:T(8,128)S(1)} %get-tuple-element.28), channel_id=1, source_target_pairs={{0,8},{1,9},{2,10},{3,11},{4,12},{5,13},{6,14},{7,15},{8,0},{9,1},... | collective-permute-start | bytes 1179656 | tf_op jit(solution)/shard_map/high_scatter_0/ppermute | solution.py:38
  8.6 3.2 %collective-permute-done = f32[4,32,768]{2,1,0:T(8,128)S(1)} collective-permute-done((f32[4,32,768]{2,1,0:T(8,128)S(1)}, f32[4,32,768]{2,1,0:T(8,128)S(1)}, u32[]{:S(2)}, u32[]{:S(2)}) %collective-permute-start) | collective-permute-done | bytes 393248 | tf_op jit(solution)/shard_map/low_scatter_0/ppermute | solution.py:38
  11.9 2.1 %collective-permute-start.1 = (f32[2,32,768]{2,1,0:T(8,128)S(1)}, f32[2,32,768]{2,1,0:T(8,128)S(1)}, u32[]{:S(2)}, u32[]{:S(2)}) collective-permute-start(f32[2,32,768]{2,1,0:T(8,128)S(1)} %get-tuple-element.50), channel_id=1, source_target_pairs={{0,4},{1,3},{2,6},{3,1},{4,0},{5,7},{6,2},{7,5},{8,12},{9,11},{10,... | collective-permute-start | bytes 589832 | tf_op jit(solution)/shard_map/low_scatter_1/ppermute | solution.py:38
  14.0 3.6 %collective-permute-done.2 = f32[4,32,768]{2,1,0:T(8,128)S(1)} collective-permute-done((f32[4,32,768]{2,1,0:T(8,128)S(1)}, f32[4,32,768]{2,1,0:T(8,128)S(1)}, u32[]{:S(2)}, u32[]{:S(2)}) %collective-permute-start.2) | collective-permute-done | bytes 393248 | tf_op jit(solution)/shard_map/high_scatter_0/ppermute | solution.py:38
  17.7 1.5 %collective-permute-start.4 = (f32[2,32,768]{2,1,0:T(8,128)S(1)}, f32[2,32,768]{2,1,0:T(8,128)S(1)}, u32[]{:S(2)}, u32[]{:S(2)}) collective-permute-start(f32[2,32,768]{2,1,0:T(8,128)S(1)} %get-tuple-element.49), channel_id=1, source_target_pairs={{0,2},{1,5},{2,0},{3,7},{4,6},{5,1},{6,4},{7,3},{8,10},{9,13},{10,... | collective-permute-start | bytes 589832 | tf_op jit(solution)/shard_map/high_scatter_1/ppermute | solution.py:38
  19.2 0.0 collective-permute-done.1
  19.3 1.7 %collective-permute-start.3 = (f32[1,32,768]{2,1,0:T(8,128)S(1)}, f32[1,32,768]{2,1,0:T(8,128)S(1)}, u32[]{:S(2)}, u32[]{:S(2)}) collective-permute-start(f32[1,32,768]{2,1,0:T(8,128)S(1)} %slice_add_fusion.6), channel_id=1, source_target_pairs={{0,8},{1,9},{2,10},{3,11},{4,12},{5,13},{6,14},{7,15},{8,0},{9,1},... | collective-permute-start | bytes 294920 | tf_op jit(solution)/shard_map/low_scatter_2/ppermute | solution.py:38
  20.9 2.5 %collective-permute-done.4 = f32[2,32,768]{2,1,0:T(8,128)S(1)} collective-permute-done((f32[2,32,768]{2,1,0:T(8,128)S(1)}, f32[2,32,768]{2,1,0:T(8,128)S(1)}, u32[]{:S(2)}, u32[]{:S(2)}) %collective-permute-start.4) | collective-permute-done | bytes 196640 | tf_op jit(solution)/shard_map/high_scatter_1/ppermute | solution.py:38
  23.5 0.4 collective-permute-start.5
  23.9 0.1 collective-permute-done.3
  24.0 2.7 %collective-permute-start.7 = (f32[32,768]{1,0:T(8,128)S(1)}, f32[32,768]{1,0:T(8,128)S(1)}, u32[]{:S(2)}, u32[]{:S(2)}) collective-permute-start(f32[32,768]{1,0:T(8,128)S(1)} %fusion.3), channel_id=1, source_target_pairs={{0,16},{2,18},{4,20},{6,22},{8,24},{10,26},{12,28},{14,30},{16,0},... | collective-permute-start | bytes 294920 | tf_op jit(solution)/shard_map/low_swap/ppermute | solution.py:42
  26.7 1.4 %collective-permute-done.5 = f32[1,32,768]{2,1,0:T(8,128)S(1)} collective-permute-done((f32[1,32,768]{2,1,0:T(8,128)S(1)}, f32[1,32,768]{2,1,0:T(8,128)S(1)}, u32[]{:S(2)}, u32[]{:S(2)}) %collective-permute-start.5) | collective-permute-done | bytes 98336 | tf_op jit(solution)/shard_map/high_scatter_2/ppermute | solution.py:38
  28.2 1.5 %collective-permute-start.6 = (f32[1,32,768]{2,1,0:T(8,128)S(1)}, f32[1,32,768]{2,1,0:T(8,128)S(1)}, u32[]{:S(2)}, u32[]{:S(2)}) collective-permute-start(f32[1,32,768]{2,1,0:T(8,128)S(1)} %bitcast.8), channel_id=1, source_target_pairs={{0,2},{1,5},{2,0},{3,7},{4,6},{5,1},{6,4},{7,3},{8,10},{9,13},{10,... | collective-permute-start | bytes 294920 | tf_op jit(solution)/shard_map/own_gather_0/ppermute | solution.py:38
  29.7 2.6 %collective-permute-start.10 = (f32[32,768]{1,0:T(8,128)S(1)}, f32[32,768]{1,0:T(8,128)S(1)}, u32[]{:S(2)}, u32[]{:S(2)}) collective-permute-start(f32[32,768]{1,0:T(8,128)S(1)} %fusion.1), channel_id=1, source_target_pairs={{0,16},{2,18},{4,20},{6,22},{8,24},{10,26},{12,28},{14,30},{16,0},... | collective-permute-start | bytes 294920 | tf_op jit(solution)/shard_map/high_swap/ppermute | solution.py:42
  32.3 1.3 %collective-permute-done.7 = f32[32,768]{1,0:T(8,128)S(1)} collective-permute-done((f32[32,768]{1,0:T(8,128)S(1)}, f32[32,768]{1,0:T(8,128)S(1)}, u32[]{:S(2)}, u32[]{:S(2)}) %collective-permute-start.7) | collective-permute-done | bytes 98336 | tf_op jit(solution)/shard_map/low_swap/ppermute | solution.py:42
  33.6 0.3 collective-permute-start.9
  33.9 0.0 collective-permute-done.6
  33.9 1.3 %collective-permute-done.10 = f32[32,768]{1,0:T(8,128)S(1)} collective-permute-done((f32[32,768]{1,0:T(8,128)S(1)}, f32[32,768]{1,0:T(8,128)S(1)}, u32[]{:S(2)}, u32[]{:S(2)}) %collective-permute-start.10) | collective-permute-done | bytes 98336 | tf_op jit(solution)/shard_map/high_swap/ppermute | solution.py:42
  35.3 0.6 collective-permute-start.8
  35.8 1.8 %collective-permute-start.13 = (f32[1,32,1024]{2,1,0:T(8,128)S(1)}, f32[1,32,1024]{2,1,0:T(8,128)S(1)}, u32[]{:S(2)}, u32[]{:S(2)}) collective-permute-start(f32[1,32,1024]{2,1,0:T(8,128)S(1)} %maximum_bitcast_fusion), channel_id=1, source_target_pairs={{0,8},{1,9},{2,10},{3,11},{4,12},{5,13},{6,14},{7,15},{8,0},{9,1},... | collective-permute-start | bytes 393224 | tf_op jit(solution)/shard_map/high_gather_0/ppermute | solution.py:38
  37.6 1.5 %collective-permute-done.9 = f32[1,32,768]{2,1,0:T(8,128)S(1)} collective-permute-done((f32[1,32,768]{2,1,0:T(8,128)S(1)}, f32[1,32,768]{2,1,0:T(8,128)S(1)}, u32[]{:S(2)}, u32[]{:S(2)}) %collective-permute-start.9) | collective-permute-done | bytes 98336 | tf_op jit(solution)/shard_map/other_gather_0/ppermute | solution.py:38
  39.2 0.2 collective-permute-start.12
  39.3 1.7 %collective-permute-done.8 = f32[2,32,768]{2,1,0:T(8,128)S(1)} collective-permute-done((f32[2,32,768]{2,1,0:T(8,128)S(1)}, f32[2,32,768]{2,1,0:T(8,128)S(1)}, u32[]{:S(2)}, u32[]{:S(2)}) %collective-permute-start.8) | collective-permute-done | bytes 196640 | tf_op jit(solution)/shard_map/own_gather_1/ppermute | solution.py:38
  41.0 1.9 %collective-permute-start.11 = (f32[4,32,768]{2,1,0:T(8,128)S(1)}, f32[4,32,768]{2,1,0:T(8,128)S(1)}, u32[]{:S(2)}, u32[]{:S(2)}) collective-permute-start(f32[4,32,768]{2,1,0:T(8,128)S(1)} %pad_maximum_fusion.1.own_low), channel_id=1, source_target_pairs={{0,8},{1,9},{2,10},{3,11},{4,12},{5,13},{6,14},{7,15},{8,0},{9,1},... | collective-permute-start | bytes 1179656 | tf_op jit(solution)/shard_map/own_gather_2/ppermute | solution.py:38
  42.9 0.0 collective-permute-done.13
  42.9 1.6 %collective-permute-start.15 = (f32[2,32,1024]{2,1,0:T(8,128)S(1)}, f32[2,32,1024]{2,1,0:T(8,128)S(1)}, u32[]{:S(2)}, u32[]{:S(2)}) collective-permute-start(f32[2,32,1024]{2,1,0:T(8,128)S(1)} %pad_maximum_fusion.3), channel_id=1, source_target_pairs={{0,2},{1,5},{2,0},{3,7},{4,6},{5,1},{6,4},{7,3},{8,10},{9,13},{10,... | collective-permute-start | bytes 786440 | tf_op jit(solution)/shard_map/high_gather_1/ppermute | solution.py:38
  44.6 2.0 %collective-permute-done.12 = f32[2,32,768]{2,1,0:T(8,128)S(1)} collective-permute-done((f32[2,32,768]{2,1,0:T(8,128)S(1)}, f32[2,32,768]{2,1,0:T(8,128)S(1)}, u32[]{:S(2)}, u32[]{:S(2)}) %collective-permute-start.12) | collective-permute-done | bytes 196640 | tf_op jit(solution)/shard_map/other_gather_1/ppermute | solution.py:38
  46.6 0.1 collective-permute-start.14
  46.7 3.0 %collective-permute-done.11.own_high = f32[4,32,768]{2,1,0:T(8,128)S(1)} collective-permute-done((f32[4,32,768]{2,1,0:T(8,128)S(1)}, f32[4,32,768]{2,1,0:T(8,128)S(1)}, u32[]{:S(2)}, u32[]{:S(2)}) %collective-permute-start.11) | collective-permute-done | bytes 393248 | tf_op jit(solution)/shard_map/own_gather_2/ppermute | solution.py:38
  49.7 0.0 collective-permute-done.15
  49.8 2.3 %collective-permute-start.16 = (f32[4,32,1024]{2,1,0:T(8,128)S(1)}, f32[4,32,1024]{2,1,0:T(8,128)S(1)}, u32[]{:S(2)}, u32[]{:S(2)}) collective-permute-start(f32[4,32,1024]{2,1,0:T(8,128)S(1)} %pad_maximum_fusion.first_ref), channel_id=1, source_target_pairs={{0,4},{1,3},{2,6},{3,1},{4,0},{5,7},{6,2},{7,5},{8,12},{9,11},{10,... | collective-permute-start | bytes 1572872 | tf_op jit(solution)/shard_map/high_gather_2/ppermute | solution.py:38
  52.1 6.3 %collective-permute-done.14.other_high = f32[4,32,768]{2,1,0:T(8,128)S(1)} collective-permute-done((f32[4,32,768]{2,1,0:T(8,128)S(1)}, f32[4,32,768]{2,1,0:T(8,128)S(1)}, u32[]{:S(2)}, u32[]{:S(2)}) %collective-permute-start.14) | collective-permute-done | bytes 393248 | tf_op jit(solution)/shard_map/other_gather_2/ppermute | solution.py:38
  58.4 2.1 %shard_map.61.update_ref = f32[2,256,512]{2,1,0:T(8,128)S(1)} custom-call(f32[4,32,768]{2,1,0:T(8,128)S(1)} %pad_maximum_fusion.1.own_low, f32[4,32,768]{2,1,0:T(8,128)S(1)} %collective-permute-done.11.own_high, f32[4,32,768]{2,1,0:T(8,128)S(1)} %pad_maximum_fusion.2.other_low, f32[4,32,768]{2,1,0:T(8,128)S(1)} %collective-permute-done.14.other_high), custom_call_target="tpu_custom_call" | custom-call | flops 3623878656 | bytes 2621440 | tf_op jit(solution)/shard_map/pallas_call | solution.py:163
  60.5 0.0 copy-start
  60.5 0.0 copy-start.1
  60.5 0.0 collective-permute-done.16.second_ref
  60.6 0.7 %shard_map.63.mine_ref = f32[256,512]{1,0:T(8,128)S(1)} custom-call(f32[4,32,1024]{2,1,0:T(8,128)S(1)} %pad_maximum_fusion.first_ref, f32[4,32,1024]{2,1,0:T(8,128)S(1)} %collective-permute-done.16.second_ref, f32[2,256,512]{2,1,0:T(8,128)S(1)} %shard_map.61.update_ref), custom_call_target="tpu_custom_call" | custom-call | flops 402653184 | bytes 2621440 | tf_op jit(solution)/shard_map/pallas_call | solution.py:163
  61.2 0.1 collective-permute-start.17
  61.3 0.4 copy-done
  61.8 0.1 copy-done.1
  61.9 1.4 %shard_map.62 = (f32[512,256]{1,0:T(8,128)}, bf16[2,512,256]{2,1,0:T(8,128)(2,1)S(1)}, f32[512,256]{1,0:T(8,128)S(1)}) custom-call(f32[512,256]{1,0:T(8,128)S(1)} %copy-done.1, f32[512,512]{1,0:T(8,128)S(1)} %copy-done, f32[2,256,512]{2,1,0:T(8,128)S(1)} %shard_map.61.update_ref), custom_call_target="tpu_custom_call" | custom-call | flops 402653184 | bytes 4718592 | tf_op jit(solution)/shard_map/pallas_call | solution.py:163
  63.3 0.0 collective-permute-done.17.other_ref
  63.3 2.2 %shard_map.64 = f32[512,256]{1,0:T(8,128)} custom-call(f32[256,512]{1,0:T(8,128)S(1)} %shard_map.63.mine_ref, f32[256,512]{1,0:T(8,128)S(1)} %collective-permute-done.17.other_ref, bf16[2,512,256]{2,1,0:T(8,128)(2,1)S(1)} %get-tuple-element.46.halves_ref, f32[512,256]{1,0:T(8,128)S(1)} %get-tuple-element.47.next_ref), custom_call_target="tpu_custom_call" | custom-call | flops 503316480 | bytes 3145728 | tf_op jit(solution)/shard_map/pallas_call | solution.py:163
  (16 shorter events, 0.3 us)
Async XLA Ops:
  0.6 5.5 %copy-start.2 = (f32[512,256]{1,0:T(8,128)S(1)}, f32[512,256]{1,0:T(8,128)}, u32[]{:S(2)}) copy-start(f32[512,256]{1,0:T(8,128)} %basis_ref.1) | copy-start | bytes 1572868
  3.1 8.8 %collective-permute-start = (f32[4,32,768]{2,1,0:T(8,128)S(1)}, f32[4,32,768]{2,1,0:T(8,128)S(1)}, u32[]{:S(2)}, u32[]{:S(2)}) collective-permute-start(f32[4,32,768]{2,1,0:T(8,128)S(1)} %get-tuple-element.26), channel_id=1, source_target_pairs={{0,2},{1,5},{2,0},{3,7},{4,6},{5,1},{6,4},{7,3},{8,10},{9,13},{10,... | collective-permute-start | bytes 1179656 | tf_op jit(solution)/shard_map/low_scatter_0/ppermute | solution.py:38
  7.0 10.7 %collective-permute-start.2 = (f32[4,32,768]{2,1,0:T(8,128)S(1)}, f32[4,32,768]{2,1,0:T(8,128)S(1)}, u32[]{:S(2)}, u32[]{:S(2)}) collective-permute-start(f32[4,32,768]{2,1,0:T(8,128)S(1)} %get-tuple-element.28), channel_id=1, source_target_pairs={{0,8},{1,9},{2,10},{3,11},{4,12},{5,13},{6,14},{7,15},{8,0},{9,1},... | collective-permute-start | bytes 1179656 | tf_op jit(solution)/shard_map/high_scatter_0/ppermute | solution.py:38
  11.9 7.3 %collective-permute-start.1 = (f32[2,32,768]{2,1,0:T(8,128)S(1)}, f32[2,32,768]{2,1,0:T(8,128)S(1)}, u32[]{:S(2)}, u32[]{:S(2)}) collective-permute-start(f32[2,32,768]{2,1,0:T(8,128)S(1)} %get-tuple-element.50), channel_id=1, source_target_pairs={{0,4},{1,3},{2,6},{3,1},{4,0},{5,7},{6,2},{7,5},{8,12},{9,11},{10,... | collective-permute-start | bytes 589832 | tf_op jit(solution)/shard_map/low_scatter_1/ppermute | solution.py:38
  17.7 5.7 %collective-permute-start.4 = (f32[2,32,768]{2,1,0:T(8,128)S(1)}, f32[2,32,768]{2,1,0:T(8,128)S(1)}, u32[]{:S(2)}, u32[]{:S(2)}) collective-permute-start(f32[2,32,768]{2,1,0:T(8,128)S(1)} %get-tuple-element.49), channel_id=1, source_target_pairs={{0,2},{1,5},{2,0},{3,7},{4,6},{5,1},{6,4},{7,3},{8,10},{9,13},{10,... | collective-permute-start | bytes 589832 | tf_op jit(solution)/shard_map/high_scatter_1/ppermute | solution.py:38
  19.3 4.7 %collective-permute-start.3 = (f32[1,32,768]{2,1,0:T(8,128)S(1)}, f32[1,32,768]{2,1,0:T(8,128)S(1)}, u32[]{:S(2)}, u32[]{:S(2)}) collective-permute-start(f32[1,32,768]{2,1,0:T(8,128)S(1)} %slice_add_fusion.6), channel_id=1, source_target_pairs={{0,8},{1,9},{2,10},{3,11},{4,12},{5,13},{6,14},{7,15},{8,0},{9,1},... | collective-permute-start | bytes 294920 | tf_op jit(solution)/shard_map/low_scatter_2/ppermute | solution.py:38
  23.5 4.7 %collective-permute-start.5 = (f32[1,32,768]{2,1,0:T(8,128)S(1)}, f32[1,32,768]{2,1,0:T(8,128)S(1)}, u32[]{:S(2)}, u32[]{:S(2)}) collective-permute-start(f32[1,32,768]{2,1,0:T(8,128)S(1)} %slice_add_fusion.5), channel_id=1, source_target_pairs={{0,4},{1,3},{2,6},{3,1},{4,0},{5,7},{6,2},{7,5},{8,12},{9,11},{10,... | collective-permute-start | bytes 294920 | tf_op jit(solution)/shard_map/high_scatter_2/ppermute | solution.py:38
  24.0 9.6 %collective-permute-start.7 = (f32[32,768]{1,0:T(8,128)S(1)}, f32[32,768]{1,0:T(8,128)S(1)}, u32[]{:S(2)}, u32[]{:S(2)}) collective-permute-start(f32[32,768]{1,0:T(8,128)S(1)} %fusion.3), channel_id=1, source_target_pairs={{0,16},{2,18},{4,20},{6,22},{8,24},{10,26},{12,28},{14,30},{16,0},... | collective-permute-start | bytes 294920 | tf_op jit(solution)/shard_map/low_swap/ppermute | solution.py:42
  28.2 5.7 %collective-permute-start.6 = (f32[1,32,768]{2,1,0:T(8,128)S(1)}, f32[1,32,768]{2,1,0:T(8,128)S(1)}, u32[]{:S(2)}, u32[]{:S(2)}) collective-permute-start(f32[1,32,768]{2,1,0:T(8,128)S(1)} %bitcast.8), channel_id=1, source_target_pairs={{0,2},{1,5},{2,0},{3,7},{4,6},{5,1},{6,4},{7,3},{8,10},{9,13},{10,... | collective-permute-start | bytes 294920 | tf_op jit(solution)/shard_map/own_gather_0/ppermute | solution.py:38
  29.7 5.6 %collective-permute-start.10 = (f32[32,768]{1,0:T(8,128)S(1)}, f32[32,768]{1,0:T(8,128)S(1)}, u32[]{:S(2)}, u32[]{:S(2)}) collective-permute-start(f32[32,768]{1,0:T(8,128)S(1)} %fusion.1), channel_id=1, source_target_pairs={{0,16},{2,18},{4,20},{6,22},{8,24},{10,26},{12,28},{14,30},{16,0},... | collective-permute-start | bytes 294920 | tf_op jit(solution)/shard_map/high_swap/ppermute | solution.py:42
  33.6 5.6 %collective-permute-start.9 = (f32[1,32,768]{2,1,0:T(8,128)S(1)}, f32[1,32,768]{2,1,0:T(8,128)S(1)}, u32[]{:S(2)}, u32[]{:S(2)}) collective-permute-start(f32[1,32,768]{2,1,0:T(8,128)S(1)} %bitcast.11), channel_id=1, source_target_pairs={{0,8},{1,9},{2,10},{3,11},{4,12},{5,13},{6,14},{7,15},{8,0},{9,1},... | collective-permute-start | bytes 294920 | tf_op jit(solution)/shard_map/other_gather_0/ppermute | solution.py:38
  35.3 5.7 %collective-permute-start.8 = (f32[2,32,768]{2,1,0:T(8,128)S(1)}, f32[2,32,768]{2,1,0:T(8,128)S(1)}, u32[]{:S(2)}, u32[]{:S(2)}) collective-permute-start(f32[2,32,768]{2,1,0:T(8,128)S(1)} %pad_maximum_fusion.4), channel_id=1, source_target_pairs={{0,4},{1,3},{2,6},{3,1},{4,0},{5,7},{6,2},{7,5},{8,12},{9,11},{10,... | collective-permute-start | bytes 589832 | tf_op jit(solution)/shard_map/own_gather_1/ppermute | solution.py:38
  35.8 7.1 %collective-permute-start.13 = (f32[1,32,1024]{2,1,0:T(8,128)S(1)}, f32[1,32,1024]{2,1,0:T(8,128)S(1)}, u32[]{:S(2)}, u32[]{:S(2)}) collective-permute-start(f32[1,32,1024]{2,1,0:T(8,128)S(1)} %maximum_bitcast_fusion), channel_id=1, source_target_pairs={{0,8},{1,9},{2,10},{3,11},{4,12},{5,13},{6,14},{7,15},{8,0},{9,1},... | collective-permute-start | bytes 393224 | tf_op jit(solution)/shard_map/high_gather_0/ppermute | solution.py:38
  39.2 7.5 %collective-permute-start.12 = (f32[2,32,768]{2,1,0:T(8,128)S(1)}, f32[2,32,768]{2,1,0:T(8,128)S(1)}, u32[]{:S(2)}, u32[]{:S(2)}) collective-permute-start(f32[2,32,768]{2,1,0:T(8,128)S(1)} %pad_maximum_fusion.5), channel_id=1, source_target_pairs={{0,4},{1,3},{2,6},{3,1},{4,0},{5,7},{6,2},{7,5},{8,12},{9,11},{10,... | collective-permute-start | bytes 589832 | tf_op jit(solution)/shard_map/other_gather_1/ppermute | solution.py:38
  41.0 8.7 %collective-permute-start.11 = (f32[4,32,768]{2,1,0:T(8,128)S(1)}, f32[4,32,768]{2,1,0:T(8,128)S(1)}, u32[]{:S(2)}, u32[]{:S(2)}) collective-permute-start(f32[4,32,768]{2,1,0:T(8,128)S(1)} %pad_maximum_fusion.1.own_low), channel_id=1, source_target_pairs={{0,8},{1,9},{2,10},{3,11},{4,12},{5,13},{6,14},{7,15},{8,0},{9,1},... | collective-permute-start | bytes 1179656 | tf_op jit(solution)/shard_map/own_gather_2/ppermute | solution.py:38
  42.9 6.8 %collective-permute-start.15 = (f32[2,32,1024]{2,1,0:T(8,128)S(1)}, f32[2,32,1024]{2,1,0:T(8,128)S(1)}, u32[]{:S(2)}, u32[]{:S(2)}) collective-permute-start(f32[2,32,1024]{2,1,0:T(8,128)S(1)} %pad_maximum_fusion.3), channel_id=1, source_target_pairs={{0,2},{1,5},{2,0},{3,7},{4,6},{5,1},{6,4},{7,3},{8,10},{9,13},{10,... | collective-permute-start | bytes 786440 | tf_op jit(solution)/shard_map/high_gather_1/ppermute | solution.py:38
  46.6 11.8 %collective-permute-start.14 = (f32[4,32,768]{2,1,0:T(8,128)S(1)}, f32[4,32,768]{2,1,0:T(8,128)S(1)}, u32[]{:S(2)}, u32[]{:S(2)}) collective-permute-start(f32[4,32,768]{2,1,0:T(8,128)S(1)} %pad_maximum_fusion.2.other_low), channel_id=1, source_target_pairs={{0,2},{1,5},{2,0},{3,7},{4,6},{5,1},{6,4},{7,3},{8,10},{9,13},{10,... | collective-permute-start | bytes 1179656 | tf_op jit(solution)/shard_map/other_gather_2/ppermute | solution.py:38
  49.8 10.8 %collective-permute-start.16 = (f32[4,32,1024]{2,1,0:T(8,128)S(1)}, f32[4,32,1024]{2,1,0:T(8,128)S(1)}, u32[]{:S(2)}, u32[]{:S(2)}) collective-permute-start(f32[4,32,1024]{2,1,0:T(8,128)S(1)} %pad_maximum_fusion.first_ref), channel_id=1, source_target_pairs={{0,4},{1,3},{2,6},{3,1},{4,0},{5,7},{6,2},{7,5},{8,12},{9,11},{10,... | collective-permute-start | bytes 1572872 | tf_op jit(solution)/shard_map/high_gather_2/ppermute | solution.py:38
  60.5 1.2 %copy-start = (f32[512,512]{1,0:T(8,128)S(1)}, f32[512,512]{1,0:T(8,128)}, u32[]{:S(2)}) copy-start(f32[512,512]{1,0:T(8,128)} %z_ref.1) | copy-start | bytes 3145732
  60.5 1.3 %copy-start.1 = (f32[512,256]{1,0:T(8,128)S(1)}, f32[512,256]{1,0:T(8,128)}, u32[]{:S(2)}) copy-start(f32[512,256]{1,0:T(8,128)} %y_ref.1) | copy-start | bytes 1572868
  61.2 2.0 %collective-permute-start.17 = (f32[256,512]{1,0:T(8,128)S(1)}, f32[256,512]{1,0:T(8,128)S(1)}, u32[]{:S(2)}, u32[]{:S(2)}) collective-permute-start(f32[256,512]{1,0:T(8,128)S(1)} %shard_map.63.mine_ref), channel_id=1, source_target_pairs={{0,1},{1,0},{2,3},{3,2},{4,5},{5,4},{6,7},{7,6},{8,9},{9,8},{10,11... | collective-permute-start | bytes 1572872 | tf_op jit(solution)/shard_map/ppermute | solution.py:42

commit v10 on v9

--- a/solution.py
+++ b/solution.py
@@ -14,7 +14,9 @@
     pair, rest = [core, 1 - core], list(range(2, bits))
     if stage == "scatter":
         return pair + rest if chain == "low" else rest + pair
-    return {"own": pair + rest, "other": rest + pair[::-1], "high": rest + pair}[chain]
+    if chain == "high":
+        return [1, 0] + rest if core == 0 else rest + [0, 1]
+    return pair + rest if chain == "own" else rest + pair[::-1]
 
 
 def relative_bits(order, r, first_is_high):
@@ -140,9 +142,11 @@
     total_ref[...] = total
 
 
-def middle_kernel(y_ref, z_ref, update_ref, pair_ref, halves_ref, next_ref):
-    rank = y_ref.shape[1]
-    middle = z_ref[...] - dot3(split(y_ref[...]), split(update_ref[0]))
+def middle_kernel(joined, update_ref, pair_ref, halves_ref, next_ref):
+    rank = pair_ref.shape[1]
+    y = (joined[0, :, :rank], joined[1, :, :rank])
+    z = joined[0, :, rank:].astype(jnp.float32) + joined[1, :, rank:].astype(jnp.float32)
+    middle = z - dot3(y, split(update_ref[0]))
     pair = middle[:, :rank]
     pair_ref[...] = pair
     halves_ref[0], halves_ref[1] = split(pair)
@@ -268,7 +272,7 @@
     pair_solved, halves, next_terms = run(
         middle_kernel,
         [array(depth, rank), array(2, depth, rank, dtype=jnp.bfloat16), array(depth, rank)],
-        [low_solved, upper_solved, update],
+        [joined, update],
         flops=2 * unit * depth,
     )
     (next_solved,) = run(

time: 65.7 us -> 64 us (0.974)
  starting transfers between devices: 26 us -> 23.3 us
  waiting for transfers between devices: 28.1 us -> 29.8 us
    ppermute x15, starting transfers between devices: 20.6 us -> 17.9 us  [step(): return lax.ppermute(x, AXES, pairs)]
    ppermute x15, waiting for transfers between devices: 25.5 us -> 26.7 us  [step(): return lax.ppermute(x, AXES, pairs)]
  transfers between devices with their start and end apart: 18 -> 18, of which waited for: 12 -> 14; matrix products, arithmetic and copies ran while one was open for 0% -> 0% of each run, Pallas kernels for 7% -> 7%
where the time goes in v10:
time: 64 us; the launch traced here: 63.9 us
  waiting for transfers between devices  29.8 us (47%)
  starting transfers between devices  23.3 us (36%)
  Pallas kernels  9.66 us (15%)
  between operations  0.77 us (1%)
    ppermute x15, waiting for transfers between devices, step(): return lax.ppermute(x, AXES, pairs)  26.7 us
    ppermute x15, starting transfers between devices, step(): return lax.ppermute(x, AXES, pairs)  17.9 us
    pallas_call x6, Pallas kernels, run(): pl.pallas_call(kernel, out_shape=shapes, in_specs=[pl.BlockSpec(memory_sp...  9.66 us
    ppermute x3, starting transfers between devices, flip(): lax.ppermute(x, axis, [(i, i ^ 1 << bit) for i in range(lax.axis_size(axi...  5.43 us
    ppermute x3, waiting for transfers between devices, flip(): lax.ppermute(x, axis, [(i, i ^ 1 << bit) for i in range(lax.axis_size(axi...  3.12 us
  transfers between devices with their start and end apart: 18, of which 14 were waited for; matrix products, arithmetic and copies ran while one was open for 0% of the time, Pallas kernels for 7%

profile of v10, /device:TPU:0, one launch (start us, length us, event | category | flops | bytes accessed | tf_op | source)
XLA Modules:
  0.0 63.9 jit_solution(7665859928941252682)
XLA Ops:
  0.6 0.0 copy-start
  0.6 2.4 %shard_map.59 = (f32[4,32,768]{2,1,0:T(8,128)S(1)}, f32[4,32,768]{2,1,0:T(8,128)S(1)}, bf16[2,512,768]{2,1,0:T(8,128)(2,1)S(1)}) custom-call(f32[512,256]{1,0:T(8,128)} %refs_0_.1, f32[512,512]{1,0:T(8,128)} %refs_1_.1, f32[512,256]{1,0:T(8,128)} %refs_2_.1), custom_call_target="tpu_custom_call" | custom-call | flops 603979776 | bytes 6029312 | tf_op jit(solution)/shard_map/pallas_call | solution.py:167
  3.1 3.0 %collective-permute-start = (f32[4,32,768]{2,1,0:T(8,128)S(1)}, f32[4,32,768]{2,1,0:T(8,128)S(1)}, u32[]{:S(2)}, u32[]{:S(2)}) collective-permute-start(f32[4,32,768]{2,1,0:T(8,128)S(1)} %get-tuple-element.27), channel_id=1, source_target_pairs={{0,2},{1,5},{2,0},{3,7},{4,6},{5,1},{6,4},{7,3},{8,10},{9,13},{10,... | collective-permute-start | bytes 1179656 | tf_op jit(solution)/shard_map/low_scatter_0/ppermute | solution.py:40
  6.1 0.0 copy-done
  6.1 0.9 %shard_map.60 = (f32[4,32,768]{2,1,0:T(8,128)S(1)}, f32[4,32,768]{2,1,0:T(8,128)S(1)}) custom-call(f32[512,256]{1,0:T(8,128)S(1)} %copy-done, bf16[2,512,768]{2,1,0:T(8,128)(2,1)S(1)} %get-tuple-element.25.joined), custom_call_target="tpu_custom_call" | custom-call | flops 603979776 | bytes 4456448 | tf_op jit(solution)/shard_map/pallas_call | solution.py:167
  7.0 1.6 %collective-permute-start.2 = (f32[4,32,768]{2,1,0:T(8,128)S(1)}, f32[4,32,768]{2,1,0:T(8,128)S(1)}, u32[]{:S(2)}, u32[]{:S(2)}) collective-permute-start(f32[4,32,768]{2,1,0:T(8,128)S(1)} %get-tuple-element.28), channel_id=1, source_target_pairs={{0,8},{1,9},{2,10},{3,11},{4,12},{5,13},{6,14},{7,15},{8,0},{9,1},... | collective-permute-start | bytes 1179656 | tf_op jit(solution)/shard_map/high_scatter_0/ppermute | solution.py:40
  8.6 3.2 %collective-permute-done = f32[4,32,768]{2,1,0:T(8,128)S(1)} collective-permute-done((f32[4,32,768]{2,1,0:T(8,128)S(1)}, f32[4,32,768]{2,1,0:T(8,128)S(1)}, u32[]{:S(2)}, u32[]{:S(2)}) %collective-permute-start) | collective-permute-done | bytes 393248 | tf_op jit(solution)/shard_map/low_scatter_0/ppermute | solution.py:40
  11.9 2.1 %collective-permute-start.1 = (f32[2,32,768]{2,1,0:T(8,128)S(1)}, f32[2,32,768]{2,1,0:T(8,128)S(1)}, u32[]{:S(2)}, u32[]{:S(2)}) collective-permute-start(f32[2,32,768]{2,1,0:T(8,128)S(1)} %get-tuple-element.50), channel_id=1, source_target_pairs={{0,4},{1,3},{2,6},{3,1},{4,0},{5,7},{6,2},{7,5},{8,12},{9,11},{10,... | collective-permute-start | bytes 589832 | tf_op jit(solution)/shard_map/low_scatter_1/ppermute | solution.py:40
  14.0 3.6 %collective-permute-done.2 = f32[4,32,768]{2,1,0:T(8,128)S(1)} collective-permute-done((f32[4,32,768]{2,1,0:T(8,128)S(1)}, f32[4,32,768]{2,1,0:T(8,128)S(1)}, u32[]{:S(2)}, u32[]{:S(2)}) %collective-permute-start.2) | collective-permute-done | bytes 393248 | tf_op jit(solution)/shard_map/high_scatter_0/ppermute | solution.py:40
  17.7 1.5 %collective-permute-start.4 = (f32[2,32,768]{2,1,0:T(8,128)S(1)}, f32[2,32,768]{2,1,0:T(8,128)S(1)}, u32[]{:S(2)}, u32[]{:S(2)}) collective-permute-start(f32[2,32,768]{2,1,0:T(8,128)S(1)} %get-tuple-element.49), channel_id=1, source_target_pairs={{0,2},{1,5},{2,0},{3,7},{4,6},{5,1},{6,4},{7,3},{8,10},{9,13},{10,... | collective-permute-start | bytes 589832 | tf_op jit(solution)/shard_map/high_scatter_1/ppermute | solution.py:40
  19.2 0.0 collective-permute-done.1
  19.3 1.7 %collective-permute-start.3 = (f32[1,32,768]{2,1,0:T(8,128)S(1)}, f32[1,32,768]{2,1,0:T(8,128)S(1)}, u32[]{:S(2)}, u32[]{:S(2)}) collective-permute-start(f32[1,32,768]{2,1,0:T(8,128)S(1)} %slice_add_fusion.6), channel_id=1, source_target_pairs={{0,8},{1,9},{2,10},{3,11},{4,12},{5,13},{6,14},{7,15},{8,0},{9,1},... | collective-permute-start | bytes 294920 | tf_op jit(solution)/shard_map/low_scatter_2/ppermute | solution.py:40
  20.9 2.5 %collective-permute-done.4 = f32[2,32,768]{2,1,0:T(8,128)S(1)} collective-permute-done((f32[2,32,768]{2,1,0:T(8,128)S(1)}, f32[2,32,768]{2,1,0:T(8,128)S(1)}, u32[]{:S(2)}, u32[]{:S(2)}) %collective-permute-start.4) | collective-permute-done | bytes 196640 | tf_op jit(solution)/shard_map/high_scatter_1/ppermute | solution.py:40
  23.5 0.4 collective-permute-start.5
  23.9 0.1 collective-permute-done.3
  24.0 2.8 %collective-permute-start.7 = (f32[32,768]{1,0:T(8,128)S(1)}, f32[32,768]{1,0:T(8,128)S(1)}, u32[]{:S(2)}, u32[]{:S(2)}) collective-permute-start(f32[32,768]{1,0:T(8,128)S(1)} %fusion.3), channel_id=1, source_target_pairs={{0,16},{2,18},{4,20},{6,22},{8,24},{10,26},{12,28},{14,30},{16,0},... | collective-permute-start | bytes 294920 | tf_op jit(solution)/shard_map/low_swap/ppermute | solution.py:44
  26.7 1.4 %collective-permute-done.5 = f32[1,32,768]{2,1,0:T(8,128)S(1)} collective-permute-done((f32[1,32,768]{2,1,0:T(8,128)S(1)}, f32[1,32,768]{2,1,0:T(8,128)S(1)}, u32[]{:S(2)}, u32[]{:S(2)}) %collective-permute-start.5) | collective-permute-done | bytes 98336 | tf_op jit(solution)/shard_map/high_scatter_2/ppermute | solution.py:40
  28.2 1.5 %collective-permute-start.6 = (f32[1,32,768]{2,1,0:T(8,128)S(1)}, f32[1,32,768]{2,1,0:T(8,128)S(1)}, u32[]{:S(2)}, u32[]{:S(2)}) collective-permute-start(f32[1,32,768]{2,1,0:T(8,128)S(1)} %bitcast.8), channel_id=1, source_target_pairs={{0,2},{1,5},{2,0},{3,7},{4,6},{5,1},{6,4},{7,3},{8,10},{9,13},{10,... | collective-permute-start | bytes 294920 | tf_op jit(solution)/shard_map/own_gather_0/ppermute | solution.py:40
  29.7 2.6 %collective-permute-start.10 = (f32[32,768]{1,0:T(8,128)S(1)}, f32[32,768]{1,0:T(8,128)S(1)}, u32[]{:S(2)}, u32[]{:S(2)}) collective-permute-start(f32[32,768]{1,0:T(8,128)S(1)} %fusion.1), channel_id=1, source_target_pairs={{0,16},{2,18},{4,20},{6,22},{8,24},{10,26},{12,28},{14,30},{16,0},... | collective-permute-start | bytes 294920 | tf_op jit(solution)/shard_map/high_swap/ppermute | solution.py:44
  32.3 1.3 %collective-permute-done.7 = f32[32,768]{1,0:T(8,128)S(1)} collective-permute-done((f32[32,768]{1,0:T(8,128)S(1)}, f32[32,768]{1,0:T(8,128)S(1)}, u32[]{:S(2)}, u32[]{:S(2)}) %collective-permute-start.7) | collective-permute-done | bytes 98336 | tf_op jit(solution)/shard_map/low_swap/ppermute | solution.py:44
  33.6 0.3 collective-permute-start.9
  33.9 0.0 collective-permute-done.6
  33.9 1.3 %collective-permute-done.10 = f32[32,768]{1,0:T(8,128)S(1)} collective-permute-done((f32[32,768]{1,0:T(8,128)S(1)}, f32[32,768]{1,0:T(8,128)S(1)}, u32[]{:S(2)}, u32[]{:S(2)}) %collective-permute-start.10) | collective-permute-done | bytes 98336 | tf_op jit(solution)/shard_map/high_swap/ppermute | solution.py:44
  35.3 0.6 collective-permute-start.8
  35.8 1.6 %collective-permute-start.13 = (f32[1,32,1024]{2,1,0:T(8,128)S(1)}, f32[1,32,1024]{2,1,0:T(8,128)S(1)}, u32[]{:S(2)}, u32[]{:S(2)}) collective-permute-start(f32[1,32,1024]{2,1,0:T(8,128)S(1)} %maximum_bitcast_fusion), channel_id=1, source_target_pairs={{0,4},{1,9},{2,6},{3,11},{4,0},{5,13},{6,2},{7,15},{8,12},{9,1},{1... | collective-permute-start | bytes 393224 | tf_op jit(solution)/shard_map/high_gather_0/ppermute | solution.py:40
  37.4 1.7 %collective-permute-done.9 = f32[1,32,768]{2,1,0:T(8,128)S(1)} collective-permute-done((f32[1,32,768]{2,1,0:T(8,128)S(1)}, f32[1,32,768]{2,1,0:T(8,128)S(1)}, u32[]{:S(2)}, u32[]{:S(2)}) %collective-permute-start.9) | collective-permute-done | bytes 98336 | tf_op jit(solution)/shard_map/other_gather_0/ppermute | solution.py:40
  39.2 0.1 collective-permute-start.12
  39.2 1.8 %collective-permute-done.8 = f32[2,32,768]{2,1,0:T(8,128)S(1)} collective-permute-done((f32[2,32,768]{2,1,0:T(8,128)S(1)}, f32[2,32,768]{2,1,0:T(8,128)S(1)}, u32[]{:S(2)}, u32[]{:S(2)}) %collective-permute-start.8) | collective-permute-done | bytes 196640 | tf_op jit(solution)/shard_map/own_gather_1/ppermute | solution.py:40
  41.0 1.9 %collective-permute-start.11 = (f32[4,32,768]{2,1,0:T(8,128)S(1)}, f32[4,32,768]{2,1,0:T(8,128)S(1)}, u32[]{:S(2)}, u32[]{:S(2)}) collective-permute-start(f32[4,32,768]{2,1,0:T(8,128)S(1)} %pad_maximum_fusion.1.own_low), channel_id=1, source_target_pairs={{0,8},{1,9},{2,10},{3,11},{4,12},{5,13},{6,14},{7,15},{8,0},{9,1},... | collective-permute-start | bytes 1179656 | tf_op jit(solution)/shard_map/own_gather_2/ppermute | solution.py:40
  42.9 0.0 collective-permute-done.13
  42.9 0.5 collective-permute-start.15
  43.4 2.4 %collective-permute-done.12 = f32[2,32,768]{2,1,0:T(8,128)S(1)} collective-permute-done((f32[2,32,768]{2,1,0:T(8,128)S(1)}, f32[2,32,768]{2,1,0:T(8,128)S(1)}, u32[]{:S(2)}, u32[]{:S(2)}) %collective-permute-start.12) | collective-permute-done | bytes 196640 | tf_op jit(solution)/shard_map/other_gather_1/ppermute | solution.py:40
  45.9 0.1 collective-permute-start.14
  46.0 3.8 %collective-permute-done.11.own_high = f32[4,32,768]{2,1,0:T(8,128)S(1)} collective-permute-done((f32[4,32,768]{2,1,0:T(8,128)S(1)}, f32[4,32,768]{2,1,0:T(8,128)S(1)}, u32[]{:S(2)}, u32[]{:S(2)}) %collective-permute-start.11) | collective-permute-done | bytes 393248 | tf_op jit(solution)/shard_map/own_gather_2/ppermute | solution.py:40
  49.7 0.0 collective-permute-done.15
  49.8 1.0 %collective-permute-start.16 = (f32[4,32,1024]{2,1,0:T(8,128)S(1)}, f32[4,32,1024]{2,1,0:T(8,128)S(1)}, u32[]{:S(2)}, u32[]{:S(2)}) collective-permute-start(f32[4,32,1024]{2,1,0:T(8,128)S(1)} %pad_maximum_fusion.first_ref), channel_id=1, source_target_pairs={{0,8},{1,5},{2,10},{3,7},{4,12},{5,1},{6,14},{7,3},{8,0},{9,13},{1... | collective-permute-start | bytes 1572872 | tf_op jit(solution)/shard_map/high_gather_2/ppermute | solution.py:40
  50.8 2.9 %collective-permute-done.14.other_high = f32[4,32,768]{2,1,0:T(8,128)S(1)} collective-permute-done((f32[4,32,768]{2,1,0:T(8,128)S(1)}, f32[4,32,768]{2,1,0:T(8,128)S(1)}, u32[]{:S(2)}, u32[]{:S(2)}) %collective-permute-start.14) | collective-permute-done | bytes 393248 | tf_op jit(solution)/shard_map/other_gather_2/ppermute | solution.py:40
  53.7 2.1 %shard_map.61.update_ref = f32[2,256,512]{2,1,0:T(8,128)S(1)} custom-call(f32[4,32,768]{2,1,0:T(8,128)S(1)} %pad_maximum_fusion.1.own_low, f32[4,32,768]{2,1,0:T(8,128)S(1)} %collective-permute-done.11.own_high, f32[4,32,768]{2,1,0:T(8,128)S(1)} %pad_maximum_fusion.2.other_low, f32[4,32,768]{2,1,0:T(8,128)S(1)} %collective-permute-done.14.other_high), custom_call_target="tpu_custom_call" | custom-call | flops 3623878656 | bytes 2621440 | tf_op jit(solution)/shard_map/pallas_call | solution.py:167
  55.8 3.2 %collective-permute-done.16.second_ref = f32[4,32,1024]{2,1,0:T(8,128)S(1)} collective-permute-done((f32[4,32,1024]{2,1,0:T(8,128)S(1)}, f32[4,32,1024]{2,1,0:T(8,128)S(1)}, u32[]{:S(2)}, u32[]{:S(2)}) %collective-permute-start.16) | collective-permute-done | bytes 524320 | tf_op jit(solution)/shard_map/high_gather_2/ppermute | solution.py:40
  59.0 0.7 %shard_map.63.mine_ref = f32[256,512]{1,0:T(8,128)S(1)} custom-call(f32[4,32,1024]{2,1,0:T(8,128)S(1)} %pad_maximum_fusion.first_ref, f32[4,32,1024]{2,1,0:T(8,128)S(1)} %collective-permute-done.16.second_ref, f32[2,256,512]{2,1,0:T(8,128)S(1)} %shard_map.61.update_ref), custom_call_target="tpu_custom_call" | custom-call | flops 402653184 | bytes 2621440 | tf_op jit(solution)/shard_map/pallas_call | solution.py:167
  59.7 0.1 collective-permute-start.17
  59.8 1.4 %shard_map.62 = (f32[512,256]{1,0:T(8,128)}, bf16[2,512,256]{2,1,0:T(8,128)(2,1)S(1)}, f32[512,256]{1,0:T(8,128)S(1)}) custom-call(bf16[2,512,768]{2,1,0:T(8,128)(2,1)S(1)} %get-tuple-element.25.joined, f32[2,256,512]{2,1,0:T(8,128)S(1)} %shard_map.61.update_ref), custom_call_target="tpu_custom_call" | custom-call | flops 402653184 | bytes 6291456 | tf_op jit(solution)/shard_map/pallas_call | solution.py:167
  61.2 0.5 collective-permute-done.17.other_ref
  61.7 2.2 %shard_map.64 = f32[512,256]{1,0:T(8,128)} custom-call(f32[256,512]{1,0:T(8,128)S(1)} %shard_map.63.mine_ref, f32[256,512]{1,0:T(8,128)S(1)} %collective-permute-done.17.other_ref, bf16[2,512,256]{2,1,0:T(8,128)(2,1)S(1)} %get-tuple-element.46.halves_ref, f32[512,256]{1,0:T(8,128)S(1)} %get-tuple-element.47.next_ref), custom_call_target="tpu_custom_call" | custom-call | flops 503316480 | bytes 3145728 | tf_op jit(solution)/shard_map/pallas_call | solution.py:167
  (16 shorter events, 0.3 us)
Async XLA Ops:
  0.6 5.5 %copy-start = (f32[512,256]{1,0:T(8,128)S(1)}, f32[512,256]{1,0:T(8,128)}, u32[]{:S(2)}) copy-start(f32[512,256]{1,0:T(8,128)} %basis_ref.1) | copy-start | bytes 1572868
  3.1 8.8 %collective-permute-start = (f32[4,32,768]{2,1,0:T(8,128)S(1)}, f32[4,32,768]{2,1,0:T(8,128)S(1)}, u32[]{:S(2)}, u32[]{:S(2)}) collective-permute-start(f32[4,32,768]{2,1,0:T(8,128)S(1)} %get-tuple-element.27), channel_id=1, source_target_pairs={{0,2},{1,5},{2,0},{3,7},{4,6},{5,1},{6,4},{7,3},{8,10},{9,13},{10,... | collective-permute-start | bytes 1179656 | tf_op jit(solution)/shard_map/low_scatter_0/ppermute | solution.py:40
  7.0 10.7 %collective-permute-start.2 = (f32[4,32,768]{2,1,0:T(8,128)S(1)}, f32[4,32,768]{2,1,0:T(8,128)S(1)}, u32[]{:S(2)}, u32[]{:S(2)}) collective-permute-start(f32[4,32,768]{2,1,0:T(8,128)S(1)} %get-tuple-element.28), channel_id=1, source_target_pairs={{0,8},{1,9},{2,10},{3,11},{4,12},{5,13},{6,14},{7,15},{8,0},{9,1},... | collective-permute-start | bytes 1179656 | tf_op jit(solution)/shard_map/high_scatter_0/ppermute | solution.py:40
  11.9 7.3 %collective-permute-start.1 = (f32[2,32,768]{2,1,0:T(8,128)S(1)}, f32[2,32,768]{2,1,0:T(8,128)S(1)}, u32[]{:S(2)}, u32[]{:S(2)}) collective-permute-start(f32[2,32,768]{2,1,0:T(8,128)S(1)} %get-tuple-element.50), channel_id=1, source_target_pairs={{0,4},{1,3},{2,6},{3,1},{4,0},{5,7},{6,2},{7,5},{8,12},{9,11},{10,... | collective-permute-start | bytes 589832 | tf_op jit(solution)/shard_map/low_scatter_1/ppermute | solution.py:40
  17.7 5.7 %collective-permute-start.4 = (f32[2,32,768]{2,1,0:T(8,128)S(1)}, f32[2,32,768]{2,1,0:T(8,128)S(1)}, u32[]{:S(2)}, u32[]{:S(2)}) collective-permute-start(f32[2,32,768]{2,1,0:T(8,128)S(1)} %get-tuple-element.49), channel_id=1, source_target_pairs={{0,2},{1,5},{2,0},{3,7},{4,6},{5,1},{6,4},{7,3},{8,10},{9,13},{10,... | collective-permute-start | bytes 589832 | tf_op jit(solution)/shard_map/high_scatter_1/ppermute | solution.py:40
  19.3 4.7 %collective-permute-start.3 = (f32[1,32,768]{2,1,0:T(8,128)S(1)}, f32[1,32,768]{2,1,0:T(8,128)S(1)}, u32[]{:S(2)}, u32[]{:S(2)}) collective-permute-start(f32[1,32,768]{2,1,0:T(8,128)S(1)} %slice_add_fusion.6), channel_id=1, source_target_pairs={{0,8},{1,9},{2,10},{3,11},{4,12},{5,13},{6,14},{7,15},{8,0},{9,1},... | collective-permute-start | bytes 294920 | tf_op jit(solution)/shard_map/low_scatter_2/ppermute | solution.py:40
  23.5 4.7 %collective-permute-start.5 = (f32[1,32,768]{2,1,0:T(8,128)S(1)}, f32[1,32,768]{2,1,0:T(8,128)S(1)}, u32[]{:S(2)}, u32[]{:S(2)}) collective-permute-start(f32[1,32,768]{2,1,0:T(8,128)S(1)} %slice_add_fusion.5), channel_id=1, source_target_pairs={{0,4},{1,3},{2,6},{3,1},{4,0},{5,7},{6,2},{7,5},{8,12},{9,11},{10,... | collective-permute-start | bytes 294920 | tf_op jit(solution)/shard_map/high_scatter_2/ppermute | solution.py:40
  24.0 9.6 %collective-permute-start.7 = (f32[32,768]{1,0:T(8,128)S(1)}, f32[32,768]{1,0:T(8,128)S(1)}, u32[]{:S(2)}, u32[]{:S(2)}) collective-permute-start(f32[32,768]{1,0:T(8,128)S(1)} %fusion.3), channel_id=1, source_target_pairs={{0,16},{2,18},{4,20},{6,22},{8,24},{10,26},{12,28},{14,30},{16,0},... | collective-permute-start | bytes 294920 | tf_op jit(solution)/shard_map/low_swap/ppermute | solution.py:44
  28.2 5.7 %collective-permute-start.6 = (f32[1,32,768]{2,1,0:T(8,128)S(1)}, f32[1,32,768]{2,1,0:T(8,128)S(1)}, u32[]{:S(2)}, u32[]{:S(2)}) collective-permute-start(f32[1,32,768]{2,1,0:T(8,128)S(1)} %bitcast.8), channel_id=1, source_target_pairs={{0,2},{1,5},{2,0},{3,7},{4,6},{5,1},{6,4},{7,3},{8,10},{9,13},{10,... | collective-permute-start | bytes 294920 | tf_op jit(solution)/shard_map/own_gather_0/ppermute | solution.py:40
  29.7 5.6 %collective-permute-start.10 = (f32[32,768]{1,0:T(8,128)S(1)}, f32[32,768]{1,0:T(8,128)S(1)}, u32[]{:S(2)}, u32[]{:S(2)}) collective-permute-start(f32[32,768]{1,0:T(8,128)S(1)} %fusion.1), channel_id=1, source_target_pairs={{0,16},{2,18},{4,20},{6,22},{8,24},{10,26},{12,28},{14,30},{16,0},... | collective-permute-start | bytes 294920 | tf_op jit(solution)/shard_map/high_swap/ppermute | solution.py:44
  33.6 5.6 %collective-permute-start.9 = (f32[1,32,768]{2,1,0:T(8,128)S(1)}, f32[1,32,768]{2,1,0:T(8,128)S(1)}, u32[]{:S(2)}, u32[]{:S(2)}) collective-permute-start(f32[1,32,768]{2,1,0:T(8,128)S(1)} %bitcast.11), channel_id=1, source_target_pairs={{0,8},{1,9},{2,10},{3,11},{4,12},{5,13},{6,14},{7,15},{8,0},{9,1},... | collective-permute-start | bytes 294920 | tf_op jit(solution)/shard_map/other_gather_0/ppermute | solution.py:40
  35.3 5.7 %collective-permute-start.8 = (f32[2,32,768]{2,1,0:T(8,128)S(1)}, f32[2,32,768]{2,1,0:T(8,128)S(1)}, u32[]{:S(2)}, u32[]{:S(2)}) collective-permute-start(f32[2,32,768]{2,1,0:T(8,128)S(1)} %pad_maximum_fusion.4), channel_id=1, source_target_pairs={{0,4},{1,3},{2,6},{3,1},{4,0},{5,7},{6,2},{7,5},{8,12},{9,11},{10,... | collective-permute-start | bytes 589832 | tf_op jit(solution)/shard_map/own_gather_1/ppermute | solution.py:40
  35.8 7.1 %collective-permute-start.13 = (f32[1,32,1024]{2,1,0:T(8,128)S(1)}, f32[1,32,1024]{2,1,0:T(8,128)S(1)}, u32[]{:S(2)}, u32[]{:S(2)}) collective-permute-start(f32[1,32,1024]{2,1,0:T(8,128)S(1)} %maximum_bitcast_fusion), channel_id=1, source_target_pairs={{0,4},{1,9},{2,6},{3,11},{4,0},{5,13},{6,2},{7,15},{8,12},{9,1},{1... | collective-permute-start | bytes 393224 | tf_op jit(solution)/shard_map/high_gather_0/ppermute | solution.py:40
  39.2 6.7 %collective-permute-start.12 = (f32[2,32,768]{2,1,0:T(8,128)S(1)}, f32[2,32,768]{2,1,0:T(8,128)S(1)}, u32[]{:S(2)}, u32[]{:S(2)}) collective-permute-start(f32[2,32,768]{2,1,0:T(8,128)S(1)} %pad_maximum_fusion.5), channel_id=1, source_target_pairs={{0,4},{1,3},{2,6},{3,1},{4,0},{5,7},{6,2},{7,5},{8,12},{9,11},{10,... | collective-permute-start | bytes 589832 | tf_op jit(solution)/shard_map/other_gather_1/ppermute | solution.py:40
  41.0 8.7 %collective-permute-start.11 = (f32[4,32,768]{2,1,0:T(8,128)S(1)}, f32[4,32,768]{2,1,0:T(8,128)S(1)}, u32[]{:S(2)}, u32[]{:S(2)}) collective-permute-start(f32[4,32,768]{2,1,0:T(8,128)S(1)} %pad_maximum_fusion.1.own_low), channel_id=1, source_target_pairs={{0,8},{1,9},{2,10},{3,11},{4,12},{5,13},{6,14},{7,15},{8,0},{9,1},... | collective-permute-start | bytes 1179656 | tf_op jit(solution)/shard_map/own_gather_2/ppermute | solution.py:40
  42.9 6.8 %collective-permute-start.15 = (f32[2,32,1024]{2,1,0:T(8,128)S(1)}, f32[2,32,1024]{2,1,0:T(8,128)S(1)}, u32[]{:S(2)}, u32[]{:S(2)}) collective-permute-start(f32[2,32,1024]{2,1,0:T(8,128)S(1)} %pad_maximum_fusion.3), channel_id=1, source_target_pairs={{0,2},{1,3},{2,0},{3,1},{4,6},{5,7},{6,4},{7,5},{8,10},{9,11},{10,... | collective-permute-start | bytes 786440 | tf_op jit(solution)/shard_map/high_gather_1/ppermute | solution.py:40
  45.9 7.8 %collective-permute-start.14 = (f32[4,32,768]{2,1,0:T(8,128)S(1)}, f32[4,32,768]{2,1,0:T(8,128)S(1)}, u32[]{:S(2)}, u32[]{:S(2)}) collective-permute-start(f32[4,32,768]{2,1,0:T(8,128)S(1)} %pad_maximum_fusion.2.other_low), channel_id=1, source_target_pairs={{0,2},{1,5},{2,0},{3,7},{4,6},{5,1},{6,4},{7,3},{8,10},{9,13},{10,... | collective-permute-start | bytes 1179656 | tf_op jit(solution)/shard_map/other_gather_2/ppermute | solution.py:40
  49.8 9.2 %collective-permute-start.16 = (f32[4,32,1024]{2,1,0:T(8,128)S(1)}, f32[4,32,1024]{2,1,0:T(8,128)S(1)}, u32[]{:S(2)}, u32[]{:S(2)}) collective-permute-start(f32[4,32,1024]{2,1,0:T(8,128)S(1)} %pad_maximum_fusion.first_ref), channel_id=1, source_target_pairs={{0,8},{1,5},{2,10},{3,7},{4,12},{5,1},{6,14},{7,3},{8,0},{9,13},{1... | collective-permute-start | bytes 1572872 | tf_op jit(solution)/shard_map/high_gather_2/ppermute | solution.py:40
  59.7 2.0 %collective-permute-start.17 = (f32[256,512]{1,0:T(8,128)S(1)}, f32[256,512]{1,0:T(8,128)S(1)}, u32[]{:S(2)}, u32[]{:S(2)}) collective-permute-start(f32[256,512]{1,0:T(8,128)S(1)} %shard_map.63.mine_ref), channel_id=1, source_target_pairs={{0,1},{1,0},{2,3},{3,2},{4,5},{5,4},{6,7},{7,6},{8,9},{9,8},{10,11... | collective-permute-start | bytes 1572872 | tf_op jit(solution)/shard_map/ppermute | solution.py:44
